TPU v7x, 512 devices: a whole 4x4x16 slice. The times are simulated.
512 devices in a mesh: pipe: 16 (over x, y_hi, core), tensor: 32 (over y_lo, z).
Axes of the slice: x: 4, y: 4 (y_hi: 2, y_lo: 2; y = y_hi * 2 + y_lo), z: 16, core: 2. Of those that a mesh axis runs over, the one named last changes fastest.
Arguments:
- ssm_inputs: bfloat16 [4096, 8192], P('pipe', 'tensor'), may hold values from -6 to 6
- step_decay: float32 [128, 4096], P('tensor', 'pipe'), may hold values from 0 to 1
- state_inputs: bfloat16 [8, 4096, 128], P(None, 'pipe'), may hold values from -1.5 to 1.5
- state_readout: bfloat16 [8, 4096, 128], P(None, 'pipe'), may hold values from -6 to 6
- skip_gain: float32 [128], P('tensor'), may hold values from 0.5 to 2
- norm_gain: float32 [8192], P('tensor'), may hold values from 0.5 to 1.5
- new_keys: bfloat16 [8, 4096, 128], P(None, 'pipe'), may hold values from -200 to 200
- new_values: bfloat16 [8, 4096, 128], P(None, 'pipe'), may hold values from -6 to 6
- cache_keys: bfloat16 [8, 2048, 128], P(None, 'pipe'), may hold values from -6 to 6
- cache_values: bfloat16 [8, 2048, 128], P(None, 'pipe'), may hold values from -6 to 6
- cache_len: int32 [16], P('pipe'), may hold values from 1 to 128, 1088 in all
- out_weight: bfloat16 [8192, 4096], P('tensor'), may hold values from -0.0625 to 0.0625
Outputs:
- mixed: bfloat16 [4096, 4096], P(('pipe', 'tensor'))
All inputs are finite; a program needn't handle non-finite values. No bound on the sum of `cache_len` on one device may be relied on, other than what follows from the above.
Results may differ from a plain program's by a relative error of at most 0.03.
Values may be sent and summed in bfloat16 or wider, within the bound.
No kernel may reach another device: no remote copies, remote signals or barrier semaphores. Data moves between devices by JAX's collectives and lax.ppermute only.
A program may use at most 64 MiB of HBM per device.

v0:
```python
import jax
import jax.numpy as jnp
from jax import lax
from jax.sharding import PartitionSpec as P

CACHE = 128
MH = 128
P_SIZE = 64
GROUPS = 8
ATT_HEADS = 64
KV = 8
HD = 128


def prefix(array, axis, combine, identity):
    size, place = (lax.axis_size(axis), lax.axis_index(axis))
    everything = jax.tree.map(lambda part: lax.all_gather(part, axis), array)
    start = jax.tree.map(
        lambda part, zero: jnp.broadcast_to(jnp.asarray(zero, part.dtype), part.shape),
        array,
        identity,
    )

    def step(k, before):
        reached = k < place
        new = combine(before, jax.tree.map(lambda part: part[k], everything))
        return jax.tree.map(lambda a, b: jnp.where(reached, a, b), new, before)

    return lax.fori_loop(0, size, step, start)


def combine_states(earlier, later):
    return (earlier[0] * later[0], later[0][:, None, None] * earlier[1] + later[1])


def per_device(
    ssm_inputs,
    step_decay,
    state_inputs,
    state_readout,
    skip_gain,
    norm_gain,
    new_keys,
    new_values,
    cache_keys,
    cache_values,
    cache_len,
    out_weight,
):
    heads = step_decay.shape[0]
    length = ssm_inputs.shape[0]
    section = lax.axis_index("pipe")
    group = lax.axis_index("tensor") * heads // (MH // GROUPS)
    b_part = lax.dynamic_index_in_dim(state_inputs, group, 0, keepdims=False)
    c_part = lax.dynamic_index_in_dim(state_readout, group, 0, keepdims=False)
    inputs = ssm_inputs.reshape(length, heads, P_SIZE)
    order = jnp.arange(length)
    causal = order[:, None] >= order[None, :]
    cum = jnp.cumsum(step_decay, axis=1)
    gram = jnp.dot(c_part, b_part.T, preferred_element_type=jnp.float32)
    diff = cum[:, :, None] - cum[:, None, :]
    seg = jnp.where(causal, jnp.exp(-jnp.where(causal, diff, 0.0)), 0.0)
    weights = (gram[None] * seg).astype(jnp.bfloat16)
    y_intra = jnp.einsum("hts,shp->thp", weights, inputs, preferred_element_type=jnp.float32)
    tail = jnp.exp(cum[:, -1:] - cum)
    weighted = (tail.T[:, :, None] * inputs.astype(jnp.float32)).astype(jnp.bfloat16)
    slice_state = jnp.einsum("shp,sn->hpn", weighted, b_part, preferred_element_type=jnp.float32)
    decay_total = jnp.exp(-cum[:, -1])
    identity = (jnp.ones_like(decay_total), jnp.zeros_like(slice_state))
    carried = prefix((decay_total, slice_state), "pipe", combine_states, identity)[1]
    y_state = jnp.exp(-cum).T[:, :, None] * jnp.einsum(
        "tn,hpn->thp", c_part.astype(jnp.float32), carried, precision=lax.Precision.HIGHEST
    )
    y_all = y_intra + y_state + skip_gain[None, :, None] * inputs.astype(jnp.float32)
    scale = lax.rsqrt(jnp.mean(y_all * y_all, axis=-1, keepdims=True) + 1e-05)
    normed = (y_all * scale * norm_gain.reshape(heads, P_SIZE)).astype(jnp.bfloat16)
    qheads = heads * P_SIZE // HD
    queries = normed.reshape(length, qheads, HD)
    kv_head = lax.axis_index("tensor") * qheads // (ATT_HEADS // KV)
    own_keys = jnp.concatenate(
        [
            lax.dynamic_index_in_dim(cache_keys, kv_head, 0, keepdims=False),
            lax.dynamic_index_in_dim(new_keys, kv_head, 0, keepdims=False),
        ],
        axis=0,
    )
    own_values = jnp.concatenate(
        [
            lax.dynamic_index_in_dim(cache_values, kv_head, 0, keepdims=False),
            lax.dynamic_index_in_dim(new_values, kv_head, 0, keepdims=False),
        ],
        axis=0,
    )
    span = CACHE + length
    slots = jnp.arange(span)
    key_bias = jnp.where((slots >= CACHE) | (slots < cache_len[0]), 0.0, -1e30).astype(jnp.bfloat16)
    start_carry = (
        jnp.full((qheads, length), -jnp.inf, jnp.float32),
        jnp.zeros((qheads, length), jnp.float32),
        jnp.zeros((qheads, length, HD), jnp.float32),
    )
    piece_keys = lax.all_gather(own_keys, "pipe", axis=0, tiled=True)
    piece_values = lax.all_gather(own_values, "pipe", axis=0, tiled=True)
    piece_bias = lax.all_gather(key_bias, "pipe", axis=0, tiled=True)
    count = piece_keys.shape[0] // span

    def single_block(index, state_now):
        block_keys = lax.dynamic_slice_in_dim(piece_keys, index * span, span, 0)
        block_values = lax.dynamic_slice_in_dim(piece_values, index * span, span, 0)
        block_bias = lax.dynamic_slice_in_dim(piece_bias, index * span, span, 0)
        running, total, accum = state_now
        scores = jnp.einsum(
            "tqd,kd->qtk", queries, block_keys, preferred_element_type=jnp.float32
        ) * HD ** (-0.5)
        scores = scores + block_bias.astype(jnp.float32)[None, None, :]
        allowed = (index < section) | (index == section) & (
            (slots[None, :] < CACHE) | (slots[None, :] - CACHE <= order[:, None])
        )
        scores = jnp.where(allowed[None], scores, -1e30)
        newer = jnp.maximum(running, jnp.max(scores, axis=-1))
        shrink = jnp.exp(running - newer)
        expo = jnp.exp(scores - newer[..., None])
        total = total * shrink + jnp.sum(expo, axis=-1)
        accum = accum * shrink[..., None] + jnp.einsum(
            "qtk,kd->qtd",
            expo.astype(jnp.bfloat16),
            block_values,
            preferred_element_type=jnp.float32,
        )
        return (newer, total, accum)

    running, total, accum = lax.fori_loop(0, count, single_block, start_carry)
    attended = (
        (accum / total[..., None])
        .astype(jnp.bfloat16)
        .transpose(1, 0, 2)
        .reshape(length, qheads * HD)
    )
    return lax.psum_scatter(
        jnp.dot(attended, out_weight, preferred_element_type=jnp.float32).astype(jnp.bfloat16),
        "tensor",
        scatter_dimension=0,
        tiled=True,
    )


def solution(mesh):
    placed = (
        P("pipe", "tensor"),
        P("tensor", "pipe"),
        P(None, "pipe", None),
        P(None, "pipe", None),
        P("tensor"),
        P("tensor"),
        P(None, "pipe", None),
        P(None, "pipe", None),
        P(None, "pipe", None),
        P(None, "pipe", None),
        P("pipe"),
        P("tensor", None),
    )
    return jax.shard_map(
        per_device,
        mesh=mesh,
        in_specs=placed,
        out_specs=P(("pipe", "tensor"), None),
        check_vma=False,
    )
```

profile of v0, /device:TPU:24, one launch (start us, length us, event | category | flops | bytes accessed | tf_op | source)
XLA Modules:
  0.0 401.4 jit_solution(17581477527020420028)
XLA Ops:
  6.5 0.9 reshape.141
  7.4 1.2 reduce-window.6
  9.3 1.0 copy.32
  10.3 1.7 fusion.31
  12.8 0.8 dynamic-slice_bitcast_fusion.1
  16.8 1.3 dynamic-slice
  19.0 32.4 %all-reduce = f32[64]{0:T(128)S(1)} all-reduce(f32[64]{0:T(128)S(1)} %bitcast_dynamic-update-slice_fusion), channel_id=2, replica_groups=mesh['pipe'=16,'tensor'=32] {'pipe'}, use_global_device_ids=true, to_apply=%add | all-reduce | flops 64 | bytes 512
  51.5 1.1 fusion.34
  53.3 25.1 %all-gather.2 = bf16[16,1,384]{2,1,0:T(2,128)(2,1)S(1)} all-gather(bf16[1,1,384]{2,1,0:T(2,128)(2,1)S(1)} %reshape.151), channel_id=1, replica_groups=mesh['pipe'=16,'tensor'=32] {'pipe'}, dimensions={0}, use_global_device_ids=true | all-gather | bytes 13056 | tf_op jit(solution)/shard_map/all_gather | solution.py:104
  79.0 16.5 %while.34 = (s32[]{:T(128)}, f32[4,64,128]{2,1,0:T(8,128)S(1)}, s32[]{:T(128)}, f32[16,4]{1,0:T(8,128)S(1)}, f32[16,4,64,128]{3,2,1,0:T(8,128)}, /*index=5*/s32[]{:T(128)}, s32[]{:T(128)}) while((s32[]{:T(128)}, f32[4,64,128]{2,1,0:T(8,128)S(1)}, s32[]{:T(128)}, f32[16,4]{1,0:T(8,128)S(1)}, f32[16,4,64,128]{3,2,1,0:T(8,128)}, ...), condition=%wide.region_3.4_spmd.clone, body=%wide.region_2.3_spmd.clone.sunk | while | flops 131076 | bytes 393369 | solution.py:29
  79.0 1.0 fusion.62
  80.0 1.0 fusion.62
  81.1 1.0 fusion.62
  82.1 1.0 fusion.62
  83.1 1.0 fusion.62
  84.2 1.0 fusion.62
  85.2 1.0 fusion.62
  86.2 1.0 fusion.62
  87.3 1.0 fusion.62
  88.3 1.0 fusion.62
  89.3 1.0 fusion.62
  90.4 1.0 fusion.62
  91.4 1.0 fusion.62
  92.5 1.0 fusion.62
  93.5 1.0 fusion.62
  94.5 1.0 fusion.62
  95.5 1.1 multiply_reduce_fusion
  96.9 46.1 %all-gather.9.cloned.1.call-done = bf16[6144,128]{1,0:T(8,128)(2,1)} async-done(((bf16[384,128]{1,0:T(8,128)(2,1)}), bf16[6144,128]{1,0:T(8,128)(2,1)}) %all-gather.9.cloned.1.call-update) | async-done | bytes 1572880 | tf_op jit(solution)/shard_map/all_gather | solution.py:103
  143.1 64.3 %all-gather.7.cloned.1.call-done = bf16[6144,128]{1,0:T(8,128)(2,1)} async-done(((bf16[384,128]{1,0:T(8,128)(2,1)}), bf16[6144,128]{1,0:T(8,128)(2,1)}) %all-gather.7.cloned.1.call-update) | async-done | bytes 1572880 | tf_op jit(solution)/shard_map/all_gather | solution.py:102
  207.3 46.8 %while.35 = (s32[]{:T(128)}, f32[2,256]{1,0:T(2,128)S(1)}, f32[2,256]{1,0:T(2,128)S(1)}, f32[2,256,128]{2,1,0:T(8,128)S(1)}, s32[]{:T(128)}, /*index=5*/bf16[614...) while((s32[]{:T(128)}, f32[2,256]{1,0:T(2,128)S(1)}, ...), condition=%wide.region_8.9_spmd.clone, body=%wide.region_5.8_spmd.clone.sunk | while | flops 102829704 | bytes 3448535 | solution.py:132
  207.6 1.2 fusion.67
  209.0 1.2 convolution_add_fusion.2
  210.5 1.2 fusion.67
  211.9 1.2 convolution_add_fusion.2
  213.5 1.2 fusion.67
  214.8 1.2 convolution_add_fusion.2
  216.4 1.2 fusion.67
  217.8 1.2 convolution_add_fusion.2
  219.3 1.2 fusion.67
  220.7 1.2 convolution_add_fusion.2
  222.2 1.2 fusion.67
  223.6 1.2 convolution_add_fusion.2
  225.2 1.2 fusion.67
  226.5 1.2 convolution_add_fusion.2
  228.1 1.2 fusion.67
  229.5 1.2 convolution_add_fusion.2
  231.0 1.2 fusion.67
  232.4 1.2 convolution_add_fusion.2
  234.0 1.2 fusion.67
  235.3 1.2 convolution_add_fusion.2
  236.9 1.2 fusion.67
  238.2 1.2 convolution_add_fusion.2
  239.8 1.2 fusion.67
  241.2 1.2 convolution_add_fusion.2
  242.7 1.2 fusion.67
  244.1 1.2 convolution_add_fusion.2
  245.7 1.2 fusion.67
  247.0 1.2 convolution_add_fusion.2
  248.6 1.2 fusion.67
  250.0 1.2 convolution_add_fusion.2
  251.5 1.2 fusion.67
  252.9 1.2 convolution_add_fusion.2
  254.3 2.1 convolution_convert_fusion
  256.4 138.5 %reduce-scatter.2.cloned.1.call-done = bf16[8,4096]{1,0:T(8,128)(2,1)} async-done(((bf16[256,4096]{1,0:T(8,128)(2,1)}), bf16[8,4096]{1,0:T(8,128)(2,1)}) %reduce-scatter.2.cloned.1.call-update) | async-done | bytes 65552 | tf_op jit(solution)/shard_map/reduce_scatter | solution.py:139
  (194 shorter events, 12.8 us)
Async XLA Ops:
  6.5 247.8 %copy-start = (bf16[256,4096]{1,0:T(8,128)(2,1)S(1)}, bf16[256,4096]{1,0:T(8,128)(2,1)}, u32[]{:S(2)}) copy-start(bf16[256,4096]{1,0:T(8,128)(2,1)} %param.27) | copy-start | bytes 6291460
  6.5 46.0 %copy-start.1 = (f32[256]{0:T(256)S(1)}, f32[256]{0:T(256)}, u32[]{:S(2)}) copy-start(f32[256]{0:T(256)} %param.21) | copy-start | bytes 3076
  6.5 72.4 %all-gather.11.cloned.1.call-start = ((), (), s32[]{:S(2)}) async-start(), calls=%async_computation.4 | async-start | bytes 2228224 | tf_op jit(solution)/shard_map/all_gather | solution.py:17
  12.0 131.1 %all-gather.9.cloned.1.call-start = ((), (), s32[]{:S(2)}) async-start(), calls=%async_computation.2 | async-start | bytes 1671168 | tf_op jit(solution)/shard_map/all_gather | solution.py:103
  14.3 193.0 %all-gather.7.cloned.1.call-start = ((), (), s32[]{:S(2)}) async-start(), calls=%async_computation.1 | async-start | bytes 1671168 | tf_op jit(solution)/shard_map/all_gather | solution.py:102
  16.7 378.2 %reduce-scatter.2.cloned.1.call-start = ((), (), s32[]{:S(2)}) async-start(), calls=%async_computation.3 | async-start | bytes 2162688 | tf_op jit(solution)/shard_map/reduce_scatter | solution.py:139
  78.5 17.1 %copy-start.2 = (f32[4]{0:T(128)S(1)}, f32[4]{0:T(128)}, u32[]{:S(2)}) copy-start(f32[4]{0:T(128)} %param.20) | copy-start | bytes 52
Sparse Core Ops, SparseCore 0:
  12.1 66.4 all-gather.10
  81.9 61.1 all-gather.8
  146.3 60.9 all-gather.6
  256.6 138.2 reduce-scatter.1
where the time goes:
time: 404 us; the launch traced here: 401 us
  waiting for transfers between devices  249 us (62%)
  blocking collectives  57.5 us (14%)
  matrix products  45.4 us (11%)
  other arithmetic  25.7 us (6%)
  between operations  14.7 us (4%)
  local copies, waits for them, and re-layouts  7.54 us (2%)
    reduce_scatter x1, waiting for transfers between devices, per_device(): lax.psum_scatter(jnp.dot(attended, out_weight, preferred_element_type=jnp...  138 us
    all_gather x1, waiting for transfers between devices, per_device(): piece_keys = lax.all_gather(own_keys, 'pipe', axis=0, tiled=True)  64.3 us
    all_gather x1, waiting for transfers between devices, per_device(): piece_values = lax.all_gather(own_values, 'pipe', axis=0, tiled=True)  46.1 us
    unnamed x1, blocking collectives  32.4 us
    all_gather x1, blocking collectives, per_device(): piece_bias = lax.all_gather(key_bias, 'pipe', axis=0, tiled=True)  25.1 us
    dot_general x16, matrix products, single_block(): jnp.einsum('qtk,kd->qtd', expo.astype(jnp.bfloat16), block_values, prefer...  19.8 us
    dot_general x16, matrix products, single_block(): jnp.einsum('tqd,kd->qtk', queries, block_keys, preferred_element_type=jnp...  19.2 us
    select_n x16, other arithmetic, step(): return jax.tree.map(lambda a, b: jnp.where(reached, a, b), new, before)  15.9 us
  transfers between devices with their start and end apart: 4, of which 3 were waited for; matrix products, arithmetic and copies ran while one was open for 6% of the time, Pallas kernels for 0%

commit v1 on v0

v1 whole, which is shorter than its diff:
```python
import functools
import math

import jax
import jax.numpy as jnp
from jax import lax
from jax.experimental import pallas as pl
from jax.experimental.pallas import tpu as pltpu
from jax.sharding import Mesh
from jax.sharding import PartitionSpec as P

CACHE = 128
MH = 128
P_SIZE = 64
HD = 128
TOKENS = 256
SPAN = CACHE + TOKENS
ROWS = 2 * SPAN + 16
CHIPS = 8
HIDDEN = -1e30
SCALE = HD ** (-0.5) * math.log2(math.e)

AXES = ("x", "yh", "c", "yl", "za", "z1", "z0")
SIZES = (4, 2, 2, 2, 4, 2, 2)
PIPE = ("x", "yh", "c")
TENSOR = ("yl", "za", "z1", "z0")
CHIP = ("x", "yh")
NEAR = ("z1", "z0")
OWNERS = ("z1", "yl", "za")

bf16 = jnp.bfloat16
f32 = jnp.float32


def dot(a, b, contract=((1,), (0,))):
    return lax.dot_general(a, b, (contract, ((), ())), preferred_element_type=f32)


def thirds(value):
    high = value.astype(bf16)
    rest = value - high.astype(f32)
    middle = rest.astype(bf16)
    low = (rest - middle.astype(f32)).astype(bf16)
    return (low, middle, high)


def tri(transposed):
    first = lax.broadcasted_iota(jnp.int32, (TOKENS, TOKENS), 0)
    second = lax.broadcasted_iota(jnp.int32, (TOKENS, TOKENS), 1)
    return (first <= second) if transposed else (first >= second)


def cum_columns(decay):
    lower = tri(False).astype(f32).astype(bf16)
    return sum(dot(lower, part, ((1,), (1,))) for part in thirds(decay))


def cum_rows(decay):
    upper = tri(True).astype(f32).astype(bf16)
    return sum(dot(part, upper) for part in thirds(decay))


def low_lanes(rows):
    return lax.broadcasted_iota(jnp.int32, (rows, 2 * P_SIZE), 1) < P_SIZE


def spread(columns, half, rows):
    left, right = columns[:, 2 * half : 2 * half + 1], columns[:, 2 * half + 1 : 2 * half + 2]
    return jnp.where(low_lanes(rows), left, right)


def state_kernel(group_ref, x_ref, decay_ref, b_ref, out_ref):
    cum = cum_columns(decay_ref[...])
    last = cum[TOKENS - 1 :, :]
    tail = jnp.exp(last - cum)
    total = jnp.exp(-last)
    for half in range(2):
        inputs = x_ref[:, half * HD : (half + 1) * HD].astype(f32)
        weighted = (spread(tail, half, TOKENS) * inputs).astype(bf16)
        out_ref[half, 0:HD, :] = dot(b_ref[0], weighted, ((0,), (0,)))
        out_ref[half, HD : HD + 8, :] = spread(jnp.broadcast_to(total, (8, 4)), half, 8)


def pair_kernel(place_ref, both_ref, out_ref):
    first, second = both_ref[0, 0], both_ref[1, 0]
    decay = second[HD : HD + 1]
    state = first[0:HD] * decay + second[0:HD]
    total = first[HD:] * second[HD:]
    for copy in range(CHIPS):
        out_ref[copy, 0:HD, :] = state
        out_ref[copy, HD : HD + 8, :] = total


def scan_kernel(place_ref, all_ref, out_ref):
    chip = place_ref[0]
    state = jnp.zeros((HD, HD), f32)
    for k in range(CHIPS - 1):
        new = all_ref[k, HD : HD + 1] * state + all_ref[k, 0:HD]
        state = jnp.where(k < chip, new, state)
    out_ref[...] = state


def inside_kernel(group_ref, x_ref, decay_ref, b_ref, c_ref, gain_ref, y_ref, fade_ref):
    decay = decay_ref[...]
    columns, rows = cum_columns(decay), cum_rows(decay)
    causal = tri(False)
    gram = dot(c_ref[0], b_ref[0], ((1,), (1,)))
    fade = jnp.exp(-columns)
    for half in range(2):
        inputs = x_ref[:, half * HD : (half + 1) * HD]
        pieces = []
        for head in (2 * half, 2 * half + 1):
            diff = jnp.where(causal, columns[:, head : head + 1] - rows[head : head + 1, :], 0.0)
            weights = jnp.where(causal, gram * jnp.exp(-diff), 0.0).astype(bf16)
            pieces.append(dot(weights, inputs))
        low = low_lanes(TOKENS)
        skip = jnp.where(low_lanes(1), gain_ref[2 * half], gain_ref[2 * half + 1])
        y_ref[half] = jnp.where(low, pieces[0], pieces[1]) + skip * inputs.astype(f32)
        fade_ref[half] = spread(fade, half, TOKENS)


def query_kernel(place_ref, y_ref, fade_ref, c_ref, carried_ref, both_ref, gain_ref, *out_refs):
    core, near = place_ref[1], place_ref[2]
    readout = c_ref[0]
    low = low_lanes(TOKENS)
    halves = []
    for half in range(2):
        carried = carried_ref[half]
        after = both_ref[0, half, HD : HD + 1] * carried + both_ref[0, half, 0:HD]
        carried = jnp.where(core == 1, after, carried)
        from_state = sum(dot(readout, part) for part in thirds(carried))
        y = y_ref[half] + fade_ref[half] * from_state
        square = y * y
        left = jnp.sum(jnp.where(low, square, 0.0), axis=1, keepdims=True)
        right = jnp.sum(jnp.where(low, 0.0, square), axis=1, keepdims=True)
        mean = jnp.where(low, left, right) * (1.0 / P_SIZE)
        halves.append(y * lax.rsqrt(mean + 1e-05) * gain_ref[0:1, half * HD : (half + 1) * HD])
    sets = []
    for member in range(4):
        pieces = [
            jnp.concatenate([half[32 * i + 8 * member : 32 * i + 8 * member + 8] for i in range(8)], axis=0)
            for half in halves
        ]
        sets.append([piece.astype(bf16) for piece in pieces])
    for mine in range(4):

        @pl.when(near == mine)
        def _():
            for i in range(4):
                for half in range(2):
                    out_refs[i][:, half * HD : (half + 1) * HD] = sets[mine ^ i][half]


def pack_kernel(place_ref, ck_ref, nk_ref, cv_ref, nv_ref, len_ref, out_ref):
    slots = lax.broadcasted_iota(jnp.int32, (16, HD), 1)
    bias = jnp.where(slots < len_ref[0], 0.0, HIDDEN).astype(bf16)
    out_ref[0, 0:CACHE, :] = ck_ref[0]
    out_ref[0, CACHE:SPAN, :] = nk_ref[0]
    out_ref[0, SPAN : SPAN + CACHE, :] = cv_ref[0]
    out_ref[0, SPAN + CACHE : 2 * SPAN, :] = nv_ref[0]
    out_ref[0, 2 * SPAN :, :] = bias


def attend_kernel(place_ref, q0, q1, q2, q3, a_ref, b_ref, out_ref, scores_ref, q_ref, top_ref, sum_ref, acc_ref):
    chip, core, near = place_ref[0], place_ref[1], place_ref[2]
    count = q_ref.shape[0]
    for i, ref in enumerate((q0, q1, q2, q3)):
        for half in range(2):
            row = (2 * i + half) * 64
            q_ref[row : row + 64, :] = ref[:, half * HD : (half + 1) * HD]
    top_ref[...] = jnp.full((count, HD), -jnp.inf, f32)

    def score(kv_ref, k, side, extra, causal):
        keys = kv_ref[pl.ds(k, 1)][0]
        bias = keys[2 * SPAN : 2 * SPAN + 1, :].astype(f32) + extra
        raw = dot(q_ref[...], keys[0:SPAN], ((1,), (1,)))
        top = top_ref[...]
        for tile in range(SPAN // HD):
            part = raw[:, tile * HD : (tile + 1) * HD]
            if tile == 0:
                part = part + bias
            elif causal:
                row = lax.broadcasted_iota(jnp.int32, (count, HD), 0) % 64
                token = 32 * (row // 8) + 8 * near + row % 8
                key = lax.broadcasted_iota(jnp.int32, (count, HD), 1) + (tile - 1) * HD
                part = jnp.where(key <= token, part, HIDDEN)
            elif extra is not None:
                part = part + extra
            top = jnp.maximum(top, part)
            scores_ref[k, :, side * SPAN + tile * HD : side * SPAN + (tile + 1) * HD] = part
        top_ref[...] = top

    def early(k, carry):
        score(a_ref, k, 0, 0.0, False)
        score(b_ref, k, 1, 0.0, False)
        return carry

    lax.fori_loop(0, chip, early, 0)
    score(a_ref, chip, 0, 0.0, True)
    score(b_ref, chip, 1, jnp.where(core == 1, 0.0, HIDDEN), False)

    top = jnp.max(top_ref[...], axis=1, keepdims=True) * SCALE
    top_ref[...] = jnp.broadcast_to(top, (count, HD))
    sum_ref[...] = jnp.zeros((count, HD), f32)
    acc_ref[...] = jnp.zeros((count, HD), f32)

    def late(k, carry):
        top = top_ref[...]
        total = sum_ref[...]
        acc = acc_ref[...]
        for side, kv_ref in enumerate((a_ref, b_ref)):
            values = kv_ref[pl.ds(k, 1)][0][SPAN : 2 * SPAN]
            probs = []
            for tile in range(SPAN // HD):
                part = scores_ref[k, :, side * SPAN + tile * HD : side * SPAN + (tile + 1) * HD]
                expo = jnp.exp2(part * SCALE - top)
                total = total + expo
                probs.append(expo.astype(bf16))
            acc = acc + dot(jnp.concatenate(probs, axis=1), values)
        sum_ref[...] = total
        acc_ref[...] = acc
        return carry

    lax.fori_loop(0, chip + 1, late, 0)
    total = jnp.sum(sum_ref[...], axis=1, keepdims=True)
    result = (acc_ref[...] / total).astype(bf16)
    for i in range(4):
        for half in range(2):
            row = (2 * i + half) * 64
            out_ref[near ^ i, :, half * HD : (half + 1) * HD] = result[row : row + 64]


def project_kernel(place_ref, att_ref, own_ref, r1, r2, r3, s1, s2, s3, out_ref):
    near, core = place_ref[2], place_ref[1]

    def run(others):
        total = None
        for i, ref in enumerate((own_ref,) + others):
            heads = jnp.concatenate([att_ref[0, near ^ i], att_ref[1, near ^ i]], axis=0)
            term = dot(heads, ref[...])
            total = term if total is None else total + term
        out_ref[...] = total.astype(bf16)

    @pl.when(pl.program_id(0) == core)
    def _():
        run((r1, r2, r3))

    @pl.when(pl.program_id(0) != core)
    def _():
        run((s1, s2, s3))


def finish_kernel(parts_ref, out_ref):
    for half in range(2):
        total = parts_ref[8 * half].astype(f32)
        for i in range(1, 8):
            total = total + parts_ref[8 * half + i].astype(f32)
        width = parts_ref.shape[2]
        out_ref[:, half * width : (half + 1) * width] = total.astype(bf16)


def whole(shape):
    return pl.BlockSpec(shape, lambda *_: (0,) * len(shape))


SMEM = pl.BlockSpec(memory_space=pltpu.SMEM)


def call(kernel, scalars, args, in_specs, out_shape, out_specs, grid=(1,), scratch=(), flops=0, nbytes=1 << 12):
    return pl.pallas_call(
        kernel,
        out_shape=out_shape,
        grid_spec=pltpu.PrefetchScalarGridSpec(
            num_scalar_prefetch=1, grid=grid, in_specs=in_specs, out_specs=out_specs, scratch_shapes=scratch
        ),
        compiler_params=pltpu.CompilerParams(vmem_limit_bytes=40 * 1024 * 1024),
        cost_estimate=pl.CostEstimate(flops=flops, bytes_accessed=nbytes, transcendentals=0),
    )(scalars, *args)


def shape(*dims, dtype=f32):
    return jax.ShapeDtypeStruct(dims, dtype)


def swap(array, axis):
    return lax.ppermute(array, axis, [(0, 1), (1, 0)])


def flip(array, i):
    return lax.ppermute(array, NEAR, [(j, j ^ i) for j in range(4)])


def per_device(
    ssm_inputs,
    step_decay,
    state_inputs,
    state_readout,
    skip_gain,
    norm_gain,
    new_keys,
    new_values,
    cache_keys,
    cache_values,
    cache_len,
    out_weight,
):
    width = out_weight.shape[1] // 4
    core = lax.axis_index("c")
    near = lax.axis_index(NEAR)
    group = lax.axis_index(("yl", "za")).astype(jnp.int32)
    place = jnp.stack([lax.axis_index(CHIP), core, near, group]).astype(jnp.int32)
    of_group = lambda rows: pl.BlockSpec((1, rows, HD), lambda i, s: (s[3], 0, 0))

    own = call(
        state_kernel,
        place,
        (ssm_inputs, step_decay, state_inputs),
        [whole((TOKENS, 2 * HD)), whole((4, TOKENS)), of_group(TOKENS)],
        shape(2, HD + 8, HD),
        whole((2, HD + 8, HD)),
    )
    both = lax.all_gather(own, "c")
    pair = call(
        pair_kernel,
        place,
        (both,),
        [pl.BlockSpec((2, 1, HD + 8, HD), lambda i, s: (0, s[1], 0, 0))],
        shape(CHIPS, HD + 8, HD),
        whole((CHIPS, HD + 8, HD)),
    )
    out_weight, pair = lax.optimization_barrier((out_weight, pair))
    columns = lambda quarter: lax.dynamic_slice_in_dim(out_weight, quarter * width, width, 1)
    first = flip(columns(2 * (near // 2) + core), 1)
    second = columns(2 * (1 - near // 2) + core)
    pairs = lax.all_to_all(pair, CHIP, 0, 0, tiled=True)
    pairs, first, second = lax.optimization_barrier((pairs, first, second))
    second = flip(second, 2)
    entering = call(
        scan_kernel, place, (pairs,), [whole((CHIPS, HD + 8, HD))], shape(HD, HD), whole((HD, HD))
    )
    carried = lax.all_gather(entering, "c")

    inside, fade = call(
        inside_kernel,
        place,
        (ssm_inputs, step_decay, state_inputs, state_readout, skip_gain),
        [whole((TOKENS, 2 * HD)), whole((4, TOKENS)), of_group(TOKENS), of_group(TOKENS), SMEM],
        (shape(2, TOKENS, HD), shape(2, TOKENS, HD)),
        (whole((2, TOKENS, HD)), whole((2, TOKENS, HD))),
    )
    packed = call(
        pack_kernel,
        place,
        (cache_keys, new_keys, cache_values, new_values, cache_len),
        [of_group(CACHE), of_group(TOKENS), of_group(CACHE), of_group(TOKENS), SMEM],
        shape(CHIPS, ROWS, HD, dtype=bf16),
        pl.BlockSpec((1, ROWS, HD), lambda i, s: (i, 0, 0)),
        grid=(CHIPS,),
    )

    queries = call(
        query_kernel,
        place,
        (inside, fade, state_readout, carried, both, norm_gain.reshape(1, 2 * HD)),
        [
            whole((2, TOKENS, HD)),
            whole((2, TOKENS, HD)),
            of_group(TOKENS),
            whole((2, HD, HD)),
            whole((2, 2, HD + 8, HD)),
            whole((1, 2 * HD)),
        ],
        tuple(shape(64, 2 * HD, dtype=bf16) for _ in range(4)),
        tuple(whole((64, 2 * HD)) for _ in range(4)),
    )
    packed, _ = lax.optimization_barrier((packed, entering))
    same = lax.all_to_all(packed, CHIP, 0, 0, tiled=True)
    queries = [queries[0]] + [flip(queries[i], i) for i in (1, 2, 3)]
    same, queries, second = lax.optimization_barrier((same, queries, second))
    other = swap(same, "c")
    third = flip(second, 1)
    swapped = [swap(part, "c") for part in (first, second)]

    attended = call(
        attend_kernel,
        place,
        (*queries, same, other),
        [whole((64, 2 * HD))] * 4 + [whole((CHIPS, ROWS, HD))] * 2,
        shape(4, 64, 2 * HD, dtype=bf16),
        whole((4, 64, 2 * HD)),
        scratch=[
            pltpu.VMEM((CHIPS, 512, 2 * SPAN), f32),
            pltpu.VMEM((512, HD), bf16),
            pltpu.VMEM((512, HD), f32),
            pltpu.VMEM((512, HD), f32),
            pltpu.VMEM((512, HD), f32),
        ],
    )
    attended, third = lax.optimization_barrier((attended, third))
    attended = lax.all_gather(attended, "z1")
    received = (first, second, third)
    swapped.append(swap(third, "c"))
    piece = whole((2 * HD, width))
    partial = call(
        project_kernel,
        place,
        (attended, out_weight, *received, *swapped),
        [whole((2, 4, 64, 2 * HD)), pl.BlockSpec((2 * HD, width), lambda i, s: (0, 2 * (s[2] // 2) + i))] + [piece] * 6,
        shape(128, 2 * width, dtype=bf16),
        pl.BlockSpec((128, width), lambda i, s: (0, i)),
        grid=(2,),
    )
    parts = lax.all_to_all(partial.reshape(16, 8, 2 * width), OWNERS, 0, 0, tiled=True)
    return pl.pallas_call(
        finish_kernel,
        out_shape=shape(8, 4 * width, dtype=bf16),
        compiler_params=pltpu.CompilerParams(vmem_limit_bytes=40 * 1024 * 1024),
    )(parts)


def solution(mesh):
    fine = Mesh(mesh.devices.reshape(SIZES), AXES)
    placed = (
        P(PIPE, TENSOR),
        P(TENSOR, PIPE),
        P(None, PIPE, None),
        P(None, PIPE, None),
        P(TENSOR),
        P(TENSOR),
        P(None, PIPE, None),
        P(None, PIPE, None),
        P(None, PIPE, None),
        P(None, PIPE, None),
        P(PIPE),
        P(TENSOR, None),
    )
    return jax.shard_map(
        per_device,
        mesh=fine,
        in_specs=placed,
        out_specs=P(PIPE + TENSOR, None),
        check_vma=False,
    )
```

time: 404 us -> 147 us (0.36)
  waiting for transfers between devices: 249 us -> 19.4 us
  matrix products: 45.4 us -> 0 us
  starting transfers between devices: 0.13 us -> 43.3 us
  other arithmetic: 25.7 us -> 0.08 us
  Pallas kernels: 0 us -> 15.3 us
  between operations: 14.7 us -> 0.95 us
    reduce_scatter x1 -> x0, waiting for transfers between devices: 138 us -> none  [per_device(): lax.psum_scatter(jnp.dot(attended, out_weight, preferred_element_type=jnp...]
    all_gather x3 -> x0, waiting for transfers between devices: 110 us -> none  [the longest x1 64.3 us: per_device(): piece_keys = lax.all_gather(own_keys, 'pipe', axis=0, tiled=True)]
    all_to_all x0 -> x1, blocking collectives: none -> 46.8 us  [per_device(): lax.all_to_all(partial.reshape(16, 8, 2 * width), OWNERS, 0, 0, tiled=True)]
    dot_general x37 -> x0, matrix products: 45.4 us -> none  [the longest x16 19.8 us: single_block(): jnp.einsum('qtk,kd->qtd', expo.astype(jnp.bfloat16), block_values, prefer...]
    unnamed x1 -> x0, blocking collectives: 32.4 us -> none
    ppermute x0 -> x10, starting transfers between devices: none -> 30.5 us  [the longest x6 22.2 us: flip(): return lax.ppermute(array, NEAR, [(j, j ^ i) for j in range(4)])]
    ppermute x0 -> x10, waiting for transfers between devices: none -> 16.1 us  [the longest x6 16.1 us: flip(): return lax.ppermute(array, NEAR, [(j, j ^ i) for j in range(4)])]
    select_n x16 -> x0, other arithmetic: 15.9 us -> none  [step(): return jax.tree.map(lambda a, b: jnp.where(reached, a, b), new, before)]
  transfers between devices with their start and end apart: 4 -> 12, of which waited for: 3 -> 3; matrix products, arithmetic and copies ran while one was open for 6% -> 0% of each run, Pallas kernels for 0% -> 6%
where the time goes in v1:
time: 147 us; the launch traced here: 146 us
  blocking collectives  61.1 us (42%)
  starting transfers between devices  43.3 us (29%)
  waiting for transfers between devices  19.4 us (13%)
  Pallas kernels  15.3 us (10%)
  local copies, waits for them, and re-layouts  5.93 us (4%)
    all_to_all x1, blocking collectives, per_device(): lax.all_to_all(partial.reshape(16, 8, 2 * width), OWNERS, 0, 0, tiled=True)  46.8 us
    ppermute x6, starting transfers between devices, flip(): return lax.ppermute(array, NEAR, [(j, j ^ i) for j in range(4)])  22.2 us
    ppermute x6, waiting for transfers between devices, flip(): return lax.ppermute(array, NEAR, [(j, j ^ i) for j in range(4)])  16.1 us
    pallas_call x8, Pallas kernels, call(): pl.pallas_call(kernel, out_shape=out_shape, grid_spec=pltpu.PrefetchScala...  14.6 us
    all_gather x1, blocking collectives, per_device(): attended = lax.all_gather(attended, 'z1')  10.3 us
    ppermute x4, starting transfers between devices, swap(): return lax.ppermute(array, axis, [(0, 1), (1, 0)])  8.29 us
    all_to_all x1, starting transfers between devices, per_device(): pairs = lax.all_to_all(pair, CHIP, 0, 0, tiled=True)  7.27 us
    all_to_all x1, starting transfers between devices, per_device(): same = lax.all_to_all(packed, CHIP, 0, 0, tiled=True)  5.54 us
  transfers between devices with their start and end apart: 12, of which 3 were waited for; matrix products, arithmetic and copies ran while one was open for 0% of the time, Pallas kernels for 6%

profile of v1, /device:TPU:24, one launch (start us, length us, event | category | flops | bytes accessed | tf_op | source)
XLA Modules:
  0.0 145.9 jit_solution(5605523133479883784)
XLA Ops:
  0.0 0.1 pad_add_fusion.place_ref.group_ref
  0.1 1.2 copy-done.3
  1.3 0.9 copy-done.9
  2.2 0.7 copy-done.13
  2.9 1.2 shard_map.119
  4.1 2.0 %all-gather = f32[4,136,128]{2,1,0:T(8,128)S(1)} all-gather(f32[2,136,128]{2,1,0:T(8,128)S(1)} %shard_map.119), channel_id=2, replica_groups=mesh['x'=4,'yh'=2,'c'=2,'yl'=2,'za'=4,'z1'=2,'z0'=2] {'c'}, dimensions={0}, use_global_device_ids=true | all-gather | bytes 417792 | tf_op jit(solution)/shard_map/all_gather | solution.py:322
  6.1 1.4 shard_map.120
  7.5 0.0 copy-done
  7.5 1.1 constant_dynamic-slice_fusion
  8.6 3.8 %collective-permute-start = (bf16[256,1024]{1,0:T(8,128)(2,1)}, bf16[256,1024]{1,0:T(8,128)(2,1)S(1)}, u32[]{:S(2)}, u32[]{:S(2)}) collective-permute-start(bf16[256,1024]{1,0:T(8,128)(2,1)} %get-tuple-element.46), channel_id=1, source_target_pairs={{0,1},{1,0},{2,3},{3,2},{4,5},{5,4},{6,7},{7,6},{8,9},{9,8},{10,11... | collective-permute-start | bytes 1572872 | tf_op jit(solution)/shard_map/ppermute | solution.py:290
  12.4 7.3 %all-to-all-start = ((f32[8,136,128]{2,1,0:T(8,128)}), f32[8,136,128]{2,1,0:T(8,128)S(1)}, u32[]{:S(2)}, u32[]{:S(2)}) async-start(f32[8,136,128]{2,1,0:T(8,128)} %shard_map.120), calls=%async_computation | async-start | bytes 1114112 | tf_op jit(solution)/shard_map/all_to_all | solution.py:335
  20.3 0.0 copy-done.7
  20.3 0.0 copy-done.8
  20.3 0.0 copy-start.11
  20.4 0.9 copy-done.11
  21.3 0.9 copy-done.12
  22.2 3.4 %shard_map.118 = bf16[8,784,128]{2,1,0:T(8,128)(2,1)} custom-call(s32[4]{0:T(128)S(1)} %pad_add_fusion.place_ref.group_ref, bf16[8,128,128]{2,1,0:T(8,128)(2,1)S(1)} %copy-done.11, bf16[8,256,128]{2,1,0:T(8,128)(2,1)S(1)} %copy-done.7, bf16[8,128,128]{2,1,0:T(8,128)(2,1)S(1)} %copy-done.12, bf16[8,256,128]{2,1,0:T(8,128)(2,1)S(1)} %copy-done.8, ...), custom_call_target="tpu_custom_call" | custom-call | bytes 4096 | tf_op jit(solution)/shard_map/pallas_call | solution.py:270
  25.7 3.3 %all-to-all-done.all_ref = f32[8,136,128]{2,1,0:T(8,128)S(1)} async-done(((f32[8,136,128]{2,1,0:T(8,128)}), f32[8,136,128]{2,1,0:T(8,128)S(1)}, u32[]{:S(2)}, u32[]{:S(2)}) %all-to-all-start) | async-done | bytes 557088 | tf_op jit(solution)/shard_map/all_to_all | solution.py:335
  29.0 0.0 collective-permute-done.r1
  29.0 0.6 shard_map.121
  29.6 0.0 copy-start.2
  29.6 0.0 copy-start.4
  29.6 0.0 copy-start.10
  29.6 0.0 copy-start.14
  29.6 0.0 copy-start.16
  29.6 0.0 copy-start.15
  29.7 0.1 copy-done.5
  29.8 5.5 %all-to-all-start.1 = ((bf16[8,784,128]{2,1,0:T(8,128)(2,1)}), bf16[8,784,128]{2,1,0:T(8,128)(2,1)S(1)}, u32[]{:S(2)}, u32[]{:S(2)}) async-start(bf16[8,784,128]{2,1,0:T(8,128)(2,1)} %shard_map.118), calls=%async_computation.1 | async-start | bytes 3211264 | tf_op jit(solution)/shard_map/all_to_all | solution.py:377
  35.3 5.2 %collective-permute-start.4 = (bf16[256,1024]{1,0:T(8,128)(2,1)}, bf16[256,1024]{1,0:T(8,128)(2,1)}, u32[]{:S(2)}, u32[]{:S(2)}) collective-permute-start(bf16[256,1024]{1,0:T(8,128)(2,1)} %get-tuple-element.35), channel_id=1, source_target_pairs={{0,2},{1,3},{2,0},{3,1},{4,6},{5,7},{6,4},{7,5},{8,10},{9,11},{10,... | collective-permute-start | bytes 1572872 | tf_op jit(solution)/shard_map/ppermute | solution.py:290
  40.5 0.0 copy-done.2
  40.5 0.0 copy-done.4
  40.5 0.0 copy-done.10
  40.5 0.0 copy-done.14
  40.5 0.0 copy-done.16
  40.5 1.8 %shard_map.122 = (f32[2,256,128]{2,1,0:T(8,128)S(1)}, f32[2,256,128]{2,1,0:T(8,128)S(1)}) custom-call(s32[4]{0:T(128)S(1)} %pad_add_fusion.place_ref.group_ref, bf16[256,256]{1,0:T(8,128)(2,1)S(1)} %copy-done.10, f32[4,256]{1,0:T(4,128)S(1)} %copy-done.14, bf16[8,256,128]{2,1,0:T(8,128)(2,1)S(1)} %copy-done.4, bf16[8,256,128]{2,1,0:T(8,128)(2,1)S(1)} %copy-done.2, ...), custom_call_target="tpu_custom_call" | custom-call | bytes 4096 | tf_op jit(solution)/shard_map/pallas_call | solution.py:270
  42.3 0.0 copy-start.6
  42.4 2.0 %all-gather.1 = f32[256,128]{1,0:T(8,128)S(1)} all-gather(f32[128,128]{1,0:T(8,128)S(1)} %shard_map.121), channel_id=3, replica_groups=mesh['x'=4,'yh'=2,'c'=2,'yl'=2,'za'=4,'z1'=2,'z0'=2] {'c'}, dimensions={0}, use_global_device_ids=true | all-gather | bytes 196608 | tf_op jit(solution)/shard_map/all_gather | solution.py:341
  44.4 1.0 shard_map.123
  45.4 2.2 %collective-permute-start.1 = (bf16[64,256]{1,0:T(8,128)(2,1)S(1)}, bf16[64,256]{1,0:T(8,128)(2,1)S(1)}, u32[]{:S(2)}, u32[]{:S(2)}) collective-permute-start(bf16[64,256]{1,0:T(8,128)(2,1)S(1)} %get-tuple-element.32), channel_id=1, source_target_pairs={{0,1},{1,0},{2,3},{3,2},{4,5},{5,4},{6,7},{7,6},{8,9},{9,8},{10,11... | collective-permute-start | bytes 98312 | tf_op jit(solution)/shard_map/ppermute | solution.py:290
  47.6 1.9 %collective-permute-start.2 = (bf16[64,256]{1,0:T(8,128)(2,1)S(1)}, bf16[64,256]{1,0:T(8,128)(2,1)S(1)}, u32[]{:S(2)}, u32[]{:S(2)}) collective-permute-start(bf16[64,256]{1,0:T(8,128)(2,1)S(1)} %get-tuple-element.33), channel_id=1, source_target_pairs={{0,2},{1,3},{2,0},{3,1},{4,6},{5,7},{6,4},{7,5},{8,10},{9,11},{10,... | collective-permute-start | bytes 98312 | tf_op jit(solution)/shard_map/ppermute | solution.py:290
  49.6 6.0 %collective-permute-start.3 = (bf16[64,256]{1,0:T(8,128)(2,1)S(1)}, bf16[64,256]{1,0:T(8,128)(2,1)S(1)}, u32[]{:S(2)}, u32[]{:S(2)}) collective-permute-start(bf16[64,256]{1,0:T(8,128)(2,1)S(1)} %get-tuple-element.34), channel_id=1, source_target_pairs={{0,3},{1,2},{2,1},{3,0},{4,7},{5,6},{6,5},{7,4},{8,11},{9,10},{10,... | collective-permute-start | bytes 98312 | tf_op jit(solution)/shard_map/ppermute | solution.py:290
  55.6 0.0 collective-permute-done.1.q1
  55.6 9.4 %collective-permute-done.2.q2 = bf16[64,256]{1,0:T(8,128)(2,1)S(1)} collective-permute-done((bf16[64,256]{1,0:T(8,128)(2,1)S(1)}, bf16[64,256]{1,0:T(8,128)(2,1)S(1)}, u32[]{:S(2)}, u32[]{:S(2)}) %collective-permute-start.2) | collective-permute-done | bytes 32800 | tf_op jit(solution)/shard_map/ppermute | solution.py:290
  65.0 0.0 collective-permute-done.3.q3
  65.0 0.0 collective-permute-done.4.r2
  65.0 0.0 all-to-all-done.1.a_ref
  65.0 0.0 copy-start.1
  65.0 2.1 %collective-permute-start.5 = (bf16[8,784,128]{2,1,0:T(8,128)(2,1)S(1)}, bf16[8,784,128]{2,1,0:T(8,128)(2,1)S(1)}, u32[]{:S(2)}, u32[]{:S(2)}) collective-permute-start(bf16[8,784,128]{2,1,0:T(8,128)(2,1)S(1)} %all-to-all-done.1.a_ref), channel_id=1, source_target_pairs={{0,32},{32,0},{1,33},{33,1},{2,34},{34,2},{3,35},{35,3},{4,36},{36... | collective-permute-start | bytes 4816904 | tf_op jit(solution)/shard_map/ppermute | solution.py:286
  67.1 3.1 %collective-permute-start.6 = (bf16[256,1024]{1,0:T(8,128)(2,1)}, bf16[256,1024]{1,0:T(8,128)(2,1)S(1)}, u32[]{:S(2)}, u32[]{:S(2)}) collective-permute-start(bf16[256,1024]{1,0:T(8,128)(2,1)} %collective-permute-done.4.r2), channel_id=1, source_target_pairs={{0,1},{1,0},{2,3},{3,2},{4,5},{5,4},{6,7},{7,6},{8,9},{9,8},{10,11... | collective-permute-start | bytes 1572872 | tf_op jit(solution)/shard_map/ppermute | solution.py:290
  70.2 0.0 copy-done.6
  70.2 2.1 %collective-permute-start.7 = (bf16[256,1024]{1,0:T(8,128)(2,1)S(1)}, bf16[256,1024]{1,0:T(8,128)(2,1)S(1)}, u32[]{:S(2)}, u32[]{:S(2)}) collective-permute-start(bf16[256,1024]{1,0:T(8,128)(2,1)S(1)} %copy-done.6), channel_id=1, source_target_pairs={{0,32},{32,0},{1,33},{33,1},{2,34},{34,2},{3,35},{35,3},{4,36},{36... | collective-permute-start | bytes 1572872 | tf_op jit(solution)/shard_map/ppermute | solution.py:286
  72.3 2.2 %collective-permute-start.8 = (bf16[256,1024]{1,0:T(8,128)(2,1)}, bf16[256,1024]{1,0:T(8,128)(2,1)S(1)}, u32[]{:S(2)}, u32[]{:S(2)}) collective-permute-start(bf16[256,1024]{1,0:T(8,128)(2,1)} %collective-permute-done.4.r2), channel_id=1, source_target_pairs={{0,32},{32,0},{1,33},{33,1},{2,34},{34,2},{3,35},{35,3},{4,36},{36... | collective-permute-start | bytes 1572872 | tf_op jit(solution)/shard_map/ppermute | solution.py:286
  74.5 0.0 collective-permute-done.5.b_ref
  74.5 2.4 %shard_map.124 = bf16[4,64,256]{2,1,0:T(8,128)(2,1)S(1)} custom-call(s32[4]{0:T(128)S(1)} %pad_add_fusion.place_ref.group_ref, bf16[64,256]{1,0:T(8,128)(2,1)S(1)} %get-tuple-element.36.q0, bf16[64,256]{1,0:T(8,128)(2,1)S(1)} %collective-permute-done.1.q1, bf16[64,256]{1,0:T(8,128)(2,1)S(1)} %collective-permute-done.2.q2, ...), custom_call_target="tpu_custom_call" | custom-call | bytes 4096 | tf_op jit(solution)/shard_map/pallas_call | solution.py:270
  76.9 6.6 %collective-permute-done.6.r3 = bf16[256,1024]{1,0:T(8,128)(2,1)S(1)} collective-permute-done((bf16[256,1024]{1,0:T(8,128)(2,1)}, bf16[256,1024]{1,0:T(8,128)(2,1)S(1)}, u32[]{:S(2)}, u32[]{:S(2)}) %collective-permute-start.6) | collective-permute-done | bytes 524320 | tf_op jit(solution)/shard_map/ppermute | solution.py:290
  83.5 1.9 %collective-permute-start.9 = (bf16[256,1024]{1,0:T(8,128)(2,1)S(1)}, bf16[256,1024]{1,0:T(8,128)(2,1)S(1)}, u32[]{:S(2)}, u32[]{:S(2)}) collective-permute-start(bf16[256,1024]{1,0:T(8,128)(2,1)S(1)} %collective-permute-done.6.r3), channel_id=1, source_target_pairs={{0,32},{32,0},{1,33},{33,1},{2,34},{34,2},{3,35},{35,3},{4,36},{36... | collective-permute-start | bytes 1572872 | tf_op jit(solution)/shard_map/ppermute | solution.py:286
  85.4 10.3 %all-gather.2 = bf16[8,64,256]{2,1,0:T(8,128)(2,1)S(1)} all-gather(bf16[4,64,256]{2,1,0:T(8,128)(2,1)S(1)} %shard_map.124), channel_id=4, replica_groups=mesh['x'=4,'yh'=2,'c'=2,'yl'=2,'za'=4,'z1'=2,'z0'=2] {'z1'}, dimensions={0}, use_global_device_ids=true | all-gather | bytes 393216 | tf_op jit(solution)/shard_map/all_gather | solution.py:400
  95.7 0.0 collective-permute-done.7.s1
  95.7 0.0 collective-permute-done.8.s2
  95.7 0.0 collective-permute-done.9.s3
  95.7 0.0 copy-done.1
  95.7 2.7 %shard_map.125 = bf16[128,2048]{1,0:T(8,128)(2,1)S(1)} custom-call(s32[4]{0:T(128)S(1)} %pad_add_fusion.place_ref.group_ref, bf16[2,4,64,256]{3,2,1,0:T(8,128)(2,1)S(1)} %bitcast.12, bf16[256,4096]{1,0:T(8,128)(2,1)S(1)} %copy-done.1, bf16[256,1024]{1,0:T(8,128)(2,1)S(1)} %copy-done.6, bf16[256,1024]{1,0:T(8,128)(2,1)} %collective-permute-done.4.r2, ...), custom_call_target="tpu_custom_call" | custom-call | bytes 4096 | tf_op jit(solution)/shard_map/pallas_call | solution.py:270
  98.5 46.8 %all_to_all.15.parts_ref = bf16[16,8,2048]{2,1,0:T(8,128)(2,1)S(1)} all-to-all(bf16[16,8,2048]{2,1,0:T(8,128)(2,1)S(1)} %bitcast.11), channel_id=1, replica_groups=mesh['x'=4,'yh'=2,'c'=2,'yl'=2,'za'=4,'z1'=2,'z0'=2] {'z1','yl','za'}, dimensions={0} | all-to-all | bytes 1048576 | tf_op jit(solution)/shard_map/all_to_all | solution.py:413
  145.2 0.7 shard_map.126
  (9 shorter events, 0.0 us)
Async XLA Ops:
  0.0 7.5 %copy-start = (bf16[256,4096]{1,0:T(8,128)(2,1)S(1)}, bf16[256,4096]{1,0:T(8,128)(2,1)}, u32[]{:S(2)}) copy-start(bf16[256,4096]{1,0:T(8,128)(2,1)} %own_ref) | copy-start | bytes 6291460
  0.1 1.2 copy-start.3
  1.3 0.9 copy-start.9
  2.2 0.7 copy-start.13
  7.5 12.8 %copy-start.7 = (bf16[8,256,128]{2,1,0:T(8,128)(2,1)S(1)}, bf16[8,256,128]{2,1,0:T(8,128)(2,1)}, u32[]{:S(2)}) copy-start(bf16[8,256,128]{2,1,0:T(8,128)(2,1)} %nk_ref.1) | copy-start | bytes 1572868
  7.5 12.8 %copy-start.8 = (bf16[8,256,128]{2,1,0:T(8,128)(2,1)S(1)}, bf16[8,256,128]{2,1,0:T(8,128)(2,1)}, u32[]{:S(2)}) copy-start(bf16[8,256,128]{2,1,0:T(8,128)(2,1)} %nv_ref.1) | copy-start | bytes 1572868
  8.6 20.4 %collective-permute-start = (bf16[256,1024]{1,0:T(8,128)(2,1)}, bf16[256,1024]{1,0:T(8,128)(2,1)S(1)}, u32[]{:S(2)}, u32[]{:S(2)}) collective-permute-start(bf16[256,1024]{1,0:T(8,128)(2,1)} %get-tuple-element.46), channel_id=1, source_target_pairs={{0,1},{1,0},{2,3},{3,2},{4,5},{5,4},{6,7},{7,6},{8,9},{9,8},{10,11... | collective-permute-start | bytes 1572872 | tf_op jit(solution)/shard_map/ppermute | solution.py:290
  12.4 16.6 %all-to-all-start = ((f32[8,136,128]{2,1,0:T(8,128)}), f32[8,136,128]{2,1,0:T(8,128)S(1)}, u32[]{:S(2)}, u32[]{:S(2)}) async-start(f32[8,136,128]{2,1,0:T(8,128)} %shard_map.120), calls=%async_computation | async-start | bytes 1114112 | tf_op jit(solution)/shard_map/all_to_all | solution.py:335
  20.3 1.0 copy-start.11
  21.3 0.9 copy-start.12
  29.0 0.8 copy-start.5
  29.6 10.9 %copy-start.2 = (bf16[8,256,128]{2,1,0:T(8,128)(2,1)S(1)}, bf16[8,256,128]{2,1,0:T(8,128)(2,1)}, u32[]{:S(2)}) copy-start(bf16[8,256,128]{2,1,0:T(8,128)(2,1)} %c_ref.3) | copy-start | bytes 1572868
  29.6 10.9 %copy-start.4 = (bf16[8,256,128]{2,1,0:T(8,128)(2,1)S(1)}, bf16[8,256,128]{2,1,0:T(8,128)(2,1)}, u32[]{:S(2)}) copy-start(bf16[8,256,128]{2,1,0:T(8,128)(2,1)} %b_ref.3) | copy-start | bytes 1572868
  29.6 10.9 %copy-start.10 = (bf16[256,256]{1,0:T(8,128)(2,1)S(1)}, bf16[256,256]{1,0:T(8,128)(2,1)}, u32[]{:S(2)}) copy-start(bf16[256,256]{1,0:T(8,128)(2,1)} %x_ref.3) | copy-start | bytes 393220
  29.6 10.9 %copy-start.14 = (f32[4,256]{1,0:T(4,128)S(1)}, f32[4,256]{1,0:T(4,128)}, u32[]{:S(2)}) copy-start(f32[4,256]{1,0:T(4,128)} %decay_ref.3) | copy-start | bytes 12292
  29.6 10.9 %copy-start.16 = (f32[4]{0:T(128)S(1)}, f32[4]{0:T(128)}, u32[]{:S(2)}) copy-start(f32[4]{0:T(128)} %gain_ref.1) | copy-start | bytes 52
  29.6 14.8 %copy-start.15 = (f32[256]{0:T(256)S(1)}, f32[256]{0:T(256)}, u32[]{:S(2)}) copy-start(f32[256]{0:T(256)} %param.17) | copy-start | bytes 3076
  29.8 35.2 %all-to-all-start.1 = ((bf16[8,784,128]{2,1,0:T(8,128)(2,1)}), bf16[8,784,128]{2,1,0:T(8,128)(2,1)S(1)}, u32[]{:S(2)}, u32[]{:S(2)}) async-start(bf16[8,784,128]{2,1,0:T(8,128)(2,1)} %shard_map.118), calls=%async_computation.1 | async-start | bytes 3211264 | tf_op jit(solution)/shard_map/all_to_all | solution.py:377
  35.3 29.7 %collective-permute-start.4 = (bf16[256,1024]{1,0:T(8,128)(2,1)}, bf16[256,1024]{1,0:T(8,128)(2,1)}, u32[]{:S(2)}, u32[]{:S(2)}) collective-permute-start(bf16[256,1024]{1,0:T(8,128)(2,1)} %get-tuple-element.35), channel_id=1, source_target_pairs={{0,2},{1,3},{2,0},{3,1},{4,6},{5,7},{6,4},{7,5},{8,10},{9,11},{10,... | collective-permute-start | bytes 1572872 | tf_op jit(solution)/shard_map/ppermute | solution.py:290
  42.3 27.8 %copy-start.6 = (bf16[256,1024]{1,0:T(8,128)(2,1)S(1)}, bf16[256,1024]{1,0:T(8,128)(2,1)}, u32[]{:S(2)}) copy-start(bf16[256,1024]{1,0:T(8,128)(2,1)} %copy-done.5) | copy-start | bytes 1572868
  45.4 10.1 %collective-permute-start.1 = (bf16[64,256]{1,0:T(8,128)(2,1)S(1)}, bf16[64,256]{1,0:T(8,128)(2,1)S(1)}, u32[]{:S(2)}, u32[]{:S(2)}) collective-permute-start(bf16[64,256]{1,0:T(8,128)(2,1)S(1)} %get-tuple-element.32), channel_id=1, source_target_pairs={{0,1},{1,0},{2,3},{3,2},{4,5},{5,4},{6,7},{7,6},{8,9},{9,8},{10,11... | collective-permute-start | bytes 98312 | tf_op jit(solution)/shard_map/ppermute | solution.py:290
  47.6 17.4 %collective-permute-start.2 = (bf16[64,256]{1,0:T(8,128)(2,1)S(1)}, bf16[64,256]{1,0:T(8,128)(2,1)S(1)}, u32[]{:S(2)}, u32[]{:S(2)}) collective-permute-start(bf16[64,256]{1,0:T(8,128)(2,1)S(1)} %get-tuple-element.33), channel_id=1, source_target_pairs={{0,2},{1,3},{2,0},{3,1},{4,6},{5,7},{6,4},{7,5},{8,10},{9,11},{10,... | collective-permute-start | bytes 98312 | tf_op jit(solution)/shard_map/ppermute | solution.py:290
  49.6 15.4 %collective-permute-start.3 = (bf16[64,256]{1,0:T(8,128)(2,1)S(1)}, bf16[64,256]{1,0:T(8,128)(2,1)S(1)}, u32[]{:S(2)}, u32[]{:S(2)}) collective-permute-start(bf16[64,256]{1,0:T(8,128)(2,1)S(1)} %get-tuple-element.34), channel_id=1, source_target_pairs={{0,3},{1,2},{2,1},{3,0},{4,7},{5,6},{6,5},{7,4},{8,11},{9,10},{10,... | collective-permute-start | bytes 98312 | tf_op jit(solution)/shard_map/ppermute | solution.py:290
  65.0 30.7 %copy-start.1 = (bf16[256,4096]{1,0:T(8,128)(2,1)S(1)}, bf16[256,4096]{1,0:T(8,128)(2,1)}, u32[]{:S(2)}) copy-start(bf16[256,4096]{1,0:T(8,128)(2,1)} %own_ref) | copy-start | bytes 6291460
  65.0 9.5 %collective-permute-start.5 = (bf16[8,784,128]{2,1,0:T(8,128)(2,1)S(1)}, bf16[8,784,128]{2,1,0:T(8,128)(2,1)S(1)}, u32[]{:S(2)}, u32[]{:S(2)}) collective-permute-start(bf16[8,784,128]{2,1,0:T(8,128)(2,1)S(1)} %all-to-all-done.1.a_ref), channel_id=1, source_target_pairs={{0,32},{32,0},{1,33},{33,1},{2,34},{34,2},{3,35},{35,3},{4,36},{36... | collective-permute-start | bytes 4816904 | tf_op jit(solution)/shard_map/ppermute | solution.py:286
  67.1 16.4 %collective-permute-start.6 = (bf16[256,1024]{1,0:T(8,128)(2,1)}, bf16[256,1024]{1,0:T(8,128)(2,1)S(1)}, u32[]{:S(2)}, u32[]{:S(2)}) collective-permute-start(bf16[256,1024]{1,0:T(8,128)(2,1)} %collective-permute-done.4.r2), channel_id=1, source_target_pairs={{0,1},{1,0},{2,3},{3,2},{4,5},{5,4},{6,7},{7,6},{8,9},{9,8},{10,11... | collective-permute-start | bytes 1572872 | tf_op jit(solution)/shard_map/ppermute | solution.py:290
  70.2 25.5 %collective-permute-start.7 = (bf16[256,1024]{1,0:T(8,128)(2,1)S(1)}, bf16[256,1024]{1,0:T(8,128)(2,1)S(1)}, u32[]{:S(2)}, u32[]{:S(2)}) collective-permute-start(bf16[256,1024]{1,0:T(8,128)(2,1)S(1)} %copy-done.6), channel_id=1, source_target_pairs={{0,32},{32,0},{1,33},{33,1},{2,34},{34,2},{3,35},{35,3},{4,36},{36... | collective-permute-start | bytes 1572872 | tf_op jit(solution)/shard_map/ppermute | solution.py:286
  72.3 23.4 %collective-permute-start.8 = (bf16[256,1024]{1,0:T(8,128)(2,1)}, bf16[256,1024]{1,0:T(8,128)(2,1)S(1)}, u32[]{:S(2)}, u32[]{:S(2)}) collective-permute-start(bf16[256,1024]{1,0:T(8,128)(2,1)} %collective-permute-done.4.r2), channel_id=1, source_target_pairs={{0,32},{32,0},{1,33},{33,1},{2,34},{34,2},{3,35},{35,3},{4,36},{36... | collective-permute-start | bytes 1572872 | tf_op jit(solution)/shard_map/ppermute | solution.py:286
  83.5 12.2 %collective-permute-start.9 = (bf16[256,1024]{1,0:T(8,128)(2,1)S(1)}, bf16[256,1024]{1,0:T(8,128)(2,1)S(1)}, u32[]{:S(2)}, u32[]{:S(2)}) collective-permute-start(bf16[256,1024]{1,0:T(8,128)(2,1)S(1)} %collective-permute-done.6.r3), channel_id=1, source_target_pairs={{0,32},{32,0},{1,33},{33,1},{2,34},{34,2},{3,35},{35,3},{4,36},{36... | collective-permute-start | bytes 1572872 | tf_op jit(solution)/shard_map/ppermute | solution.py:286

commit v2 on v1

v2 whole, which is shorter than its diff:
```python
import functools
import math

import jax
import jax.numpy as jnp
from jax import lax
from jax.experimental import pallas as pl
from jax.experimental.pallas import tpu as pltpu
from jax.sharding import Mesh
from jax.sharding import PartitionSpec as P

CACHE = 128
MH = 128
P_SIZE = 64
HD = 128
TOKENS = 256
SPAN = CACHE + TOKENS
HEAD = 2 * HD + 16
ROWS = HEAD + 2 * SPAN
CHIPS = 8
HIDDEN = -1e30
SCALE = HD ** (-0.5) * math.log2(math.e)

AXES = ("x", "yh", "c", "yl", "za", "z1", "z0")
SIZES = (4, 2, 2, 2, 4, 2, 2)
PIPE = ("x", "yh", "c")
TENSOR = ("yl", "za", "z1", "z0")
CHIP = ("x", "yh")
NEAR = ("z1", "z0")
OWNERS = ("za", "z1")

bf16 = jnp.bfloat16
f32 = jnp.float32


def dot(a, b, contract=((1,), (0,))):
    return lax.dot_general(a, b, (contract, ((), ())), preferred_element_type=f32)


def thirds(value):
    high = value.astype(bf16)
    rest = value - high.astype(f32)
    middle = rest.astype(bf16)
    low = (rest - middle.astype(f32)).astype(bf16)
    return (low, middle, high)


def tri(transposed):
    first = lax.broadcasted_iota(jnp.int32, (TOKENS, TOKENS), 0)
    second = lax.broadcasted_iota(jnp.int32, (TOKENS, TOKENS), 1)
    return (first <= second) if transposed else (first >= second)


def cum_columns(decay):
    lower = tri(False).astype(f32).astype(bf16)
    return sum(dot(lower, part, ((1,), (1,))) for part in thirds(decay))


def cum_rows(decay):
    upper = tri(True).astype(f32).astype(bf16)
    return sum(dot(part, upper) for part in thirds(decay))


def low_lanes(rows):
    return lax.broadcasted_iota(jnp.int32, (rows, 2 * P_SIZE), 1) < P_SIZE


def spread(columns, half, rows):
    left, right = columns[:, 2 * half : 2 * half + 1], columns[:, 2 * half + 1 : 2 * half + 2]
    return jnp.where(low_lanes(rows), left, right)


def state_kernel(group_ref, x_ref, decay_ref, b_ref, out_ref):
    cum = cum_columns(decay_ref[...])
    last = cum[TOKENS - 1 :, :]
    tail = jnp.exp(last - cum)
    total = jnp.exp(-last)
    for half in range(2):
        inputs = x_ref[:, half * HD : (half + 1) * HD].astype(f32)
        weighted = (spread(tail, half, TOKENS) * inputs).astype(bf16)
        out_ref[half, 0:HD, :] = dot(b_ref[0], weighted, ((0,), (0,)))
        out_ref[half, HD : HD + 8, :] = spread(jnp.broadcast_to(total, (8, 4)), half, 8)


def spread_copies(held, out_ref, begin, sems):
    rows = held.shape[0]
    copies = [pltpu.make_async_copy(held, out_ref.at[k, begin : begin + rows], sems.at[k]) for k in range(CHIPS)]
    for copy in copies:
        copy.start()
    for copy in copies:
        copy.wait()


def fill_kernel(place_ref, ck_ref, nk_ref, cv_ref, nv_ref, out_ref, held, sems):
    for begin, ref in ((0, ck_ref), (CACHE, nk_ref), (SPAN, cv_ref), (SPAN + CACHE, nv_ref)):
        held[begin : begin + ref.shape[1], :] = ref[0]
    spread_copies(held, out_ref, HEAD, sems)


def pack_kernel(place_ref, both_ref, len_ref, filled_ref, out_ref, held, sems):
    first, second = both_ref[0, 0], both_ref[1, 0]
    state = first[0:HD] * second[HD : HD + 1] + second[0:HD]
    high = state.astype(bf16)
    held[0:HD, :] = high
    held[HD : 2 * HD, :] = (state - high.astype(f32)).astype(bf16)
    slots = lax.broadcasted_iota(jnp.int32, (16, HD), 1)
    row = lax.broadcasted_iota(jnp.int32, (16, HD), 0)
    tile = jnp.where(slots < len_ref[0], 0.0, HIDDEN)
    for i, part in enumerate(thirds(first[HD : HD + 1] * second[HD : HD + 1])):
        tile = jnp.where(row == i + 1, part.astype(f32), tile)
    held[2 * HD : HEAD, :] = tile.astype(bf16)
    spread_copies(held, out_ref, 0, sems)


def scan_kernel(place_ref, all_ref, out_ref):
    chip = place_ref[0]
    state = jnp.zeros((HD, HD), f32)
    for k in range(CHIPS - 1):
        tile = all_ref[k, 2 * HD : HEAD, :].astype(f32)
        decay = tile[1:2] + tile[2:3] + tile[3:4]
        here = all_ref[k, 0:HD, :].astype(f32) + all_ref[k, HD : 2 * HD, :].astype(f32)
        state = jnp.where(k < chip, decay * state + here, state)
    out_ref[...] = state


def inside_kernel(group_ref, x_ref, decay_ref, b_ref, c_ref, gain_ref, y_ref, fade_ref):
    decay = decay_ref[...]
    columns, rows = cum_columns(decay), cum_rows(decay)
    causal = tri(False)
    gram = dot(c_ref[0], b_ref[0], ((1,), (1,)))
    fade = jnp.exp(-columns)
    for half in range(2):
        inputs = x_ref[:, half * HD : (half + 1) * HD]
        pieces = []
        for head in (2 * half, 2 * half + 1):
            diff = jnp.where(causal, columns[:, head : head + 1] - rows[head : head + 1, :], 0.0)
            weights = jnp.where(causal, gram * jnp.exp(-diff), 0.0).astype(bf16)
            pieces.append(dot(weights, inputs))
        low = low_lanes(TOKENS)
        skip = jnp.where(low_lanes(1), gain_ref[2 * half], gain_ref[2 * half + 1])
        y_ref[half] = jnp.where(low, pieces[0], pieces[1]) + skip * inputs.astype(f32)
        fade_ref[half] = spread(fade, half, TOKENS)


def query_kernel(place_ref, y_ref, fade_ref, c_ref, carried_ref, both_ref, gain_ref, out_ref):
    core = place_ref[1]
    readout = c_ref[0]
    low = low_lanes(TOKENS)
    for half in range(2):
        carried = carried_ref[half]
        after = both_ref[0, half, HD : HD + 1] * carried + both_ref[0, half, 0:HD]
        carried = jnp.where(core == 1, after, carried)
        from_state = sum(dot(readout, part) for part in thirds(carried))
        y = y_ref[half] + fade_ref[half] * from_state
        square = y * y
        left = jnp.sum(jnp.where(low, square, 0.0), axis=1, keepdims=True)
        right = jnp.sum(jnp.where(low, 0.0, square), axis=1, keepdims=True)
        mean = jnp.where(low, left, right) * (1.0 / P_SIZE)
        normed = y * lax.rsqrt(mean + 1e-05) * gain_ref[0:1, half * HD : (half + 1) * HD]
        out_ref[half * TOKENS : (half + 1) * TOKENS, :] = normed.astype(bf16)


def attend_kernel(place_ref, q_ref, a_ref, b_ref, out_ref, scores_ref, top_ref, sum_ref, acc_ref):
    chip, core = place_ref[0], place_ref[1]
    count = q_ref.shape[0]
    sides = (a_ref, b_ref)
    top_ref[...] = jnp.full((count, HD), -jnp.inf, f32)

    def score(k, side, extra, causal):
        bias = sides[side][k, 2 * HD : HEAD, :].astype(f32)[0:1]
        raw = dot(q_ref[...], sides[side][k, HEAD : HEAD + SPAN, :], ((1,), (1,)))
        top = top_ref[...]
        for tile in range(SPAN // HD):
            part = raw[:, tile * HD : (tile + 1) * HD]
            if tile == 0:
                part = part + (bias if extra is None else bias + extra)
            elif causal:
                token = lax.broadcasted_iota(jnp.int32, (count, HD), 0) % TOKENS
                key = lax.broadcasted_iota(jnp.int32, (count, HD), 1) + (tile - 1) * HD
                part = jnp.where(key <= token, part, HIDDEN)
            elif extra is not None:
                part = part + extra
            top = jnp.maximum(top, part)
            scores_ref[k, :, side * SPAN + tile * HD : side * SPAN + (tile + 1) * HD] = part
        top_ref[...] = top

    def early(k, carry):
        score(k, 0, None, False)
        score(k, 1, None, False)
        return carry

    lax.fori_loop(0, chip, early, 0)
    score(chip, 0, None, True)
    score(chip, 1, jnp.where(core == 1, 0.0, HIDDEN), False)

    top = jnp.max(top_ref[...], axis=1, keepdims=True) * SCALE
    top_ref[...] = jnp.broadcast_to(top, (count, HD))
    sum_ref[...] = jnp.zeros((count, HD), f32)
    acc_ref[...] = jnp.zeros((count, HD), f32)

    def late(k, carry):
        top = top_ref[...]
        total = sum_ref[...]
        acc = acc_ref[...]
        for side in range(2):
            probs = []
            for tile in range(SPAN // HD):
                part = scores_ref[k, :, side * SPAN + tile * HD : side * SPAN + (tile + 1) * HD]
                expo = jnp.exp2(part * SCALE - top)
                total = total + expo
                probs.append(expo.astype(bf16))
            acc = acc + dot(jnp.concatenate(probs, axis=1), sides[side][k, HEAD + SPAN :, :])
        sum_ref[...] = total
        acc_ref[...] = acc
        return carry

    lax.fori_loop(0, chip + 1, late, 0)
    total = jnp.sum(sum_ref[...], axis=1, keepdims=True)
    result = acc_ref[...] / total
    for z0 in range(2):
        for half in range(2):
            blocks = [16 * yl + 4 * za + 2 * z1 + z0 for yl in range(2) for za in range(4) for z1 in range(2)]
            rows = [half * TOKENS + 8 * block for block in blocks]
            piece = jnp.concatenate([result[row : row + 8] for row in rows], axis=0).astype(bf16)
            for z1 in range(2):
                out_ref[2 * z1 + z0, :, half * HD : (half + 1) * HD] = piece


def project_kernel(place_ref, att_ref, own_ref, r1, r2, r3, s1, s2, s3, keep_ref, send_ref):
    near, core, side = place_ref[2], place_ref[1], place_ref[3] // 4
    rows, width = keep_ref.shape[0], r1.shape[1]

    def run(others, begin):
        total = dot(att_ref[near], own_ref[:, begin : begin + width])
        for i, ref in enumerate(others):
            total = total + dot(att_ref[near ^ (i + 1)], ref[...])
        total = total.astype(bf16)

        @pl.when(side == 0)
        def _():
            keep_ref[:, begin : begin + width] = total[:rows]
            send_ref[:, begin : begin + width] = total[rows:]

        @pl.when(side == 1)
        def _():
            keep_ref[:, begin : begin + width] = total[rows:]
            send_ref[:, begin : begin + width] = total[:rows]

    @pl.when(core == 0)
    def _():
        run((r1, r2, r3), 0)
        run((s1, s2, s3), width)

    @pl.when(core == 1)
    def _():
        run((s1, s2, s3), 0)
        run((r1, r2, r3), width)


def add_kernel(first_ref, second_ref, out_ref):
    out_ref[...] = (first_ref[...].astype(f32) + second_ref[...].astype(f32)).astype(bf16)


def finish_kernel(parts_ref, out_ref):
    for half in range(2):
        total = parts_ref[half].astype(f32)
        for i in range(1, 4):
            total = total + parts_ref[2 * i + half].astype(f32)
        width = parts_ref.shape[2]
        out_ref[:, half * width : (half + 1) * width] = total.astype(bf16)


def whole(shape):
    return pl.BlockSpec(shape, lambda *_: (0,) * len(shape))


SMEM = pl.BlockSpec(memory_space=pltpu.SMEM)


def call(kernel, scalars, args, in_specs, out_shape, out_specs, grid=(1,), scratch=(), room=40, aliases=None):
    return pl.pallas_call(
        kernel,
        out_shape=out_shape,
        grid_spec=pltpu.PrefetchScalarGridSpec(
            num_scalar_prefetch=1, grid=grid, in_specs=in_specs, out_specs=out_specs, scratch_shapes=scratch
        ),
        input_output_aliases=aliases or {},
        compiler_params=pltpu.CompilerParams(vmem_limit_bytes=room * 1024 * 1024),
        cost_estimate=pl.CostEstimate(flops=0, bytes_accessed=1 << 12, transcendentals=0),
    )(scalars, *args)


def shape(*dims, dtype=f32):
    return jax.ShapeDtypeStruct(dims, dtype)


def swap(array, axis):
    return lax.ppermute(array, axis, [(0, 1), (1, 0)])


def flip(array, i):
    return lax.ppermute(array, NEAR, [(j, j ^ i) for j in range(4)])


def per_device(
    ssm_inputs,
    step_decay,
    state_inputs,
    state_readout,
    skip_gain,
    norm_gain,
    new_keys,
    new_values,
    cache_keys,
    cache_values,
    cache_len,
    out_weight,
):
    width = out_weight.shape[1] // 4
    core = lax.axis_index("c")
    near = lax.axis_index(NEAR)
    group = lax.axis_index(("yl", "za")).astype(jnp.int32)
    place = jnp.stack([lax.axis_index(CHIP), core, near, group]).astype(jnp.int32)
    of_group = lambda rows: pl.BlockSpec((1, rows, HD), lambda i, s: (s[3], 0, 0))

    filled = call(
        fill_kernel,
        place,
        (cache_keys, new_keys, cache_values, new_values),
        [of_group(CACHE), of_group(TOKENS), of_group(CACHE), of_group(TOKENS)],
        shape(CHIPS, ROWS, HD, dtype=bf16),
        pl.BlockSpec(memory_space=pl.ANY),
        scratch=[pltpu.VMEM((2 * SPAN, HD), bf16), pltpu.SemaphoreType.DMA((CHIPS,))],
        room=60,
    )
    place, filled = lax.optimization_barrier((place, filled))

    own = call(
        state_kernel,
        place,
        (ssm_inputs, step_decay, state_inputs),
        [whole((TOKENS, 2 * HD)), whole((4, TOKENS)), of_group(TOKENS)],
        shape(2, HD + 8, HD),
        whole((2, HD + 8, HD)),
    )
    both = lax.all_gather(own, "c")
    packed = call(
        pack_kernel,
        place,
        (both, cache_len, filled),
        [
            pl.BlockSpec((2, 1, HD + 8, HD), lambda i, s: (0, s[1], 0, 0)),
            SMEM,
            pl.BlockSpec(memory_space=pl.ANY),
        ],
        shape(CHIPS, ROWS, HD, dtype=bf16),
        pl.BlockSpec(memory_space=pl.ANY),
        scratch=[pltpu.VMEM((HEAD, HD), bf16), pltpu.SemaphoreType.DMA((CHIPS,))],
        room=60,
        aliases={3: 0},
    )

    columns = lambda quarter: lax.dynamic_slice_in_dim(out_weight, quarter * width, width, 1)
    second = flip(columns(2 * (1 - near // 2) + core), 2)
    first = flip(columns(2 * (near // 2) + core), 1)
    third = flip(second, 1)
    own_columns = lax.dynamic_slice_in_dim(out_weight, 2 * (near // 2) * width, 2 * width, 1)
    same = lax.all_to_all(packed, CHIP, 0, 0, tiled=True)
    inside, fade = call(
        inside_kernel,
        place,
        (ssm_inputs, step_decay, state_inputs, state_readout, skip_gain),
        [whole((TOKENS, 2 * HD)), whole((4, TOKENS)), of_group(TOKENS), of_group(TOKENS), SMEM],
        (shape(2, TOKENS, HD), shape(2, TOKENS, HD)),
        (whole((2, TOKENS, HD)), whole((2, TOKENS, HD))),
    )
    same, first, second, inside, fade, own_columns = lax.optimization_barrier(
        (same, first, second, inside, fade, own_columns)
    )
    other = swap(same, "c")
    entering = call(
        scan_kernel,
        place,
        (same,),
        [pl.BlockSpec((CHIPS, HEAD, HD), lambda i, s: (0, 0, 0))],
        shape(HD, HD),
        whole((HD, HD)),
    )
    carried = lax.all_gather(entering, "c")
    queries = call(
        query_kernel,
        place,
        (inside, fade, state_readout, carried, both, norm_gain.reshape(1, 2 * HD)),
        [
            whole((2, TOKENS, HD)),
            whole((2, TOKENS, HD)),
            of_group(TOKENS),
            whole((2, HD, HD)),
            whole((2, 2, HD + 8, HD)),
            whole((1, 2 * HD)),
        ],
        shape(2 * TOKENS, HD, dtype=bf16),
        whole((2 * TOKENS, HD)),
    )

    attended = call(
        attend_kernel,
        place,
        (queries, same, other),
        [whole((2 * TOKENS, HD))] + [whole((CHIPS, ROWS, HD))] * 2,
        shape(4, TOKENS // 2, 2 * HD, dtype=bf16),
        whole((4, TOKENS // 2, 2 * HD)),
        scratch=[
            pltpu.VMEM((CHIPS, 2 * TOKENS, 2 * SPAN), f32),
            pltpu.VMEM((2 * TOKENS, HD), f32),
            pltpu.VMEM((2 * TOKENS, HD), f32),
            pltpu.VMEM((2 * TOKENS, HD), f32),
        ],
    )
    attended, first, second = lax.optimization_barrier((attended, first, second))
    received = (first, second, third)
    swapped = [swap(part, "c") for part in received]
    attended = lax.all_to_all(attended, NEAR, 0, 0, tiled=True)
    vmem = pl.BlockSpec(memory_space=pltpu.VMEM)
    keep, send = call(
        project_kernel,
        place,
        (attended, own_columns, *received, *swapped),
        [vmem] * 8,
        (shape(64, 2 * width, dtype=bf16),) * 2,
        (vmem,) * 2,
    )
    simple = functools.partial(pl.pallas_call, compiler_params=pltpu.CompilerParams(vmem_limit_bytes=40 * 1024 * 1024))
    partial = simple(add_kernel, out_shape=shape(64, 2 * width, dtype=bf16))(keep, swap(send, "yl"))
    parts = lax.all_to_all(partial.reshape(8, 8, 2 * width), OWNERS, 0, 0, tiled=True)
    return simple(finish_kernel, out_shape=shape(8, 4 * width, dtype=bf16))(parts)


def solution(mesh):
    fine = Mesh(mesh.devices.reshape(SIZES), AXES)
    placed = (
        P(PIPE, TENSOR),
        P(TENSOR, PIPE),
        P(None, PIPE, None),
        P(None, PIPE, None),
        P(TENSOR),
        P(TENSOR),
        P(None, PIPE, None),
        P(None, PIPE, None),
        P(None, PIPE, None),
        P(None, PIPE, None),
        P(PIPE),
        P(TENSOR, None),
    )
    return jax.shard_map(
        per_device,
        mesh=fine,
        in_specs=placed,
        out_specs=P(PIPE + TENSOR, None),
        check_vma=False,
    )
```

time: 147 us -> 129 us (0.88)
  blocking collectives: 61.1 us -> 38 us
  waiting for transfers between devices: 19.4 us -> 32.2 us
  starting transfers between devices: 43.3 us -> 33.2 us
  Pallas kernels: 15.3 us -> 16.8 us
    all_to_all x1, blocking collectives: 46.8 us -> 33.9 us  [per_device(): lax.all_to_all(partial.reshape(8, 8, 2 * width), OWNERS, 0, 0, tiled=True)]
    ppermute x6 -> x3, starting transfers between devices: 22.2 us -> 10.9 us  [flip(): return lax.ppermute(array, NEAR, [(j, j ^ i) for j in range(4)])]
    all_gather x1 -> x0, blocking collectives: 10.3 us -> none  [per_device(): attended = lax.all_gather(attended, 'z1')]
    ppermute x4 -> x5, waiting for transfers between devices: 0.01 us -> 9.64 us  [swap(): return lax.ppermute(array, axis, [(0, 1), (1, 0)])]
    ppermute x6 -> x3, waiting for transfers between devices: 16.1 us -> 22.5 us  [flip(): return lax.ppermute(array, NEAR, [(j, j ^ i) for j in range(4)])]
    unnamed x34 -> x28, local copies, waits for them, and re-layouts: 4.84 us -> 1.47 us
    all_to_all x1, waiting for transfers between devices: 3.29 us -> 0.01 us  [per_device(): attended = lax.all_to_all(attended, NEAR, 0, 0, tiled=True)]
    all_to_all x1, starting transfers between devices: 7.27 us -> 4.03 us  [per_device(): attended = lax.all_to_all(attended, NEAR, 0, 0, tiled=True)]
  transfers between devices with their start and end apart: 12 -> 10, of which waited for: 3 -> 5; matrix products, arithmetic and copies ran while one was open for 0% -> 3% of each run, Pallas kernels for 6% -> 5%
where the time goes in v2:
time: 129 us; the launch traced here: 127 us
  blocking collectives  38 us (29%)
  starting transfers between devices  33.2 us (26%)
  waiting for transfers between devices  32.2 us (25%)
  Pallas kernels  16.8 us (13%)
  local copies, waits for them, and re-layouts  5.09 us (4%)
    all_to_all x1, blocking collectives, per_device(): lax.all_to_all(partial.reshape(8, 8, 2 * width), OWNERS, 0, 0, tiled=True)  33.9 us
    ppermute x3, waiting for transfers between devices, flip(): return lax.ppermute(array, NEAR, [(j, j ^ i) for j in range(4)])  22.5 us
    pallas_call x8, Pallas kernels, call(): pl.pallas_call(kernel, out_shape=out_shape, grid_spec=pltpu.PrefetchScala...  16.1 us
    ppermute x5, starting transfers between devices, swap(): return lax.ppermute(array, axis, [(0, 1), (1, 0)])  10.9 us
    ppermute x3, starting transfers between devices, flip(): return lax.ppermute(array, NEAR, [(j, j ^ i) for j in range(4)])  10.9 us
    ppermute x5, waiting for transfers between devices, swap(): return lax.ppermute(array, axis, [(0, 1), (1, 0)])  9.64 us
    all_to_all x1, starting transfers between devices, per_device(): same = lax.all_to_all(packed, CHIP, 0, 0, tiled=True)  7.27 us
    all_to_all x1, starting transfers between devices, per_device(): attended = lax.all_to_all(attended, NEAR, 0, 0, tiled=True)  4.03 us
  transfers between devices with their start and end apart: 10, of which 5 were waited for; matrix products, arithmetic and copies ran while one was open for 3% of the time, Pallas kernels for 5%

profile of v2, /device:TPU:24, one launch (start us, length us, event | category | flops | bytes accessed | tf_op | source)
XLA Modules:
  0.0 126.8 jit_solution(13090679842962071920)
XLA Ops:
  0.0 0.0 copy-start.4
  0.0 0.0 copy-start.11
  0.0 0.0 copy-start.3
  0.0 0.6 pad_add_fusion.place_ref.group_ref
  0.6 0.0 copy-start.9
  0.6 3.0 %shard_map.118.filled_ref = bf16[8,1040,128]{2,1,0:T(8,128)(2,1)} custom-call(s32[4]{0:T(128)} %pad_add_fusion.place_ref.group_ref, bf16[8,128,128]{2,1,0:T(8,128)(2,1)} %ck_ref.1, bf16[8,256,128]{2,1,0:T(8,128)(2,1)} %nk_ref.1, bf16[8,128,128]{2,1,0:T(8,128)(2,1)} %cv_ref.1, bf16[8,256,128]{2,1,0:T(8,128)(2,1)} %nv_ref.1), custom_call_target="tpu_custom_call" | custom-call | bytes 4096 | tf_op jit(solution)/shard_map/pallas_call | solution.py:281
  3.6 0.0 copy-done.4
  3.6 0.0 copy-done.11
  3.6 0.0 copy-done.3
  3.7 0.0 copy-done.9
  3.7 1.2 shard_map.119
  4.9 2.1 %all-gather = f32[4,136,128]{2,1,0:T(8,128)} all-gather(f32[2,136,128]{2,1,0:T(8,128)S(1)} %shard_map.119), channel_id=2, replica_groups=mesh['x'=4,'yh'=2,'c'=2,'yl'=2,'za'=4,'z1'=2,'z0'=2] {'c'}, dimensions={0}, use_global_device_ids=true | all-gather | bytes 417792 | tf_op jit(solution)/shard_map/all_gather | solution.py:346
  7.7 2.5 %shard_map.120 = bf16[8,1040,128]{2,1,0:T(8,128)(2,1)} custom-call(s32[4]{0:T(128)} %pad_add_fusion.place_ref.group_ref, f32[2,2,136,128]{3,2,1,0:T(8,128)} %bitcast.8, s32[1]{0:T(128)S(6)} %copy.15.len_ref, bf16[8,1040,128]{2,1,0:T(8,128)(2,1)} %shard_map.118.filled_ref), custom_call_target="tpu_custom_call", output_to_operand_aliasing={{}: (3, {})} | custom-call | bytes 4096 | tf_op jit(solution)/shard_map/pallas_call | solution.py:281
  10.2 7.3 %all-to-all-start = ((bf16[8,1040,128]{2,1,0:T(8,128)(2,1)}), bf16[8,1040,128]{2,1,0:T(8,128)(2,1)S(1)}, u32[]{:S(2)}, u32[]{:S(2)}) async-start(bf16[8,1040,128]{2,1,0:T(8,128)(2,1)} %shard_map.120), calls=%async_computation | async-start | bytes 4259840 | tf_op jit(solution)/shard_map/all_to_all | solution.py:368
  17.5 0.0 copy-start.1
  17.5 0.0 copy-start.10
  17.5 0.0 copy-start.13
  17.5 2.3 %constant_dynamic-slice_fusion.1 = (bf16[256,1024]{1,0:T(8,128)(2,1)}, bf16[256,1024]{1,0:T(8,128)(2,1)}) fusion(bf16[256,4096]{1,0:T(8,128)(2,1)} %param.23, s32[]{:T(128)S(6)} %select_n.18, s32[]{:T(128)S(6)} %select_n.17), kind=kLoop, calls=%fused_computation.1 | loop fusion | bytes 2097160 | tf_op jit(solution)/shard_map/dynamic_slice | solution.py:363
  19.8 3.8 %collective-permute-start = (bf16[256,1024]{1,0:T(8,128)(2,1)}, bf16[256,1024]{1,0:T(8,128)(2,1)}, u32[]{:S(2)}, u32[]{:S(2)}) collective-permute-start(bf16[256,1024]{1,0:T(8,128)(2,1)} %get-tuple-element.36), channel_id=1, source_target_pairs={{0,1},{1,0},{2,3},{3,2},{4,5},{5,4},{6,7},{7,6},{8,9},{9,8},{10,11... | collective-permute-start | bytes 1572872 | tf_op jit(solution)/shard_map/ppermute | solution.py:302
  23.6 5.2 %collective-permute-start.1 = (bf16[256,1024]{1,0:T(8,128)(2,1)}, bf16[256,1024]{1,0:T(8,128)(2,1)}, u32[]{:S(2)}, u32[]{:S(2)}) collective-permute-start(bf16[256,1024]{1,0:T(8,128)(2,1)} %get-tuple-element.35), channel_id=1, source_target_pairs={{0,2},{1,3},{2,0},{3,1},{4,6},{5,7},{6,4},{7,5},{8,10},{9,11},{10,... | collective-permute-start | bytes 1572872 | tf_op jit(solution)/shard_map/ppermute | solution.py:302
  28.8 0.0 copy-done.1
  28.8 0.0 copy-done.10
  28.8 0.0 copy-done.13
  28.8 1.8 %shard_map.121 = (f32[2,256,128]{2,1,0:T(8,128)S(1)}, f32[2,256,128]{2,1,0:T(8,128)S(1)}) custom-call(s32[4]{0:T(128)S(1)} %copy-done.10, bf16[256,256]{1,0:T(8,128)(2,1)S(1)} %copy-done.4, f32[4,256]{1,0:T(4,128)S(1)} %copy-done.11, bf16[8,256,128]{2,1,0:T(8,128)(2,1)S(1)} %copy-done.3, bf16[8,256,128]{2,1,0:T(8,128)(2,1)S(1)} %copy-done.1, f32[4]{0:T(128)S(1)} %copy-done.13), custom_call_target="tpu_custom_call" | custom-call | bytes 4096 | tf_op jit(solution)/shard_map/pallas_call | solution.py:281
  30.6 0.0 copy-start.5
  30.7 0.7 copy-done.5
  31.4 0.0 copy-start.7
  31.4 0.7 copy-done.7
  32.1 0.0 copy-start
  32.1 0.0 copy-start.12
  32.1 1.3 %constant_dynamic-slice_fusion.own_ref = bf16[256,2048]{1,0:T(8,128)(2,1)S(1)} fusion(bf16[256,4096]{1,0:T(8,128)(2,1)} %param.23, s32[]{:T(128)S(6)} %select_n.19), kind=kLoop, calls=%fused_computation | loop fusion | bytes 2097156 | tf_op jit(solution)/shard_map/dynamic_slice | solution.py:367
  33.4 11.3 %collective-permute-done.r1 = bf16[256,1024]{1,0:T(8,128)(2,1)} collective-permute-done((bf16[256,1024]{1,0:T(8,128)(2,1)}, bf16[256,1024]{1,0:T(8,128)(2,1)}, u32[]{:S(2)}, u32[]{:S(2)}) %collective-permute-start) | collective-permute-done | bytes 524320 | tf_op jit(solution)/shard_map/ppermute | solution.py:302
  44.7 7.1 %collective-permute-done.1.r2 = bf16[256,1024]{1,0:T(8,128)(2,1)} collective-permute-done((bf16[256,1024]{1,0:T(8,128)(2,1)}, bf16[256,1024]{1,0:T(8,128)(2,1)}, u32[]{:S(2)}, u32[]{:S(2)}) %collective-permute-start.1) | collective-permute-done | bytes 524320 | tf_op jit(solution)/shard_map/ppermute | solution.py:302
  51.8 0.0 all-to-all-done.all_ref.a_ref
  51.8 0.0 copy-start.2
  51.8 0.0 copy-start.6
  51.8 0.0 copy-start.8
  51.8 2.1 %collective-permute-start.2 = (bf16[8,1040,128]{2,1,0:T(8,128)(2,1)S(1)}, bf16[8,1040,128]{2,1,0:T(8,128)(2,1)S(1)}, u32[]{:S(2)}, u32[]{:S(2)}) collective-permute-start(bf16[8,1040,128]{2,1,0:T(8,128)(2,1)S(1)} %all-to-all-done.all_ref.a_ref), channel_id=1, source_target_pairs={{0,32},{32,0},{1,33},{33,1},{2,34},{34,2},{3,35},{35,3},{4,36},{36... | collective-permute-start | bytes 6389768 | tf_op jit(solution)/shard_map/ppermute | solution.py:298
  53.9 1.9 %collective-permute-start.3 = (bf16[256,1024]{1,0:T(8,128)(2,1)}, bf16[256,1024]{1,0:T(8,128)(2,1)}, u32[]{:S(2)}, u32[]{:S(2)}) collective-permute-start(bf16[256,1024]{1,0:T(8,128)(2,1)} %collective-permute-done.1.r2), channel_id=1, source_target_pairs={{0,1},{1,0},{2,3},{3,2},{4,5},{5,4},{6,7},{7,6},{8,9},{9,8},{10,11... | collective-permute-start | bytes 1572872 | tf_op jit(solution)/shard_map/ppermute | solution.py:302
  55.8 0.7 shard_map.122
  56.5 2.0 %all-gather.1 = f32[256,128]{1,0:T(8,128)S(1)} all-gather(f32[128,128]{1,0:T(8,128)S(1)} %shard_map.122), channel_id=3, replica_groups=mesh['x'=4,'yh'=2,'c'=2,'yl'=2,'za'=4,'z1'=2,'z0'=2] {'c'}, dimensions={0}, use_global_device_ids=true | all-gather | bytes 196608 | tf_op jit(solution)/shard_map/all_gather | solution.py:389
  58.5 0.0 copy-done
  58.5 0.0 copy-done.12
  58.5 0.0 copy-done.2
  58.5 0.0 copy-done.6
  58.5 0.0 copy-done.8
  58.5 1.0 shard_map.123.q_ref
  59.5 0.0 collective-permute-done.2.b_ref
  59.6 3.0 %shard_map.124 = bf16[4,128,256]{2,1,0:T(8,128)(2,1)} custom-call(s32[4]{0:T(128)S(1)} %copy-done.10, bf16[512,128]{1,0:T(8,128)(2,1)S(1)} %shard_map.123.q_ref, bf16[8,1040,128]{2,1,0:T(8,128)(2,1)S(1)} %all-to-all-done.all_ref.a_ref, bf16[8,1040,128]{2,1,0:T(8,128)(2,1)S(1)} %collective-permute-done.2.b_ref), custom_call_target="tpu_custom_call" | custom-call | bytes 4096 | tf_op jit(solution)/shard_map/pallas_call | solution.py:281
  62.6 4.0 %all-to-all-start.1 = ((bf16[4,128,256]{2,1,0:T(8,128)(2,1)}), bf16[4,128,256]{2,1,0:T(8,128)(2,1)S(1)}, u32[]{:S(2)}, u32[]{:S(2)}) async-start(bf16[4,128,256]{2,1,0:T(8,128)(2,1)} %shard_map.124), calls=%async_computation.1 | async-start | bytes 524288 | tf_op jit(solution)/shard_map/all_to_all | solution.py:423
  66.6 4.2 %collective-permute-done.3.r3 = bf16[256,1024]{1,0:T(8,128)(2,1)} collective-permute-done((bf16[256,1024]{1,0:T(8,128)(2,1)}, bf16[256,1024]{1,0:T(8,128)(2,1)}, u32[]{:S(2)}, u32[]{:S(2)}) %collective-permute-start.3) | collective-permute-done | bytes 524320 | tf_op jit(solution)/shard_map/ppermute | solution.py:302
  70.8 1.9 %collective-permute-start.6 = (bf16[256,1024]{1,0:T(8,128)(2,1)}, bf16[256,1024]{1,0:T(8,128)(2,1)S(1)}, u32[]{:S(2)}, u32[]{:S(2)}) collective-permute-start(bf16[256,1024]{1,0:T(8,128)(2,1)} %collective-permute-done.3.r3), channel_id=1, source_target_pairs={{0,32},{32,0},{1,33},{33,1},{2,34},{34,2},{3,35},{35,3},{4,36},{36... | collective-permute-start | bytes 1572872 | tf_op jit(solution)/shard_map/ppermute | solution.py:298
  72.7 2.4 %collective-permute-start.4 = (bf16[256,1024]{1,0:T(8,128)(2,1)}, bf16[256,1024]{1,0:T(8,128)(2,1)S(1)}, u32[]{:S(2)}, u32[]{:S(2)}) collective-permute-start(bf16[256,1024]{1,0:T(8,128)(2,1)} %collective-permute-done.r1), channel_id=1, source_target_pairs={{0,32},{32,0},{1,33},{33,1},{2,34},{34,2},{3,35},{35,3},{4,36},{36... | collective-permute-start | bytes 1572872 | tf_op jit(solution)/shard_map/ppermute | solution.py:298
  75.1 1.9 %collective-permute-start.5 = (bf16[256,1024]{1,0:T(8,128)(2,1)}, bf16[256,1024]{1,0:T(8,128)(2,1)S(1)}, u32[]{:S(2)}, u32[]{:S(2)}) collective-permute-start(bf16[256,1024]{1,0:T(8,128)(2,1)} %collective-permute-done.1.r2), channel_id=1, source_target_pairs={{0,32},{32,0},{1,33},{33,1},{2,34},{34,2},{3,35},{35,3},{4,36},{36... | collective-permute-start | bytes 1572872 | tf_op jit(solution)/shard_map/ppermute | solution.py:298
  77.0 0.0 collective-permute-done.6.s3
  77.1 0.0 collective-permute-done.4.s1
  77.1 2.1 %collective-permute-done.5.s2 = bf16[256,1024]{1,0:T(8,128)(2,1)S(1)} collective-permute-done((bf16[256,1024]{1,0:T(8,128)(2,1)}, bf16[256,1024]{1,0:T(8,128)(2,1)S(1)}, u32[]{:S(2)}, u32[]{:S(2)}) %collective-permute-start.5) | collective-permute-done | bytes 524320 | tf_op jit(solution)/shard_map/ppermute | solution.py:298
  79.1 0.0 all-to-all-done.1.att_ref
  79.1 2.8 %shard_map.125 = (bf16[64,2048]{1,0:T(8,128)(2,1)S(1)}, bf16[64,2048]{1,0:T(8,128)(2,1)S(1)}) custom-call(s32[4]{0:T(128)S(1)} %copy-done.10, bf16[4,128,256]{2,1,0:T(8,128)(2,1)S(1)} %all-to-all-done.1.att_ref, bf16[256,2048]{1,0:T(8,128)(2,1)S(1)} %constant_dynamic-slice_fusion.own_ref, bf16[256,1024]{1,0:T(8,128)(2,1)} %collective-permute-done.r1, ...), custom_call_target="tpu_custom_call" | custom-call | bytes 4096 | tf_op jit(solution)/shard_map/pallas_call | solution.py:281
  82.0 2.7 %collective-permute-start.7 = (bf16[64,2048]{1,0:T(8,128)(2,1)S(1)}, bf16[64,2048]{1,0:T(8,128)(2,1)S(1)}, u32[]{:S(2)}, u32[]{:S(2)}) collective-permute-start(bf16[64,2048]{1,0:T(8,128)(2,1)S(1)} %get-tuple-element.34), channel_id=1, source_target_pairs={{0,16},{16,0},{1,17},{17,1},{2,18},{18,2},{3,19},{19,3},{4,20},{20... | collective-permute-start | bytes 786440 | tf_op jit(solution)/shard_map/ppermute | solution.py:298
  84.6 7.6 %collective-permute-done.7.second_ref = bf16[64,2048]{1,0:T(8,128)(2,1)S(1)} collective-permute-done((bf16[64,2048]{1,0:T(8,128)(2,1)S(1)}, bf16[64,2048]{1,0:T(8,128)(2,1)S(1)}, u32[]{:S(2)}, u32[]{:S(2)}) %collective-permute-start.7) | collective-permute-done | bytes 262176 | tf_op jit(solution)/shard_map/ppermute | solution.py:298
  92.2 0.1 shard_map.126
  92.3 33.9 %all_to_all.15.parts_ref = bf16[8,8,2048]{2,1,0:T(8,128)(2,1)S(1)} all-to-all(bf16[8,8,2048]{2,1,0:T(8,128)(2,1)S(1)} %bitcast.10), channel_id=1, replica_groups=mesh['x'=4,'yh'=2,'c'=2,'yl'=2,'za'=4,'z1'=2,'z0'=2] {'za','z1'}, dimensions={0} | all-to-all | bytes 524288 | tf_op jit(solution)/shard_map/all_to_all | solution.py:435
  126.1 0.7 shard_map.127
Async XLA Ops:
  0.0 3.6 %copy-start.4 = (bf16[256,256]{1,0:T(8,128)(2,1)S(1)}, bf16[256,256]{1,0:T(8,128)(2,1)}, u32[]{:S(2)}) copy-start(bf16[256,256]{1,0:T(8,128)(2,1)} %x_ref.3) | copy-start | bytes 393220
  0.0 3.6 %copy-start.11 = (f32[4,256]{1,0:T(4,128)S(1)}, f32[4,256]{1,0:T(4,128)}, u32[]{:S(2)}) copy-start(f32[4,256]{1,0:T(4,128)} %decay_ref.3) | copy-start | bytes 12292
  0.0 3.6 %copy-start.3 = (bf16[8,256,128]{2,1,0:T(8,128)(2,1)S(1)}, bf16[8,256,128]{2,1,0:T(8,128)(2,1)}, u32[]{:S(2)}) copy-start(bf16[8,256,128]{2,1,0:T(8,128)(2,1)} %b_ref.3) | copy-start | bytes 1572868
  0.6 3.0 %copy-start.9 = (s32[4]{0:T(128)S(1)}, s32[4]{0:T(128)}, u32[]{:S(2)}) copy-start(s32[4]{0:T(128)} %pad_add_fusion.place_ref.group_ref) | copy-start | bytes 52
  10.2 41.6 %all-to-all-start = ((bf16[8,1040,128]{2,1,0:T(8,128)(2,1)}), bf16[8,1040,128]{2,1,0:T(8,128)(2,1)S(1)}, u32[]{:S(2)}, u32[]{:S(2)}) async-start(bf16[8,1040,128]{2,1,0:T(8,128)(2,1)} %shard_map.120), calls=%async_computation | async-start | bytes 4259840 | tf_op jit(solution)/shard_map/all_to_all | solution.py:368
  17.5 11.4 %copy-start.1 = (bf16[8,256,128]{2,1,0:T(8,128)(2,1)S(1)}, bf16[8,256,128]{2,1,0:T(8,128)(2,1)}, u32[]{:S(2)}) copy-start(bf16[8,256,128]{2,1,0:T(8,128)(2,1)} %c_ref.3) | copy-start | bytes 1572868
  17.5 11.4 %copy-start.10 = (s32[4]{0:T(128)S(1)}, s32[4]{0:T(128)}, u32[]{:S(2)}) copy-start(s32[4]{0:T(128)} %pad_add_fusion.place_ref.group_ref) | copy-start | bytes 52
  17.5 11.4 %copy-start.13 = (f32[4]{0:T(128)S(1)}, f32[4]{0:T(128)}, u32[]{:S(2)}) copy-start(f32[4]{0:T(128)} %gain_ref.1) | copy-start | bytes 52
  19.8 24.9 %collective-permute-start = (bf16[256,1024]{1,0:T(8,128)(2,1)}, bf16[256,1024]{1,0:T(8,128)(2,1)}, u32[]{:S(2)}, u32[]{:S(2)}) collective-permute-start(bf16[256,1024]{1,0:T(8,128)(2,1)} %get-tuple-element.36), channel_id=1, source_target_pairs={{0,1},{1,0},{2,3},{3,2},{4,5},{5,4},{6,7},{7,6},{8,9},{9,8},{10,11... | collective-permute-start | bytes 1572872 | tf_op jit(solution)/shard_map/ppermute | solution.py:302
  23.6 28.2 %collective-permute-start.1 = (bf16[256,1024]{1,0:T(8,128)(2,1)}, bf16[256,1024]{1,0:T(8,128)(2,1)}, u32[]{:S(2)}, u32[]{:S(2)}) collective-permute-start(bf16[256,1024]{1,0:T(8,128)(2,1)} %get-tuple-element.35), channel_id=1, source_target_pairs={{0,2},{1,3},{2,0},{3,1},{4,6},{5,7},{6,4},{7,5},{8,10},{9,11},{10,... | collective-permute-start | bytes 1572872 | tf_op jit(solution)/shard_map/ppermute | solution.py:302
  30.6 0.7 copy-start.5
  31.4 0.7 copy-start.7
  32.1 26.4 %copy-start = (f32[4,136,128]{2,1,0:T(8,128)S(1)}, f32[4,136,128]{2,1,0:T(8,128)}, u32[]{:S(2)}) copy-start(f32[4,136,128]{2,1,0:T(8,128)} %all-gather) | copy-start | bytes 835588
  32.1 26.4 %copy-start.12 = (f32[256]{0:T(256)S(1)}, f32[256]{0:T(256)}, u32[]{:S(2)}) copy-start(f32[256]{0:T(256)} %param.17) | copy-start | bytes 3076
  51.8 6.7 %copy-start.2 = (bf16[8,256,128]{2,1,0:T(8,128)(2,1)S(1)}, bf16[8,256,128]{2,1,0:T(8,128)(2,1)}, u32[]{:S(2)}) copy-start(bf16[8,256,128]{2,1,0:T(8,128)(2,1)} %c_ref.3) | copy-start | bytes 1572868
  51.8 6.7 %copy-start.6 = (f32[2,256,128]{2,1,0:T(8,128)S(1)}, f32[2,256,128]{2,1,0:T(8,128)}, u32[]{:S(2)}) copy-start(f32[2,256,128]{2,1,0:T(8,128)} %copy-done.5) | copy-start | bytes 786436
  51.8 6.7 %copy-start.8 = (f32[2,256,128]{2,1,0:T(8,128)S(1)}, f32[2,256,128]{2,1,0:T(8,128)}, u32[]{:S(2)}) copy-start(f32[2,256,128]{2,1,0:T(8,128)} %copy-done.7) | copy-start | bytes 786436
  51.8 7.8 %collective-permute-start.2 = (bf16[8,1040,128]{2,1,0:T(8,128)(2,1)S(1)}, bf16[8,1040,128]{2,1,0:T(8,128)(2,1)S(1)}, u32[]{:S(2)}, u32[]{:S(2)}) collective-permute-start(bf16[8,1040,128]{2,1,0:T(8,128)(2,1)S(1)} %all-to-all-done.all_ref.a_ref), channel_id=1, source_target_pairs={{0,32},{32,0},{1,33},{33,1},{2,34},{34,2},{3,35},{35,3},{4,36},{36... | collective-permute-start | bytes 6389768 | tf_op jit(solution)/shard_map/ppermute | solution.py:298
  53.9 16.9 %collective-permute-start.3 = (bf16[256,1024]{1,0:T(8,128)(2,1)}, bf16[256,1024]{1,0:T(8,128)(2,1)}, u32[]{:S(2)}, u32[]{:S(2)}) collective-permute-start(bf16[256,1024]{1,0:T(8,128)(2,1)} %collective-permute-done.1.r2), channel_id=1, source_target_pairs={{0,1},{1,0},{2,3},{3,2},{4,5},{5,4},{6,7},{7,6},{8,9},{9,8},{10,11... | collective-permute-start | bytes 1572872 | tf_op jit(solution)/shard_map/ppermute | solution.py:302
  62.6 16.5 %all-to-all-start.1 = ((bf16[4,128,256]{2,1,0:T(8,128)(2,1)}), bf16[4,128,256]{2,1,0:T(8,128)(2,1)S(1)}, u32[]{:S(2)}, u32[]{:S(2)}) async-start(bf16[4,128,256]{2,1,0:T(8,128)(2,1)} %shard_map.124), calls=%async_computation.1 | async-start | bytes 524288 | tf_op jit(solution)/shard_map/all_to_all | solution.py:423
  70.8 6.3 %collective-permute-start.6 = (bf16[256,1024]{1,0:T(8,128)(2,1)}, bf16[256,1024]{1,0:T(8,128)(2,1)S(1)}, u32[]{:S(2)}, u32[]{:S(2)}) collective-permute-start(bf16[256,1024]{1,0:T(8,128)(2,1)} %collective-permute-done.3.r3), channel_id=1, source_target_pairs={{0,32},{32,0},{1,33},{33,1},{2,34},{34,2},{3,35},{35,3},{4,36},{36... | collective-permute-start | bytes 1572872 | tf_op jit(solution)/shard_map/ppermute | solution.py:298
  72.7 4.4 %collective-permute-start.4 = (bf16[256,1024]{1,0:T(8,128)(2,1)}, bf16[256,1024]{1,0:T(8,128)(2,1)S(1)}, u32[]{:S(2)}, u32[]{:S(2)}) collective-permute-start(bf16[256,1024]{1,0:T(8,128)(2,1)} %collective-permute-done.r1), channel_id=1, source_target_pairs={{0,32},{32,0},{1,33},{33,1},{2,34},{34,2},{3,35},{35,3},{4,36},{36... | collective-permute-start | bytes 1572872 | tf_op jit(solution)/shard_map/ppermute | solution.py:298
  75.1 4.0 %collective-permute-start.5 = (bf16[256,1024]{1,0:T(8,128)(2,1)}, bf16[256,1024]{1,0:T(8,128)(2,1)S(1)}, u32[]{:S(2)}, u32[]{:S(2)}) collective-permute-start(bf16[256,1024]{1,0:T(8,128)(2,1)} %collective-permute-done.1.r2), channel_id=1, source_target_pairs={{0,32},{32,0},{1,33},{33,1},{2,34},{34,2},{3,35},{35,3},{4,36},{36... | collective-permute-start | bytes 1572872 | tf_op jit(solution)/shard_map/ppermute | solution.py:298
  82.0 10.2 %collective-permute-start.7 = (bf16[64,2048]{1,0:T(8,128)(2,1)S(1)}, bf16[64,2048]{1,0:T(8,128)(2,1)S(1)}, u32[]{:S(2)}, u32[]{:S(2)}) collective-permute-start(bf16[64,2048]{1,0:T(8,128)(2,1)S(1)} %get-tuple-element.34), channel_id=1, source_target_pairs={{0,16},{16,0},{1,17},{17,1},{2,18},{18,2},{3,19},{19,3},{4,20},{20... | collective-permute-start | bytes 786440 | tf_op jit(solution)/shard_map/ppermute | solution.py:298

commit v3 on v2

--- a/solution.py
+++ b/solution.py
@@ -91,10 +91,22 @@
         copy.wait()
 
 
-def fill_kernel(place_ref, ck_ref, nk_ref, cv_ref, nv_ref, out_ref, held, sems):
+def spread_copies(held, out_ref, begin, sems):
+    rows = held.shape[0]
+    copies = [pltpu.make_async_copy(held, out_ref.at[k, begin : begin + rows], sems.at[k]) for k in range(CHIPS)]
+    for copy in copies:
+        copy.start()
+    return copies
+
+
+def fill_kernel(place_ref, ck_ref, nk_ref, cv_ref, nv_ref, w1_ref, w2_ref, out_ref, out1_ref, out2_ref, held, sems):
     for begin, ref in ((0, ck_ref), (CACHE, nk_ref), (SPAN, cv_ref), (SPAN + CACHE, nv_ref)):
         held[begin : begin + ref.shape[1], :] = ref[0]
-    spread_copies(held, out_ref, HEAD, sems)
+    copies = spread_copies(held, out_ref, HEAD, sems)
+    out1_ref[...] = w1_ref[...]
+    out2_ref[...] = w2_ref[...]
+    for copy in copies:
+        copy.wait()
 
 
 def pack_kernel(place_ref, both_ref, len_ref, filled_ref, out_ref, held, sems):
@@ -109,7 +121,8 @@
     for i, part in enumerate(thirds(first[HD : HD + 1] * second[HD : HD + 1])):
         tile = jnp.where(row == i + 1, part.astype(f32), tile)
     held[2 * HD : HEAD, :] = tile.astype(bf16)
-    spread_copies(held, out_ref, 0, sems)
+    for copy in spread_copies(held, out_ref, 0, sems):
+        copy.wait()
 
 
 def scan_kernel(place_ref, all_ref, out_ref):
@@ -123,12 +136,11 @@
     out_ref[...] = state
 
 
-def inside_kernel(group_ref, x_ref, decay_ref, b_ref, c_ref, gain_ref, y_ref, fade_ref):
+def inside_kernel(group_ref, x_ref, decay_ref, b_ref, c_ref, gain_ref, y_ref):
     decay = decay_ref[...]
     columns, rows = cum_columns(decay), cum_rows(decay)
     causal = tri(False)
     gram = dot(c_ref[0], b_ref[0], ((1,), (1,)))
-    fade = jnp.exp(-columns)
     for half in range(2):
         inputs = x_ref[:, half * HD : (half + 1) * HD]
         pieces = []
@@ -139,19 +151,19 @@
         low = low_lanes(TOKENS)
         skip = jnp.where(low_lanes(1), gain_ref[2 * half], gain_ref[2 * half + 1])
         y_ref[half] = jnp.where(low, pieces[0], pieces[1]) + skip * inputs.astype(f32)
-        fade_ref[half] = spread(fade, half, TOKENS)
-
-
-def query_kernel(place_ref, y_ref, fade_ref, c_ref, carried_ref, both_ref, gain_ref, out_ref):
+
+
+def query_kernel(place_ref, y_ref, decay_ref, c_ref, carried_ref, both_ref, gain_ref, out_ref):
     core = place_ref[1]
     readout = c_ref[0]
     low = low_lanes(TOKENS)
+    fade = jnp.exp(-cum_columns(decay_ref[...]))
     for half in range(2):
         carried = carried_ref[half]
         after = both_ref[0, half, HD : HD + 1] * carried + both_ref[0, half, 0:HD]
         carried = jnp.where(core == 1, after, carried)
         from_state = sum(dot(readout, part) for part in thirds(carried))
-        y = y_ref[half] + fade_ref[half] * from_state
+        y = y_ref[half] + spread(fade, half, TOKENS) * from_state
         square = y * y
         left = jnp.sum(jnp.where(low, square, 0.0), axis=1, keepdims=True)
         right = jnp.sum(jnp.where(low, 0.0, square), axis=1, keepdims=True)
@@ -277,7 +289,7 @@
 SMEM = pl.BlockSpec(memory_space=pltpu.SMEM)
 
 
-def call(kernel, scalars, args, in_specs, out_shape, out_specs, grid=(1,), scratch=(), room=40, aliases=None):
+def call(kernel, scalars, args, in_specs, out_shape, out_specs, grid=(1,), scratch=(), room=16, aliases=None):
     return pl.pallas_call(
         kernel,
         out_shape=out_shape,
@@ -323,13 +335,18 @@
     place = jnp.stack([lax.axis_index(CHIP), core, near, group]).astype(jnp.int32)
     of_group = lambda rows: pl.BlockSpec((1, rows, HD), lambda i, s: (s[3], 0, 0))
 
-    filled = call(
+    piece = whole((2 * HD, width))
+    filled, first, second = call(
         fill_kernel,
         place,
-        (cache_keys, new_keys, cache_values, new_values),
-        [of_group(CACHE), of_group(TOKENS), of_group(CACHE), of_group(TOKENS)],
-        shape(CHIPS, ROWS, HD, dtype=bf16),
-        pl.BlockSpec(memory_space=pl.ANY),
+        (cache_keys, new_keys, cache_values, new_values, out_weight, out_weight),
+        [of_group(CACHE), of_group(TOKENS), of_group(CACHE), of_group(TOKENS)]
+        + [
+            pl.BlockSpec((2 * HD, width), lambda i, s: (0, 2 * (s[2] // 2) + s[1])),
+            pl.BlockSpec((2 * HD, width), lambda i, s: (0, 2 * (1 - s[2] // 2) + s[1])),
+        ],
+        (shape(CHIPS, ROWS, HD, dtype=bf16),) + (shape(2 * HD, width, dtype=bf16),) * 2,
+        (pl.BlockSpec(memory_space=pl.ANY), piece, piece),
         scratch=[pltpu.VMEM((2 * SPAN, HD), bf16), pltpu.SemaphoreType.DMA((CHIPS,))],
         room=60,
     )
@@ -360,22 +377,22 @@
         aliases={3: 0},
     )
 
-    columns = lambda quarter: lax.dynamic_slice_in_dim(out_weight, quarter * width, width, 1)
-    second = flip(columns(2 * (1 - near // 2) + core), 2)
-    first = flip(columns(2 * (near // 2) + core), 1)
+    second = flip(second, 2)
     third = flip(second, 1)
-    own_columns = lax.dynamic_slice_in_dim(out_weight, 2 * (near // 2) * width, 2 * width, 1)
     same = lax.all_to_all(packed, CHIP, 0, 0, tiled=True)
-    inside, fade = call(
+    inside = call(
         inside_kernel,
         place,
         (ssm_inputs, step_decay, state_inputs, state_readout, skip_gain),
         [whole((TOKENS, 2 * HD)), whole((4, TOKENS)), of_group(TOKENS), of_group(TOKENS), SMEM],
-        (shape(2, TOKENS, HD), shape(2, TOKENS, HD)),
-        (whole((2, TOKENS, HD)), whole((2, TOKENS, HD))),
-    )
-    same, first, second, inside, fade, own_columns = lax.optimization_barrier(
-        (same, first, second, inside, fade, own_columns)
+        shape(2, TOKENS, HD),
+        whole((2, TOKENS, HD)),
+    )
+    first = flip(first, 1)
+    swapped = [swap(first, "c")]
+    own_columns = lax.dynamic_slice_in_dim(out_weight, 2 * (near // 2) * width, 2 * width, 1)
+    same, first, second, swapped, own_columns, inside = lax.optimization_barrier(
+        (same, first, second, swapped, own_columns, inside)
     )
     other = swap(same, "c")
     entering = call(
@@ -390,10 +407,10 @@
     queries = call(
         query_kernel,
         place,
-        (inside, fade, state_readout, carried, both, norm_gain.reshape(1, 2 * HD)),
+        (inside, step_decay, state_readout, carried, both, norm_gain.reshape(1, 2 * HD)),
         [
             whole((2, TOKENS, HD)),
-            whole((2, TOKENS, HD)),
+            whole((4, TOKENS)),
             of_group(TOKENS),
             whole((2, HD, HD)),
             whole((2, 2, HD + 8, HD)),
@@ -407,7 +424,7 @@
         attend_kernel,
         place,
         (queries, same, other),
-        [whole((2 * TOKENS, HD))] + [whole((CHIPS, ROWS, HD))] * 2,
+        [pl.BlockSpec(memory_space=pltpu.VMEM)] * 3,
         shape(4, TOKENS // 2, 2 * HD, dtype=bf16),
         whole((4, TOKENS // 2, 2 * HD)),
         scratch=[
@@ -416,10 +433,11 @@
             pltpu.VMEM((2 * TOKENS, HD), f32),
             pltpu.VMEM((2 * TOKENS, HD), f32),
         ],
-    )
-    attended, first, second = lax.optimization_barrier((attended, first, second))
+        room=24,
+    )
+    attended, second = lax.optimization_barrier((attended, second))
     received = (first, second, third)
-    swapped = [swap(part, "c") for part in received]
+    swapped = swapped + [swap(part, "c") for part in (second, third)]
     attended = lax.all_to_all(attended, NEAR, 0, 0, tiled=True)
     vmem = pl.BlockSpec(memory_space=pltpu.VMEM)
     keep, send = call(

time: 129 us -> 126 us (0.977)
  local copies, waits for them, and re-layouts: 5.09 us -> 1.47 us
  waiting for transfers between devices: 32.2 us -> 29.6 us
  starting transfers between devices: 33.2 us -> 35.6 us
  Pallas kernels: 16.8 us -> 18.6 us
    dynamic_slice x1 -> x0, local copies, waits for them, and re-layouts: 2.29 us -> none  [per_device(): lax.dynamic_slice_in_dim(out_weight, quarter * width, width, 1)]
    ppermute x3, waiting for transfers between devices: 22.5 us -> 20.5 us  [flip(): return lax.ppermute(array, NEAR, [(j, j ^ i) for j in range(4)])]
    pallas_call x8, Pallas kernels: 16.1 us -> 17.9 us  [call(): pl.pallas_call(kernel, out_shape=out_shape, grid_spec=pltpu.PrefetchScala...]
    unnamed x28 -> x24, local copies, waits for them, and re-layouts: 1.47 us -> 0.06 us
  transfers between devices with their start and end apart: 10 -> 10, of which waited for: 5 -> 6; matrix products, arithmetic and copies ran while one was open for 3% -> 1% of each run, Pallas kernels for 5% -> 5%
where the time goes in v3:
time: 126 us; the launch traced here: 125 us
  blocking collectives  38.2 us (30%)
  starting transfers between devices  35.6 us (28%)
  waiting for transfers between devices  29.6 us (23%)
  Pallas kernels  18.6 us (15%)
  local copies, waits for them, and re-layouts  1.47 us (1%)
    all_to_all x1, blocking collectives, per_device(): lax.all_to_all(partial.reshape(8, 8, 2 * width), OWNERS, 0, 0, tiled=True)  34.1 us
    ppermute x3, waiting for transfers between devices, flip(): return lax.ppermute(array, NEAR, [(j, j ^ i) for j in range(4)])  20.5 us
    pallas_call x8, Pallas kernels, call(): pl.pallas_call(kernel, out_shape=out_shape, grid_spec=pltpu.PrefetchScala...  17.9 us
    ppermute x5, starting transfers between devices, swap(): return lax.ppermute(array, axis, [(0, 1), (1, 0)])  12.2 us
    ppermute x3, starting transfers between devices, flip(): return lax.ppermute(array, NEAR, [(j, j ^ i) for j in range(4)])  11.4 us
    ppermute x5, waiting for transfers between devices, swap(): return lax.ppermute(array, axis, [(0, 1), (1, 0)])  8.54 us
    all_to_all x1, starting transfers between devices, per_device(): same = lax.all_to_all(packed, CHIP, 0, 0, tiled=True)  7.41 us
    all_to_all x1, starting transfers between devices, per_device(): attended = lax.all_to_all(attended, NEAR, 0, 0, tiled=True)  4.54 us
  transfers between devices with their start and end apart: 10, of which 6 were waited for; matrix products, arithmetic and copies ran while one was open for 1% of the time, Pallas kernels for 5%

profile of v3, /device:TPU:24, one launch (start us, length us, event | category | flops | bytes accessed | tf_op | source)
XLA Modules:
  0.0 125.0 jit_solution(16076214118774458366)
XLA Ops:
  0.0 0.6 pad_add_fusion.place_ref.group_ref
  0.6 0.0 copy-start.1
  0.6 0.0 copy-start.6
  0.6 0.0 copy-start.7
  0.6 0.0 copy-start.9
  0.6 4.4 %shard_map.118 = (bf16[8,1040,128]{2,1,0:T(8,128)(2,1)}, bf16[256,1024]{1,0:T(8,128)(2,1)}, bf16[256,1024]{1,0:T(8,128)(2,1)}) custom-call(s32[4]{0:T(128)} %pad_add_fusion.place_ref.group_ref, bf16[8,128,128]{2,1,0:T(8,128)(2,1)} %ck_ref.1, bf16[8,256,128]{2,1,0:T(8,128)(2,1)} %nk_ref.1, bf16[8,128,128]{2,1,0:T(8,128)(2,1)} %cv_ref.1, ...), custom_call_target="tpu_custom_call" | custom-call | bytes 4096 | tf_op jit(solution)/shard_map/pallas_call | solution.py:293
  5.0 0.0 copy-done.1
  5.0 0.0 copy-done.6
  5.0 0.0 copy-done.7
  5.0 0.0 copy-done.9
  5.0 1.2 shard_map.119
  6.3 2.1 %all-gather = f32[4,136,128]{2,1,0:T(8,128)} all-gather(f32[2,136,128]{2,1,0:T(8,128)S(1)} %shard_map.119), channel_id=2, replica_groups=mesh['x'=4,'yh'=2,'c'=2,'yl'=2,'za'=4,'z1'=2,'z0'=2] {'c'}, dimensions={0}, use_global_device_ids=true | all-gather | bytes 417792 | tf_op jit(solution)/shard_map/all_gather | solution.py:363
  9.1 2.5 %shard_map.120 = bf16[8,1040,128]{2,1,0:T(8,128)(2,1)} custom-call(s32[4]{0:T(128)} %pad_add_fusion.place_ref.group_ref, f32[2,2,136,128]{3,2,1,0:T(8,128)} %bitcast.8, s32[1]{0:T(128)S(6)} %copy.15.len_ref, bf16[8,1040,128]{2,1,0:T(8,128)(2,1)} %get-tuple-element.22.filled_ref), custom_call_target="tpu_custom_call", output_to_operand_aliasing={{}: (3, {})} | custom-call | bytes 4096 | tf_op jit(solution)/shard_map/pallas_call | solution.py:293
  11.6 0.0 copy-start.2
  11.6 0.0 copy-start.8
  11.6 0.0 copy-start.11
  11.6 7.4 %all-to-all-start = ((bf16[8,1040,128]{2,1,0:T(8,128)(2,1)}), bf16[8,1040,128]{2,1,0:T(8,128)(2,1)S(1)}, u32[]{:S(2)}, u32[]{:S(2)}) async-start(bf16[8,1040,128]{2,1,0:T(8,128)(2,1)} %shard_map.120), calls=%async_computation | async-start | bytes 4259840 | tf_op jit(solution)/shard_map/all_to_all | solution.py:382
  19.0 3.8 %collective-permute-start = (bf16[256,1024]{1,0:T(8,128)(2,1)}, bf16[256,1024]{1,0:T(8,128)(2,1)}, u32[]{:S(2)}, u32[]{:S(2)}) collective-permute-start(bf16[256,1024]{1,0:T(8,128)(2,1)} %get-tuple-element.23), channel_id=1, source_target_pairs={{0,1},{1,0},{2,3},{3,2},{4,5},{5,4},{6,7},{7,6},{8,9},{9,8},{10,11... | collective-permute-start | bytes 1572872 | tf_op jit(solution)/shard_map/ppermute | solution.py:314
  22.9 5.2 %collective-permute-start.1 = (bf16[256,1024]{1,0:T(8,128)(2,1)}, bf16[256,1024]{1,0:T(8,128)(2,1)}, u32[]{:S(2)}, u32[]{:S(2)}) collective-permute-start(bf16[256,1024]{1,0:T(8,128)(2,1)} %get-tuple-element.24), channel_id=1, source_target_pairs={{0,2},{1,3},{2,0},{3,1},{4,6},{5,7},{6,4},{7,5},{8,10},{9,11},{10,... | collective-permute-start | bytes 1572872 | tf_op jit(solution)/shard_map/ppermute | solution.py:314
  28.1 15.9 %collective-permute-done.r1 = bf16[256,1024]{1,0:T(8,128)(2,1)} collective-permute-done((bf16[256,1024]{1,0:T(8,128)(2,1)}, bf16[256,1024]{1,0:T(8,128)(2,1)}, u32[]{:S(2)}, u32[]{:S(2)}) %collective-permute-start) | collective-permute-done | bytes 524320 | tf_op jit(solution)/shard_map/ppermute | solution.py:314
  43.9 1.9 %collective-permute-start.2 = (bf16[256,1024]{1,0:T(8,128)(2,1)}, bf16[256,1024]{1,0:T(8,128)(2,1)}, u32[]{:S(2)}, u32[]{:S(2)}) collective-permute-start(bf16[256,1024]{1,0:T(8,128)(2,1)} %collective-permute-done.r1), channel_id=1, source_target_pairs={{0,32},{32,0},{1,33},{33,1},{2,34},{34,2},{3,35},{35,3},{4,36},{36... | collective-permute-start | bytes 1572872 | tf_op jit(solution)/shard_map/ppermute | solution.py:310
  45.9 0.0 copy-done.2
  45.9 0.0 copy-done.8
  45.9 0.0 copy-done.11
  45.9 1.8 %shard_map.121.y_ref = f32[2,256,128]{2,1,0:T(8,128)S(1)} custom-call(s32[4]{0:T(128)S(1)} %copy-done.8, bf16[256,256]{1,0:T(8,128)(2,1)S(1)} %copy-done.6, f32[4,256]{1,0:T(4,128)S(1)} %copy-done.9, bf16[8,256,128]{2,1,0:T(8,128)(2,1)S(1)} %copy-done.1, bf16[8,256,128]{2,1,0:T(8,128)(2,1)S(1)} %copy-done.2, f32[4]{0:T(128)S(1)} %copy-done.11), custom_call_target="tpu_custom_call" | custom-call | bytes 4096 | tf_op jit(solution)/shard_map/pallas_call | solution.py:293
  47.7 0.0 copy-start.4
  47.7 0.0 copy-start
  47.7 0.0 copy-start.10
  47.7 1.4 %constant_dynamic-slice_fusion.own_ref = bf16[256,2048]{1,0:T(8,128)(2,1)S(1)} fusion(bf16[256,4096]{1,0:T(8,128)(2,1)} %w2_ref.1, s32[]{:T(128)S(6)} %select_n.9), kind=kLoop, calls=%fused_computation.1 | loop fusion | bytes 2097156 | tf_op jit(solution)/shard_map/dynamic_slice | solution.py:393
  49.1 1.9 %collective-permute-done.1.r2 = bf16[256,1024]{1,0:T(8,128)(2,1)} collective-permute-done((bf16[256,1024]{1,0:T(8,128)(2,1)}, bf16[256,1024]{1,0:T(8,128)(2,1)}, u32[]{:S(2)}, u32[]{:S(2)}) %collective-permute-start.1) | collective-permute-done | bytes 524320 | tf_op jit(solution)/shard_map/ppermute | solution.py:314
  51.0 0.0 copy-done.4
  51.0 0.0 collective-permute-done.2.s1
  51.0 0.0 all-to-all-done.all_ref.a_ref
  51.0 0.0 copy-start.3
  51.1 0.0 copy-start.5
  51.1 2.1 %collective-permute-start.3 = (bf16[8,1040,128]{2,1,0:T(8,128)(2,1)S(1)}, bf16[8,1040,128]{2,1,0:T(8,128)(2,1)S(1)}, u32[]{:S(2)}, u32[]{:S(2)}) collective-permute-start(bf16[8,1040,128]{2,1,0:T(8,128)(2,1)S(1)} %all-to-all-done.all_ref.a_ref), channel_id=1, source_target_pairs={{0,32},{32,0},{1,33},{33,1},{2,34},{34,2},{3,35},{35,3},{4,36},{36... | collective-permute-start | bytes 6389768 | tf_op jit(solution)/shard_map/ppermute | solution.py:310
  53.1 2.5 %collective-permute-start.4 = (bf16[256,1024]{1,0:T(8,128)(2,1)}, bf16[256,1024]{1,0:T(8,128)(2,1)}, u32[]{:S(2)}, u32[]{:S(2)}) collective-permute-start(bf16[256,1024]{1,0:T(8,128)(2,1)} %collective-permute-done.1.r2), channel_id=1, source_target_pairs={{0,1},{1,0},{2,3},{3,2},{4,5},{5,4},{6,7},{7,6},{8,9},{9,8},{10,11... | collective-permute-start | bytes 1572872 | tf_op jit(solution)/shard_map/ppermute | solution.py:314
  55.6 0.7 shard_map.122
  56.3 1.9 %all-gather.1 = f32[256,128]{1,0:T(8,128)S(1)} all-gather(f32[128,128]{1,0:T(8,128)S(1)} %shard_map.122), channel_id=3, replica_groups=mesh['x'=4,'yh'=2,'c'=2,'yl'=2,'za'=4,'z1'=2,'z0'=2] {'c'}, dimensions={0}, use_global_device_ids=true | all-gather | bytes 196608 | tf_op jit(solution)/shard_map/all_gather | solution.py:406
  58.2 0.0 copy-done
  58.2 0.0 copy-done.10
  58.2 0.0 copy-done.3
  58.2 0.0 copy-done.5
  58.2 1.2 shard_map.123.q_ref
  59.4 0.0 collective-permute-done.3.b_ref
  59.4 3.0 %shard_map.124 = bf16[4,128,256]{2,1,0:T(8,128)(2,1)} custom-call(s32[4]{0:T(128)S(1)} %copy-done.8, bf16[512,128]{1,0:T(8,128)(2,1)S(1)} %shard_map.123.q_ref, bf16[8,1040,128]{2,1,0:T(8,128)(2,1)S(1)} %all-to-all-done.all_ref.a_ref, bf16[8,1040,128]{2,1,0:T(8,128)(2,1)S(1)} %collective-permute-done.3.b_ref), custom_call_target="tpu_custom_call" | custom-call | bytes 4096 | tf_op jit(solution)/shard_map/pallas_call | solution.py:293
  62.5 4.5 %all-to-all-start.1 = ((bf16[4,128,256]{2,1,0:T(8,128)(2,1)}), bf16[4,128,256]{2,1,0:T(8,128)(2,1)S(1)}, u32[]{:S(2)}, u32[]{:S(2)}) async-start(bf16[4,128,256]{2,1,0:T(8,128)(2,1)} %shard_map.124), calls=%async_computation.1 | async-start | bytes 524288 | tf_op jit(solution)/shard_map/all_to_all | solution.py:441
  67.0 2.7 %collective-permute-done.4.r3 = bf16[256,1024]{1,0:T(8,128)(2,1)} collective-permute-done((bf16[256,1024]{1,0:T(8,128)(2,1)}, bf16[256,1024]{1,0:T(8,128)(2,1)}, u32[]{:S(2)}, u32[]{:S(2)}) %collective-permute-start.4) | collective-permute-done | bytes 524320 | tf_op jit(solution)/shard_map/ppermute | solution.py:314
  69.7 1.9 %collective-permute-start.6 = (bf16[256,1024]{1,0:T(8,128)(2,1)}, bf16[256,1024]{1,0:T(8,128)(2,1)S(1)}, u32[]{:S(2)}, u32[]{:S(2)}) collective-permute-start(bf16[256,1024]{1,0:T(8,128)(2,1)} %collective-permute-done.4.r3), channel_id=1, source_target_pairs={{0,32},{32,0},{1,33},{33,1},{2,34},{34,2},{3,35},{35,3},{4,36},{36... | collective-permute-start | bytes 1572872 | tf_op jit(solution)/shard_map/ppermute | solution.py:310
  71.6 2.4 %collective-permute-start.5 = (bf16[256,1024]{1,0:T(8,128)(2,1)}, bf16[256,1024]{1,0:T(8,128)(2,1)S(1)}, u32[]{:S(2)}, u32[]{:S(2)}) collective-permute-start(bf16[256,1024]{1,0:T(8,128)(2,1)} %collective-permute-done.1.r2), channel_id=1, source_target_pairs={{0,32},{32,0},{1,33},{33,1},{2,34},{34,2},{3,35},{35,3},{4,36},{36... | collective-permute-start | bytes 1572872 | tf_op jit(solution)/shard_map/ppermute | solution.py:310
  74.0 0.0 collective-permute-done.6.s3
  74.0 1.7 %collective-permute-done.5.s2 = bf16[256,1024]{1,0:T(8,128)(2,1)S(1)} collective-permute-done((bf16[256,1024]{1,0:T(8,128)(2,1)}, bf16[256,1024]{1,0:T(8,128)(2,1)S(1)}, u32[]{:S(2)}, u32[]{:S(2)}) %collective-permute-start.5) | collective-permute-done | bytes 524320 | tf_op jit(solution)/shard_map/ppermute | solution.py:310
  75.7 0.6 all-to-all-done.1.att_ref
  76.3 3.1 %shard_map.125 = (bf16[64,2048]{1,0:T(8,128)(2,1)S(1)}, bf16[64,2048]{1,0:T(8,128)(2,1)S(1)}) custom-call(s32[4]{0:T(128)S(1)} %copy-done.8, bf16[4,128,256]{2,1,0:T(8,128)(2,1)S(1)} %all-to-all-done.1.att_ref, bf16[256,2048]{1,0:T(8,128)(2,1)S(1)} %constant_dynamic-slice_fusion.own_ref, bf16[256,1024]{1,0:T(8,128)(2,1)} %collective-permute-done.r1, ...), custom_call_target="tpu_custom_call" | custom-call | bytes 4096 | tf_op jit(solution)/shard_map/pallas_call | solution.py:293
  79.4 3.9 %collective-permute-start.7 = (bf16[64,2048]{1,0:T(8,128)(2,1)S(1)}, bf16[64,2048]{1,0:T(8,128)(2,1)S(1)}, u32[]{:S(2)}, u32[]{:S(2)}) collective-permute-start(bf16[64,2048]{1,0:T(8,128)(2,1)S(1)} %get-tuple-element.34), channel_id=1, source_target_pairs={{0,16},{16,0},{1,17},{17,1},{2,18},{18,2},{3,19},{19,3},{4,20},{20... | collective-permute-start | bytes 786440 | tf_op jit(solution)/shard_map/ppermute | solution.py:310
  83.3 6.8 %collective-permute-done.7.second_ref = bf16[64,2048]{1,0:T(8,128)(2,1)S(1)} collective-permute-done((bf16[64,2048]{1,0:T(8,128)(2,1)S(1)}, bf16[64,2048]{1,0:T(8,128)(2,1)S(1)}, u32[]{:S(2)}, u32[]{:S(2)}) %collective-permute-start.7) | collective-permute-done | bytes 262176 | tf_op jit(solution)/shard_map/ppermute | solution.py:310
  90.1 0.1 shard_map.126
  90.2 34.1 %all_to_all.15.parts_ref = bf16[8,8,2048]{2,1,0:T(8,128)(2,1)S(1)} all-to-all(bf16[8,8,2048]{2,1,0:T(8,128)(2,1)S(1)} %bitcast.10), channel_id=1, replica_groups=mesh['x'=4,'yh'=2,'c'=2,'yl'=2,'za'=4,'z1'=2,'z0'=2] {'za','z1'}, dimensions={0} | all-to-all | bytes 524288 | tf_op jit(solution)/shard_map/all_to_all | solution.py:453
  124.3 0.7 shard_map.127
Async XLA Ops:
  0.6 4.4 %copy-start.1 = (bf16[8,256,128]{2,1,0:T(8,128)(2,1)S(1)}, bf16[8,256,128]{2,1,0:T(8,128)(2,1)}, u32[]{:S(2)}) copy-start(bf16[8,256,128]{2,1,0:T(8,128)(2,1)} %b_ref.3) | copy-start | bytes 1572868
  0.6 4.4 %copy-start.6 = (bf16[256,256]{1,0:T(8,128)(2,1)S(1)}, bf16[256,256]{1,0:T(8,128)(2,1)}, u32[]{:S(2)}) copy-start(bf16[256,256]{1,0:T(8,128)(2,1)} %x_ref.3) | copy-start | bytes 393220
  0.6 4.4 %copy-start.7 = (s32[4]{0:T(128)S(1)}, s32[4]{0:T(128)}, u32[]{:S(2)}) copy-start(s32[4]{0:T(128)} %pad_add_fusion.place_ref.group_ref) | copy-start | bytes 52
  0.6 4.4 %copy-start.9 = (f32[4,256]{1,0:T(4,128)S(1)}, f32[4,256]{1,0:T(4,128)}, u32[]{:S(2)}) copy-start(f32[4,256]{1,0:T(4,128)} %decay_ref.5) | copy-start | bytes 12292
  11.6 34.3 %copy-start.2 = (bf16[8,256,128]{2,1,0:T(8,128)(2,1)S(1)}, bf16[8,256,128]{2,1,0:T(8,128)(2,1)}, u32[]{:S(2)}) copy-start(bf16[8,256,128]{2,1,0:T(8,128)(2,1)} %c_ref.3) | copy-start | bytes 1572868
  11.6 34.3 %copy-start.8 = (s32[4]{0:T(128)S(1)}, s32[4]{0:T(128)}, u32[]{:S(2)}) copy-start(s32[4]{0:T(128)} %pad_add_fusion.place_ref.group_ref) | copy-start | bytes 52
  11.6 34.3 %copy-start.11 = (f32[4]{0:T(128)S(1)}, f32[4]{0:T(128)}, u32[]{:S(2)}) copy-start(f32[4]{0:T(128)} %gain_ref.1) | copy-start | bytes 52
  11.6 39.4 %all-to-all-start = ((bf16[8,1040,128]{2,1,0:T(8,128)(2,1)}), bf16[8,1040,128]{2,1,0:T(8,128)(2,1)S(1)}, u32[]{:S(2)}, u32[]{:S(2)}) async-start(bf16[8,1040,128]{2,1,0:T(8,128)(2,1)} %shard_map.120), calls=%async_computation | async-start | bytes 4259840 | tf_op jit(solution)/shard_map/all_to_all | solution.py:382
  19.0 24.9 %collective-permute-start = (bf16[256,1024]{1,0:T(8,128)(2,1)}, bf16[256,1024]{1,0:T(8,128)(2,1)}, u32[]{:S(2)}, u32[]{:S(2)}) collective-permute-start(bf16[256,1024]{1,0:T(8,128)(2,1)} %get-tuple-element.23), channel_id=1, source_target_pairs={{0,1},{1,0},{2,3},{3,2},{4,5},{5,4},{6,7},{7,6},{8,9},{9,8},{10,11... | collective-permute-start | bytes 1572872 | tf_op jit(solution)/shard_map/ppermute | solution.py:314
  22.9 28.2 %collective-permute-start.1 = (bf16[256,1024]{1,0:T(8,128)(2,1)}, bf16[256,1024]{1,0:T(8,128)(2,1)}, u32[]{:S(2)}, u32[]{:S(2)}) collective-permute-start(bf16[256,1024]{1,0:T(8,128)(2,1)} %get-tuple-element.24), channel_id=1, source_target_pairs={{0,2},{1,3},{2,0},{3,1},{4,6},{5,7},{6,4},{7,5},{8,10},{9,11},{10,... | collective-permute-start | bytes 1572872 | tf_op jit(solution)/shard_map/ppermute | solution.py:314
  43.9 7.1 %collective-permute-start.2 = (bf16[256,1024]{1,0:T(8,128)(2,1)}, bf16[256,1024]{1,0:T(8,128)(2,1)}, u32[]{:S(2)}, u32[]{:S(2)}) collective-permute-start(bf16[256,1024]{1,0:T(8,128)(2,1)} %collective-permute-done.r1), channel_id=1, source_target_pairs={{0,32},{32,0},{1,33},{33,1},{2,34},{34,2},{3,35},{35,3},{4,36},{36... | collective-permute-start | bytes 1572872 | tf_op jit(solution)/shard_map/ppermute | solution.py:310
  47.7 3.4 %copy-start.4 = (f32[2,256,128]{2,1,0:T(8,128)}, f32[2,256,128]{2,1,0:T(8,128)S(1)}, u32[]{:S(2)}) copy-start(f32[2,256,128]{2,1,0:T(8,128)S(1)} %shard_map.121.y_ref) | copy-start | bytes 786436
  47.7 10.5 %copy-start = (f32[4,136,128]{2,1,0:T(8,128)S(1)}, f32[4,136,128]{2,1,0:T(8,128)}, u32[]{:S(2)}) copy-start(f32[4,136,128]{2,1,0:T(8,128)} %all-gather) | copy-start | bytes 835588
  47.7 10.5 %copy-start.10 = (f32[256]{0:T(256)S(1)}, f32[256]{0:T(256)}, u32[]{:S(2)}) copy-start(f32[256]{0:T(256)} %param.17) | copy-start | bytes 3076
  51.0 7.1 %copy-start.3 = (bf16[8,256,128]{2,1,0:T(8,128)(2,1)S(1)}, bf16[8,256,128]{2,1,0:T(8,128)(2,1)}, u32[]{:S(2)}) copy-start(bf16[8,256,128]{2,1,0:T(8,128)(2,1)} %c_ref.3) | copy-start | bytes 1572868
  51.1 7.1 %copy-start.5 = (f32[2,256,128]{2,1,0:T(8,128)S(1)}, f32[2,256,128]{2,1,0:T(8,128)}, u32[]{:S(2)}) copy-start(f32[2,256,128]{2,1,0:T(8,128)} %copy-done.4) | copy-start | bytes 786436
  51.1 8.4 %collective-permute-start.3 = (bf16[8,1040,128]{2,1,0:T(8,128)(2,1)S(1)}, bf16[8,1040,128]{2,1,0:T(8,128)(2,1)S(1)}, u32[]{:S(2)}, u32[]{:S(2)}) collective-permute-start(bf16[8,1040,128]{2,1,0:T(8,128)(2,1)S(1)} %all-to-all-done.all_ref.a_ref), channel_id=1, source_target_pairs={{0,32},{32,0},{1,33},{33,1},{2,34},{34,2},{3,35},{35,3},{4,36},{36... | collective-permute-start | bytes 6389768 | tf_op jit(solution)/shard_map/ppermute | solution.py:310
  53.1 16.5 %collective-permute-start.4 = (bf16[256,1024]{1,0:T(8,128)(2,1)}, bf16[256,1024]{1,0:T(8,128)(2,1)}, u32[]{:S(2)}, u32[]{:S(2)}) collective-permute-start(bf16[256,1024]{1,0:T(8,128)(2,1)} %collective-permute-done.1.r2), channel_id=1, source_target_pairs={{0,1},{1,0},{2,3},{3,2},{4,5},{5,4},{6,7},{7,6},{8,9},{9,8},{10,11... | collective-permute-start | bytes 1572872 | tf_op jit(solution)/shard_map/ppermute | solution.py:314
  62.5 13.8 %all-to-all-start.1 = ((bf16[4,128,256]{2,1,0:T(8,128)(2,1)}), bf16[4,128,256]{2,1,0:T(8,128)(2,1)S(1)}, u32[]{:S(2)}, u32[]{:S(2)}) async-start(bf16[4,128,256]{2,1,0:T(8,128)(2,1)} %shard_map.124), calls=%async_computation.1 | async-start | bytes 524288 | tf_op jit(solution)/shard_map/all_to_all | solution.py:441
  69.7 4.3 %collective-permute-start.6 = (bf16[256,1024]{1,0:T(8,128)(2,1)}, bf16[256,1024]{1,0:T(8,128)(2,1)S(1)}, u32[]{:S(2)}, u32[]{:S(2)}) collective-permute-start(bf16[256,1024]{1,0:T(8,128)(2,1)} %collective-permute-done.4.r3), channel_id=1, source_target_pairs={{0,32},{32,0},{1,33},{33,1},{2,34},{34,2},{3,35},{35,3},{4,36},{36... | collective-permute-start | bytes 1572872 | tf_op jit(solution)/shard_map/ppermute | solution.py:310
  71.6 4.1 %collective-permute-start.5 = (bf16[256,1024]{1,0:T(8,128)(2,1)}, bf16[256,1024]{1,0:T(8,128)(2,1)S(1)}, u32[]{:S(2)}, u32[]{:S(2)}) collective-permute-start(bf16[256,1024]{1,0:T(8,128)(2,1)} %collective-permute-done.1.r2), channel_id=1, source_target_pairs={{0,32},{32,0},{1,33},{33,1},{2,34},{34,2},{3,35},{35,3},{4,36},{36... | collective-permute-start | bytes 1572872 | tf_op jit(solution)/shard_map/ppermute | solution.py:310
  79.4 10.8 %collective-permute-start.7 = (bf16[64,2048]{1,0:T(8,128)(2,1)S(1)}, bf16[64,2048]{1,0:T(8,128)(2,1)S(1)}, u32[]{:S(2)}, u32[]{:S(2)}) collective-permute-start(bf16[64,2048]{1,0:T(8,128)(2,1)S(1)} %get-tuple-element.34), channel_id=1, source_target_pairs={{0,16},{16,0},{1,17},{17,1},{2,18},{18,2},{3,19},{19,3},{4,20},{20... | collective-permute-start | bytes 786440 | tf_op jit(solution)/shard_map/ppermute | solution.py:310

commit v4 on v3

--- a/solution.py
+++ b/solution.py
@@ -15,7 +15,8 @@
 HD = 128
 TOKENS = 256
 SPAN = CACHE + TOKENS
-HEAD = 2 * HD + 16
+TILE = 2 * HD + 16
+HEAD = TILE + 16
 ROWS = HEAD + 2 * SPAN
 CHIPS = 8
 HIDDEN = -1e30
@@ -70,15 +71,22 @@
     return jnp.where(low_lanes(rows), left, right)
 
 
-def state_kernel(group_ref, x_ref, decay_ref, b_ref, out_ref):
+def own_group():
+    return lax.axis_index(("yl", "za"))
+
+
+def state_kernel(x_ref, decay_ref, b_hbm, out_ref, b_ref, sem):
+    copy = pltpu.make_async_copy(b_hbm.at[own_group()], b_ref, sem)
+    copy.start()
     cum = cum_columns(decay_ref[...])
     last = cum[TOKENS - 1 :, :]
     tail = jnp.exp(last - cum)
     total = jnp.exp(-last)
+    copy.wait()
     for half in range(2):
         inputs = x_ref[:, half * HD : (half + 1) * HD].astype(f32)
         weighted = (spread(tail, half, TOKENS) * inputs).astype(bf16)
-        out_ref[half, 0:HD, :] = dot(b_ref[0], weighted, ((0,), (0,)))
+        out_ref[half, 0:HD, :] = dot(b_ref[...], weighted, ((0,), (0,)))
         out_ref[half, HD : HD + 8, :] = spread(jnp.broadcast_to(total, (8, 4)), half, 8)
 
 
@@ -99,28 +107,48 @@
     return copies
 
 
-def fill_kernel(place_ref, ck_ref, nk_ref, cv_ref, nv_ref, w1_ref, w2_ref, out_ref, out1_ref, out2_ref, held, sems):
-    for begin, ref in ((0, ck_ref), (CACHE, nk_ref), (SPAN, cv_ref), (SPAN + CACHE, nv_ref)):
-        held[begin : begin + ref.shape[1], :] = ref[0]
-    copies = spread_copies(held, out_ref, HEAD, sems)
-    out1_ref[...] = w1_ref[...]
-    out2_ref[...] = w2_ref[...]
+def fill_kernel(ck_ref, nk_ref, cv_ref, nv_ref, w_ref, len_hbm, out_ref, *refs):
+    w_outs, (held, w_held, len_ref, in_sems, w_sems, sems) = refs[:2], refs[2:]
+    core, side, group = lax.axis_index("c"), lax.axis_index("z1"), own_group()
+    width = w_held.shape[2]
+    loads, begin = [], HEAD - TILE
+    for i, ref in enumerate((ck_ref, nk_ref, cv_ref, nv_ref)):
+        rows = ref.shape[1]
+        loads.append(pltpu.make_async_copy(ref.at[group], held.at[begin : begin + rows], in_sems.at[i]))
+        begin = begin + rows
+    pieces = []
+    for i, half in enumerate((side, 1 - side)):
+        columns = pl.ds(pl.multiple_of((2 * half + core) * width, width), width)
+        pieces.append(pltpu.make_async_copy(w_ref.at[:, columns], w_held.at[i], in_sems.at[4 + i]))
+    loads.append(pltpu.make_async_copy(len_hbm, len_ref, in_sems.at[6]))
+    for copy in loads + pieces:
+        copy.start()
+    loads.pop().wait()
+    slots = lax.broadcasted_iota(jnp.int32, (HEAD - TILE, HD), 1)
+    held[0 : HEAD - TILE, :] = jnp.where(slots < len_ref[0], 0.0, HIDDEN).astype(bf16)
+    for copy in loads:
+        copy.wait()
+    copies = spread_copies(held, out_ref, TILE, sems)
+    for i, copy in enumerate(pieces):
+        copy.wait()
+        copies.append(pltpu.make_async_copy(w_held.at[i], w_outs[i], w_sems.at[i]))
+        copies[-1].start()
     for copy in copies:
         copy.wait()
 
 
-def pack_kernel(place_ref, both_ref, len_ref, filled_ref, out_ref, held, sems):
-    first, second = both_ref[0, 0], both_ref[1, 0]
+def pack_kernel(both_ref, filled_ref, out_ref, held, sems):
+    core = lax.axis_index("c")
+    first, second = both_ref[0, core], both_ref[1, core]
     state = first[0:HD] * second[HD : HD + 1] + second[0:HD]
     high = state.astype(bf16)
     held[0:HD, :] = high
     held[HD : 2 * HD, :] = (state - high.astype(f32)).astype(bf16)
-    slots = lax.broadcasted_iota(jnp.int32, (16, HD), 1)
-    row = lax.broadcasted_iota(jnp.int32, (16, HD), 0)
-    tile = jnp.where(slots < len_ref[0], 0.0, HIDDEN)
+    row = lax.broadcasted_iota(jnp.int32, (TILE - 2 * HD, HD), 0)
+    tile = jnp.zeros((TILE - 2 * HD, HD), f32)
     for i, part in enumerate(thirds(first[HD : HD + 1] * second[HD : HD + 1])):
-        tile = jnp.where(row == i + 1, part.astype(f32), tile)
-    held[2 * HD : HEAD, :] = tile.astype(bf16)
+        tile = jnp.where(row == i, part.astype(f32), tile)
+    held[2 * HD : TILE, :] = tile.astype(bf16)
     for copy in spread_copies(held, out_ref, 0, sems):
         copy.wait()
 
@@ -129,8 +157,8 @@
     chip = place_ref[0]
     state = jnp.zeros((HD, HD), f32)
     for k in range(CHIPS - 1):
-        tile = all_ref[k, 2 * HD : HEAD, :].astype(f32)
-        decay = tile[1:2] + tile[2:3] + tile[3:4]
+        tile = all_ref[k, 2 * HD : TILE, :].astype(f32)
+        decay = tile[0:1] + tile[1:2] + tile[2:3]
         here = all_ref[k, 0:HD, :].astype(f32) + all_ref[k, HD : 2 * HD, :].astype(f32)
         state = jnp.where(k < chip, decay * state + here, state)
     out_ref[...] = state
@@ -179,8 +207,8 @@
     top_ref[...] = jnp.full((count, HD), -jnp.inf, f32)
 
     def score(k, side, extra, causal):
-        bias = sides[side][k, 2 * HD : HEAD, :].astype(f32)[0:1]
-        raw = dot(q_ref[...], sides[side][k, HEAD : HEAD + SPAN, :], ((1,), (1,)))
+        bias = sides[side][k, TILE:HEAD, :].astype(f32)[0:1]
+        raw = dot(q_ref[...], sides[side][k, HEAD : HEAD + SPAN, :], ((1,), (1,))) * SCALE
         top = top_ref[...]
         for tile in range(SPAN // HD):
             part = raw[:, tile * HD : (tile + 1) * HD]
@@ -205,7 +233,7 @@
     score(chip, 0, None, True)
     score(chip, 1, jnp.where(core == 1, 0.0, HIDDEN), False)
 
-    top = jnp.max(top_ref[...], axis=1, keepdims=True) * SCALE
+    top = jnp.max(top_ref[...], axis=1, keepdims=True)
     top_ref[...] = jnp.broadcast_to(top, (count, HD))
     sum_ref[...] = jnp.zeros((count, HD), f32)
     acc_ref[...] = jnp.zeros((count, HD), f32)
@@ -218,7 +246,7 @@
             probs = []
             for tile in range(SPAN // HD):
                 part = scores_ref[k, :, side * SPAN + tile * HD : side * SPAN + (tile + 1) * HD]
-                expo = jnp.exp2(part * SCALE - top)
+                expo = jnp.exp2(part - top)
                 total = total + expo
                 probs.append(expo.astype(bf16))
             acc = acc + dot(jnp.concatenate(probs, axis=1), sides[side][k, HEAD + SPAN :, :])
@@ -300,6 +328,19 @@
         compiler_params=pltpu.CompilerParams(vmem_limit_bytes=room * 1024 * 1024),
         cost_estimate=pl.CostEstimate(flops=0, bytes_accessed=1 << 12, transcendentals=0),
     )(scalars, *args)
+
+
+def plain(kernel, args, in_specs, out_shape, out_specs, scratch, aliases=None):
+    return pl.pallas_call(
+        kernel,
+        out_shape=out_shape,
+        in_specs=in_specs,
+        out_specs=out_specs,
+        scratch_shapes=scratch,
+        input_output_aliases=aliases or {},
+        compiler_params=pltpu.CompilerParams(vmem_limit_bytes=60 * 1024 * 1024),
+        cost_estimate=pl.CostEstimate(flops=0, bytes_accessed=1 << 12, transcendentals=0),
+    )(*args)
 
 
 def shape(*dims, dtype=f32):
@@ -332,51 +373,47 @@
     core = lax.axis_index("c")
     near = lax.axis_index(NEAR)
     group = lax.axis_index(("yl", "za")).astype(jnp.int32)
+    of_group = lambda rows: pl.BlockSpec((1, rows, HD), lambda i, s: (s[3], 0, 0))
+
+    hbm = pl.BlockSpec(memory_space=pltpu.HBM)
+    vmem = pl.BlockSpec(memory_space=pltpu.VMEM)
+    filled, first, second = plain(
+        fill_kernel,
+        (cache_keys, new_keys, cache_values, new_values, out_weight, cache_len),
+        [hbm] * 6,
+        (shape(CHIPS, ROWS, HD, dtype=bf16),) + (shape(2 * HD, width, dtype=bf16),) * 2,
+        (hbm,) * 3,
+        [
+            pltpu.VMEM((ROWS - TILE, HD), bf16),
+            pltpu.VMEM((2, 2 * HD, width), bf16),
+            pltpu.SMEM((1,), jnp.int32),
+            pltpu.SemaphoreType.DMA((7,)),
+            pltpu.SemaphoreType.DMA((2,)),
+            pltpu.SemaphoreType.DMA((CHIPS,)),
+        ],
+    )
+    step_decay, filled = lax.optimization_barrier((step_decay, filled))
+
+    own = pl.pallas_call(
+        state_kernel,
+        out_shape=shape(2, HD + 8, HD),
+        in_specs=[vmem, vmem, hbm],
+        out_specs=vmem,
+        scratch_shapes=[pltpu.VMEM((TOKENS, HD), bf16), pltpu.SemaphoreType.DMA],
+        compiler_params=pltpu.CompilerParams(vmem_limit_bytes=16 * 1024 * 1024),
+        cost_estimate=pl.CostEstimate(flops=0, bytes_accessed=1 << 12, transcendentals=0),
+    )(ssm_inputs, step_decay, state_inputs)
+    both = lax.all_gather(own, "c")
+    packed = plain(
+        pack_kernel,
+        (both, filled),
+        [vmem, hbm],
+        shape(CHIPS, ROWS, HD, dtype=bf16),
+        hbm,
+        [pltpu.VMEM((TILE, HD), bf16), pltpu.SemaphoreType.DMA((CHIPS,))],
+        {1: 0},
+    )
     place = jnp.stack([lax.axis_index(CHIP), core, near, group]).astype(jnp.int32)
-    of_group = lambda rows: pl.BlockSpec((1, rows, HD), lambda i, s: (s[3], 0, 0))
-
-    piece = whole((2 * HD, width))
-    filled, first, second = call(
-        fill_kernel,
-        place,
-        (cache_keys, new_keys, cache_values, new_values, out_weight, out_weight),
-        [of_group(CACHE), of_group(TOKENS), of_group(CACHE), of_group(TOKENS)]
-        + [
-            pl.BlockSpec((2 * HD, width), lambda i, s: (0, 2 * (s[2] // 2) + s[1])),
-            pl.BlockSpec((2 * HD, width), lambda i, s: (0, 2 * (1 - s[2] // 2) + s[1])),
-        ],
-        (shape(CHIPS, ROWS, HD, dtype=bf16),) + (shape(2 * HD, width, dtype=bf16),) * 2,
-        (pl.BlockSpec(memory_space=pl.ANY), piece, piece),
-        scratch=[pltpu.VMEM((2 * SPAN, HD), bf16), pltpu.SemaphoreType.DMA((CHIPS,))],
-        room=60,
-    )
-    place, filled = lax.optimization_barrier((place, filled))
-
-    own = call(
-        state_kernel,
-        place,
-        (ssm_inputs, step_decay, state_inputs),
-        [whole((TOKENS, 2 * HD)), whole((4, TOKENS)), of_group(TOKENS)],
-        shape(2, HD + 8, HD),
-        whole((2, HD + 8, HD)),
-    )
-    both = lax.all_gather(own, "c")
-    packed = call(
-        pack_kernel,
-        place,
-        (both, cache_len, filled),
-        [
-            pl.BlockSpec((2, 1, HD + 8, HD), lambda i, s: (0, s[1], 0, 0)),
-            SMEM,
-            pl.BlockSpec(memory_space=pl.ANY),
-        ],
-        shape(CHIPS, ROWS, HD, dtype=bf16),
-        pl.BlockSpec(memory_space=pl.ANY),
-        scratch=[pltpu.VMEM((HEAD, HD), bf16), pltpu.SemaphoreType.DMA((CHIPS,))],
-        room=60,
-        aliases={3: 0},
-    )
-
     second = flip(second, 2)
     third = flip(second, 1)
     same = lax.all_to_all(packed, CHIP, 0, 0, tiled=True)
@@ -389,17 +426,16 @@
         whole((2, TOKENS, HD)),
     )
     first = flip(first, 1)
+    own_columns = lax.dynamic_slice_in_dim(out_weight, 2 * (near // 2) * width, 2 * width, 1)
+    first, inside = lax.optimization_barrier((first, inside))
     swapped = [swap(first, "c")]
-    own_columns = lax.dynamic_slice_in_dim(out_weight, 2 * (near // 2) * width, 2 * width, 1)
-    same, first, second, swapped, own_columns, inside = lax.optimization_barrier(
-        (same, first, second, swapped, own_columns, inside)
-    )
+    same, second, swapped, own_columns = lax.optimization_barrier((same, second, swapped, own_columns))
     other = swap(same, "c")
     entering = call(
         scan_kernel,
         place,
         (same,),
-        [pl.BlockSpec((CHIPS, HEAD, HD), lambda i, s: (0, 0, 0))],
+        [pl.BlockSpec((CHIPS, TILE, HD), lambda i, s: (0, 0, 0))],
         shape(HD, HD),
         whole((HD, HD)),
     )

time: 126 us -> 123 us (0.976)
  Pallas kernels: 18.6 us -> 15.7 us
    pallas_call x8 -> x5, Pallas kernels: 17.9 us -> 9.65 us  [call(): pl.pallas_call(kernel, out_shape=out_shape, grid_spec=pltpu.PrefetchScala...]
    pallas_call x0 -> x3, Pallas kernels: none -> 5.28 us  [the longest x2 4.46 us: plain(): pl.pallas_call(kernel, out_shape=out_shape, in_specs=in_specs, out_specs=...]
where the time goes in v4:
time: 123 us; the launch traced here: 122 us
  blocking collectives  38.2 us (31%)
  starting transfers between devices  36.1 us (29%)
  waiting for transfers between devices  28.9 us (23%)
  Pallas kernels  15.7 us (13%)
  local copies, waits for them, and re-layouts  2.1 us (2%)
    all_to_all x1, blocking collectives, per_device(): lax.all_to_all(partial.reshape(8, 8, 2 * width), OWNERS, 0, 0, tiled=True)  34.1 us
    ppermute x3, waiting for transfers between devices, flip(): return lax.ppermute(array, NEAR, [(j, j ^ i) for j in range(4)])  19.3 us
    ppermute x5, starting transfers between devices, swap(): return lax.ppermute(array, axis, [(0, 1), (1, 0)])  12.3 us
    ppermute x3, starting transfers between devices, flip(): return lax.ppermute(array, NEAR, [(j, j ^ i) for j in range(4)])  11.9 us
    pallas_call x5, Pallas kernels, call(): pl.pallas_call(kernel, out_shape=out_shape, grid_spec=pltpu.PrefetchScala...  9.65 us
    ppermute x5, waiting for transfers between devices, swap(): return lax.ppermute(array, axis, [(0, 1), (1, 0)])  8.53 us
    all_to_all x1, starting transfers between devices, per_device(): same = lax.all_to_all(packed, CHIP, 0, 0, tiled=True)  7.41 us
    all_to_all x1, starting transfers between devices, per_device(): attended = lax.all_to_all(attended, NEAR, 0, 0, tiled=True)  4.54 us
  transfers between devices with their start and end apart: 10, of which 6 were waited for; matrix products, arithmetic and copies ran while one was open for 1% of the time, Pallas kernels for 5%

profile of v4, /device:TPU:24, one launch (start us, length us, event | category | flops | bytes accessed | tf_op | source)
XLA Modules:
  0.0 122.0 jit_solution(2613353044573879579)
XLA Ops:
  0.0 0.0 copy-start.7
  0.0 0.0 copy-start.6
  0.0 0.0 copy-start.1
  0.7 2.6 %shard_map.118 = (bf16[8,1056,128]{2,1,0:T(8,128)(2,1)}, bf16[256,1024]{1,0:T(8,128)(2,1)}, bf16[256,1024]{1,0:T(8,128)(2,1)}) custom-call(bf16[8,128,128]{2,1,0:T(8,128)(2,1)} %ck_ref.1, bf16[8,256,128]{2,1,0:T(8,128)(2,1)} %nk_ref.1, bf16[8,128,128]{2,1,0:T(8,128)(2,1)} %cv_ref.1, bf16[8,256,128]{2,1,0:T(8,128)(2,1)} %nv_ref.1, bf16[256,4096]{1,0:T(8,128)(2,1)} %w_ref.1, ...), custom_call_target="tpu_custom_call" | custom-call | bytes 4096 | tf_op jit(solution)/shard_map/pallas_call | solution.py:334
  3.3 0.0 copy-done.7
  3.3 0.0 copy-done.6
  3.3 0.0 copy-done.1
  3.3 0.8 shard_map.120
  4.2 2.1 %all-gather = f32[4,136,128]{2,1,0:T(8,128)} all-gather(f32[2,136,128]{2,1,0:T(8,128)S(1)} %shard_map.120), channel_id=2, replica_groups=mesh['x'=4,'yh'=2,'c'=2,'yl'=2,'za'=4,'z1'=2,'z0'=2] {'c'}, dimensions={0}, use_global_device_ids=true | all-gather | bytes 417792 | tf_op jit(solution)/shard_map/all_gather | solution.py:406
  6.3 1.9 %shard_map.121 = bf16[8,1056,128]{2,1,0:T(8,128)(2,1)} custom-call(f32[2,2,136,128]{3,2,1,0:T(8,128)} %bitcast.8, bf16[8,1056,128]{2,1,0:T(8,128)(2,1)} %get-tuple-element.24.filled_ref), custom_call_target="tpu_custom_call", output_to_operand_aliasing={{}: (1, {})} | custom-call | bytes 4096 | tf_op jit(solution)/shard_map/pallas_call | solution.py:334
  8.2 0.0 copy-start.2
  8.2 0.0 copy-start.9
  8.2 7.4 %all-to-all-start = ((bf16[8,1056,128]{2,1,0:T(8,128)(2,1)}), bf16[8,1056,128]{2,1,0:T(8,128)(2,1)S(1)}, u32[]{:S(2)}, u32[]{:S(2)}) async-start(bf16[8,1056,128]{2,1,0:T(8,128)(2,1)} %shard_map.121), calls=%async_computation | async-start | bytes 4325376 | tf_op jit(solution)/shard_map/all_to_all | solution.py:419
  15.6 3.8 %collective-permute-start = (bf16[256,1024]{1,0:T(8,128)(2,1)}, bf16[256,1024]{1,0:T(8,128)(2,1)}, u32[]{:S(2)}, u32[]{:S(2)}) collective-permute-start(bf16[256,1024]{1,0:T(8,128)(2,1)} %get-tuple-element.20), channel_id=1, source_target_pairs={{0,1},{1,0},{2,3},{3,2},{4,5},{5,4},{6,7},{7,6},{8,9},{9,8},{10,11... | collective-permute-start | bytes 1572872 | tf_op jit(solution)/shard_map/ppermute | solution.py:355
  19.5 5.2 %collective-permute-start.1 = (bf16[256,1024]{1,0:T(8,128)(2,1)}, bf16[256,1024]{1,0:T(8,128)(2,1)}, u32[]{:S(2)}, u32[]{:S(2)}) collective-permute-start(bf16[256,1024]{1,0:T(8,128)(2,1)} %get-tuple-element.25), channel_id=1, source_target_pairs={{0,2},{1,3},{2,0},{3,1},{4,6},{5,7},{6,4},{7,5},{8,10},{9,11},{10,... | collective-permute-start | bytes 1572872 | tf_op jit(solution)/shard_map/ppermute | solution.py:355
  24.7 0.1 pad_add_fusion.group_ref.place_ref
  24.7 0.0 copy-done.2
  24.7 0.0 copy-done.9
  24.7 1.8 %shard_map.119.y_ref = f32[2,256,128]{2,1,0:T(8,128)S(1)} custom-call(s32[4]{0:T(128)S(1)} %pad_add_fusion.group_ref.place_ref, bf16[256,256]{1,0:T(8,128)(2,1)S(1)} %copy-done.6, f32[4,256]{1,0:T(4,128)S(1)} %copy-done.7, bf16[8,256,128]{2,1,0:T(8,128)(2,1)S(1)} %copy-done.1, bf16[8,256,128]{2,1,0:T(8,128)(2,1)S(1)} %copy-done.2, f32[4]{0:T(128)S(1)} %copy-done.9), custom_call_target="tpu_custom_call" | custom-call | bytes 4096 | tf_op jit(solution)/shard_map/pallas_call | solution.py:321
  26.5 0.0 copy-start.4
  26.5 0.7 copy-done.4
  27.2 13.3 %collective-permute-done.r1 = bf16[256,1024]{1,0:T(8,128)(2,1)} collective-permute-done((bf16[256,1024]{1,0:T(8,128)(2,1)}, bf16[256,1024]{1,0:T(8,128)(2,1)}, u32[]{:S(2)}, u32[]{:S(2)}) %collective-permute-start) | collective-permute-done | bytes 524320 | tf_op jit(solution)/shard_map/ppermute | solution.py:355
  40.5 1.9 %collective-permute-start.2 = (bf16[256,1024]{1,0:T(8,128)(2,1)}, bf16[256,1024]{1,0:T(8,128)(2,1)}, u32[]{:S(2)}, u32[]{:S(2)}) collective-permute-start(bf16[256,1024]{1,0:T(8,128)(2,1)} %collective-permute-done.r1), channel_id=1, source_target_pairs={{0,32},{32,0},{1,33},{33,1},{2,34},{34,2},{3,35},{35,3},{4,36},{36... | collective-permute-start | bytes 1572872 | tf_op jit(solution)/shard_map/ppermute | solution.py:351
  42.5 0.0 copy-start
  42.5 0.0 copy-start.8
  42.5 1.3 %constant_dynamic-slice_fusion.own_ref = bf16[256,2048]{1,0:T(8,128)(2,1)S(1)} fusion(bf16[256,4096]{1,0:T(8,128)(2,1)} %w_ref.1, s32[]{:T(128)S(6)} %select_n.9), kind=kLoop, calls=%fused_computation.1 | loop fusion | bytes 2097156 | tf_op jit(solution)/shard_map/dynamic_slice | solution.py:429
  43.8 3.8 %collective-permute-done.1.r2 = bf16[256,1024]{1,0:T(8,128)(2,1)} collective-permute-done((bf16[256,1024]{1,0:T(8,128)(2,1)}, bf16[256,1024]{1,0:T(8,128)(2,1)}, u32[]{:S(2)}, u32[]{:S(2)}) %collective-permute-start.1) | collective-permute-done | bytes 524320 | tf_op jit(solution)/shard_map/ppermute | solution.py:355
  47.6 0.0 collective-permute-done.2.s1
  47.6 0.0 all-to-all-done.all_ref.a_ref
  47.6 0.0 copy-start.3
  47.6 0.0 copy-start.5
  47.6 2.1 %collective-permute-start.3 = (bf16[8,1056,128]{2,1,0:T(8,128)(2,1)S(1)}, bf16[8,1056,128]{2,1,0:T(8,128)(2,1)S(1)}, u32[]{:S(2)}, u32[]{:S(2)}) collective-permute-start(bf16[8,1056,128]{2,1,0:T(8,128)(2,1)S(1)} %all-to-all-done.all_ref.a_ref), channel_id=1, source_target_pairs={{0,32},{32,0},{1,33},{33,1},{2,34},{34,2},{3,35},{35,3},{4,36},{36... | collective-permute-start | bytes 6488072 | tf_op jit(solution)/shard_map/ppermute | solution.py:351
  49.7 2.9 %collective-permute-start.4 = (bf16[256,1024]{1,0:T(8,128)(2,1)}, bf16[256,1024]{1,0:T(8,128)(2,1)}, u32[]{:S(2)}, u32[]{:S(2)}) collective-permute-start(bf16[256,1024]{1,0:T(8,128)(2,1)} %collective-permute-done.1.r2), channel_id=1, source_target_pairs={{0,1},{1,0},{2,3},{3,2},{4,5},{5,4},{6,7},{7,6},{8,9},{9,8},{10,11... | collective-permute-start | bytes 1572872 | tf_op jit(solution)/shard_map/ppermute | solution.py:355
  52.6 0.7 shard_map.122
  53.3 1.9 %all-gather.1 = f32[256,128]{1,0:T(8,128)S(1)} all-gather(f32[128,128]{1,0:T(8,128)S(1)} %shard_map.122), channel_id=3, replica_groups=mesh['x'=4,'yh'=2,'c'=2,'yl'=2,'za'=4,'z1'=2,'z0'=2] {'c'}, dimensions={0}, use_global_device_ids=true | all-gather | bytes 196608 | tf_op jit(solution)/shard_map/all_gather | solution.py:442
  55.2 0.0 copy-done
  55.2 0.0 copy-done.8
  55.2 0.0 copy-done.3
  55.2 0.0 copy-done.5
  55.2 1.2 %shard_map.123.q_ref = bf16[512,128]{1,0:T(8,128)(2,1)S(1)} custom-call(s32[4]{0:T(128)S(1)} %pad_add_fusion.group_ref.place_ref, f32[2,256,128]{2,1,0:T(8,128)S(1)} %copy-done.5, f32[4,256]{1,0:T(4,128)S(1)} %copy-done.7, bf16[8,256,128]{2,1,0:T(8,128)(2,1)S(1)} %copy-done.3, f32[2,128,128]{2,1,0:T(8,128)S(1)} %bitcast.11, f32[2,2,136,128]{3,2,1,0:T(8,128)S(1)} %bitcast.9, ...), custom_call_target="tpu_custom_call" | custom-call | bytes 4096 | tf_op jit(solution)/shard_map/pallas_call | solution.py:321
  56.5 0.0 collective-permute-done.3.b_ref
  56.5 3.0 %shard_map.124 = bf16[4,128,256]{2,1,0:T(8,128)(2,1)} custom-call(s32[4]{0:T(128)S(1)} %pad_add_fusion.group_ref.place_ref, bf16[512,128]{1,0:T(8,128)(2,1)S(1)} %shard_map.123.q_ref, bf16[8,1056,128]{2,1,0:T(8,128)(2,1)S(1)} %all-to-all-done.all_ref.a_ref, bf16[8,1056,128]{2,1,0:T(8,128)(2,1)S(1)} %collective-permute-done.3.b_ref), custom_call_target="tpu_custom_call" | custom-call | bytes 4096 | tf_op jit(solution)/shard_map/pallas_call | solution.py:321
  59.5 4.5 %all-to-all-start.1 = ((bf16[4,128,256]{2,1,0:T(8,128)(2,1)}), bf16[4,128,256]{2,1,0:T(8,128)(2,1)S(1)}, u32[]{:S(2)}, u32[]{:S(2)}) async-start(bf16[4,128,256]{2,1,0:T(8,128)(2,1)} %shard_map.124), calls=%async_computation.1 | async-start | bytes 524288 | tf_op jit(solution)/shard_map/all_to_all | solution.py:477
  64.0 2.2 %collective-permute-done.4.r3 = bf16[256,1024]{1,0:T(8,128)(2,1)} collective-permute-done((bf16[256,1024]{1,0:T(8,128)(2,1)}, bf16[256,1024]{1,0:T(8,128)(2,1)}, u32[]{:S(2)}, u32[]{:S(2)}) %collective-permute-start.4) | collective-permute-done | bytes 524320 | tf_op jit(solution)/shard_map/ppermute | solution.py:355
  66.2 1.9 %collective-permute-start.6 = (bf16[256,1024]{1,0:T(8,128)(2,1)}, bf16[256,1024]{1,0:T(8,128)(2,1)S(1)}, u32[]{:S(2)}, u32[]{:S(2)}) collective-permute-start(bf16[256,1024]{1,0:T(8,128)(2,1)} %collective-permute-done.4.r3), channel_id=1, source_target_pairs={{0,32},{32,0},{1,33},{33,1},{2,34},{34,2},{3,35},{35,3},{4,36},{36... | collective-permute-start | bytes 1572872 | tf_op jit(solution)/shard_map/ppermute | solution.py:351
  68.2 2.4 %collective-permute-start.5 = (bf16[256,1024]{1,0:T(8,128)(2,1)}, bf16[256,1024]{1,0:T(8,128)(2,1)S(1)}, u32[]{:S(2)}, u32[]{:S(2)}) collective-permute-start(bf16[256,1024]{1,0:T(8,128)(2,1)} %collective-permute-done.1.r2), channel_id=1, source_target_pairs={{0,32},{32,0},{1,33},{33,1},{2,34},{34,2},{3,35},{35,3},{4,36},{36... | collective-permute-start | bytes 1572872 | tf_op jit(solution)/shard_map/ppermute | solution.py:351
  70.6 0.0 collective-permute-done.6.s3
  70.6 1.7 %collective-permute-done.5.s2 = bf16[256,1024]{1,0:T(8,128)(2,1)S(1)} collective-permute-done((bf16[256,1024]{1,0:T(8,128)(2,1)}, bf16[256,1024]{1,0:T(8,128)(2,1)S(1)}, u32[]{:S(2)}, u32[]{:S(2)}) %collective-permute-start.5) | collective-permute-done | bytes 524320 | tf_op jit(solution)/shard_map/ppermute | solution.py:351
  72.3 1.0 all-to-all-done.1.att_ref
  73.3 3.0 %shard_map.125 = (bf16[64,2048]{1,0:T(8,128)(2,1)S(1)}, bf16[64,2048]{1,0:T(8,128)(2,1)S(1)}) custom-call(s32[4]{0:T(128)S(1)} %pad_add_fusion.group_ref.place_ref, bf16[4,128,256]{2,1,0:T(8,128)(2,1)S(1)} %all-to-all-done.1.att_ref, bf16[256,2048]{1,0:T(8,128)(2,1)S(1)} %constant_dynamic-slice_fusion.own_ref, bf16[256,1024]{1,0:T(8,128)(2,1)} %collective-permute-done.r1, ...), custom_call_target="tpu_custom_call" | custom-call | bytes 4096 | tf_op jit(solution)/shard_map/pallas_call | solution.py:321
  76.3 4.0 %collective-permute-start.7 = (bf16[64,2048]{1,0:T(8,128)(2,1)S(1)}, bf16[64,2048]{1,0:T(8,128)(2,1)S(1)}, u32[]{:S(2)}, u32[]{:S(2)}) collective-permute-start(bf16[64,2048]{1,0:T(8,128)(2,1)S(1)} %get-tuple-element.34), channel_id=1, source_target_pairs={{0,16},{16,0},{1,17},{17,1},{2,18},{18,2},{3,19},{19,3},{4,20},{20... | collective-permute-start | bytes 786440 | tf_op jit(solution)/shard_map/ppermute | solution.py:351
  80.3 6.8 %collective-permute-done.7.second_ref = bf16[64,2048]{1,0:T(8,128)(2,1)S(1)} collective-permute-done((bf16[64,2048]{1,0:T(8,128)(2,1)S(1)}, bf16[64,2048]{1,0:T(8,128)(2,1)S(1)}, u32[]{:S(2)}, u32[]{:S(2)}) %collective-permute-start.7) | collective-permute-done | bytes 262176 | tf_op jit(solution)/shard_map/ppermute | solution.py:351
  87.1 0.1 shard_map.126
  87.2 34.1 %all_to_all.15.parts_ref = bf16[8,8,2048]{2,1,0:T(8,128)(2,1)S(1)} all-to-all(bf16[8,8,2048]{2,1,0:T(8,128)(2,1)S(1)} %bitcast.10), channel_id=1, replica_groups=mesh['x'=4,'yh'=2,'c'=2,'yl'=2,'za'=4,'z1'=2,'z0'=2] {'za','z1'}, dimensions={0} | all-to-all | bytes 524288 | tf_op jit(solution)/shard_map/all_to_all | solution.py:489
  121.3 0.7 shard_map.127
Async XLA Ops:
  0.0 3.3 %copy-start.7 = (f32[4,256]{1,0:T(4,128)S(1)}, f32[4,256]{1,0:T(4,128)}, u32[]{:S(2)}) copy-start(f32[4,256]{1,0:T(4,128)} %decay_ref.2) | copy-start | bytes 12292
  0.0 3.3 %copy-start.6 = (bf16[256,256]{1,0:T(8,128)(2,1)S(1)}, bf16[256,256]{1,0:T(8,128)(2,1)}, u32[]{:S(2)}) copy-start(bf16[256,256]{1,0:T(8,128)(2,1)} %x_ref.3) | copy-start | bytes 393220
  0.0 3.3 %copy-start.1 = (bf16[8,256,128]{2,1,0:T(8,128)(2,1)S(1)}, bf16[8,256,128]{2,1,0:T(8,128)(2,1)}, u32[]{:S(2)}) copy-start(bf16[8,256,128]{2,1,0:T(8,128)(2,1)} %b_hbm.1) | copy-start | bytes 1572868
  8.2 16.5 %copy-start.2 = (bf16[8,256,128]{2,1,0:T(8,128)(2,1)S(1)}, bf16[8,256,128]{2,1,0:T(8,128)(2,1)}, u32[]{:S(2)}) copy-start(bf16[8,256,128]{2,1,0:T(8,128)(2,1)} %c_ref.3) | copy-start | bytes 1572868
  8.2 16.5 %copy-start.9 = (f32[4]{0:T(128)S(1)}, f32[4]{0:T(128)}, u32[]{:S(2)}) copy-start(f32[4]{0:T(128)} %gain_ref.1) | copy-start | bytes 52
  8.2 39.4 %all-to-all-start = ((bf16[8,1056,128]{2,1,0:T(8,128)(2,1)}), bf16[8,1056,128]{2,1,0:T(8,128)(2,1)S(1)}, u32[]{:S(2)}, u32[]{:S(2)}) async-start(bf16[8,1056,128]{2,1,0:T(8,128)(2,1)} %shard_map.121), calls=%async_computation | async-start | bytes 4325376 | tf_op jit(solution)/shard_map/all_to_all | solution.py:419
  15.6 24.9 %collective-permute-start = (bf16[256,1024]{1,0:T(8,128)(2,1)}, bf16[256,1024]{1,0:T(8,128)(2,1)}, u32[]{:S(2)}, u32[]{:S(2)}) collective-permute-start(bf16[256,1024]{1,0:T(8,128)(2,1)} %get-tuple-element.20), channel_id=1, source_target_pairs={{0,1},{1,0},{2,3},{3,2},{4,5},{5,4},{6,7},{7,6},{8,9},{9,8},{10,11... | collective-permute-start | bytes 1572872 | tf_op jit(solution)/shard_map/ppermute | solution.py:355
  19.5 28.2 %collective-permute-start.1 = (bf16[256,1024]{1,0:T(8,128)(2,1)}, bf16[256,1024]{1,0:T(8,128)(2,1)}, u32[]{:S(2)}, u32[]{:S(2)}) collective-permute-start(bf16[256,1024]{1,0:T(8,128)(2,1)} %get-tuple-element.25), channel_id=1, source_target_pairs={{0,2},{1,3},{2,0},{3,1},{4,6},{5,7},{6,4},{7,5},{8,10},{9,11},{10,... | collective-permute-start | bytes 1572872 | tf_op jit(solution)/shard_map/ppermute | solution.py:355
  26.5 0.7 copy-start.4
  40.5 7.1 %collective-permute-start.2 = (bf16[256,1024]{1,0:T(8,128)(2,1)}, bf16[256,1024]{1,0:T(8,128)(2,1)}, u32[]{:S(2)}, u32[]{:S(2)}) collective-permute-start(bf16[256,1024]{1,0:T(8,128)(2,1)} %collective-permute-done.r1), channel_id=1, source_target_pairs={{0,32},{32,0},{1,33},{33,1},{2,34},{34,2},{3,35},{35,3},{4,36},{36... | collective-permute-start | bytes 1572872 | tf_op jit(solution)/shard_map/ppermute | solution.py:351
  42.5 12.8 %copy-start = (f32[4,136,128]{2,1,0:T(8,128)S(1)}, f32[4,136,128]{2,1,0:T(8,128)}, u32[]{:S(2)}) copy-start(f32[4,136,128]{2,1,0:T(8,128)} %all-gather) | copy-start | bytes 835588
  42.5 12.8 %copy-start.8 = (f32[256]{0:T(256)S(1)}, f32[256]{0:T(256)}, u32[]{:S(2)}) copy-start(f32[256]{0:T(256)} %param.17) | copy-start | bytes 3076
  47.6 7.6 %copy-start.3 = (bf16[8,256,128]{2,1,0:T(8,128)(2,1)S(1)}, bf16[8,256,128]{2,1,0:T(8,128)(2,1)}, u32[]{:S(2)}) copy-start(bf16[8,256,128]{2,1,0:T(8,128)(2,1)} %c_ref.3) | copy-start | bytes 1572868
  47.6 7.6 %copy-start.5 = (f32[2,256,128]{2,1,0:T(8,128)S(1)}, f32[2,256,128]{2,1,0:T(8,128)}, u32[]{:S(2)}) copy-start(f32[2,256,128]{2,1,0:T(8,128)} %copy-done.4) | copy-start | bytes 786436
  47.6 8.8 %collective-permute-start.3 = (bf16[8,1056,128]{2,1,0:T(8,128)(2,1)S(1)}, bf16[8,1056,128]{2,1,0:T(8,128)(2,1)S(1)}, u32[]{:S(2)}, u32[]{:S(2)}) collective-permute-start(bf16[8,1056,128]{2,1,0:T(8,128)(2,1)S(1)} %all-to-all-done.all_ref.a_ref), channel_id=1, source_target_pairs={{0,32},{32,0},{1,33},{33,1},{2,34},{34,2},{3,35},{35,3},{4,36},{36... | collective-permute-start | bytes 6488072 | tf_op jit(solution)/shard_map/ppermute | solution.py:351
  49.7 16.5 %collective-permute-start.4 = (bf16[256,1024]{1,0:T(8,128)(2,1)}, bf16[256,1024]{1,0:T(8,128)(2,1)}, u32[]{:S(2)}, u32[]{:S(2)}) collective-permute-start(bf16[256,1024]{1,0:T(8,128)(2,1)} %collective-permute-done.1.r2), channel_id=1, source_target_pairs={{0,1},{1,0},{2,3},{3,2},{4,5},{5,4},{6,7},{7,6},{8,9},{9,8},{10,11... | collective-permute-start | bytes 1572872 | tf_op jit(solution)/shard_map/ppermute | solution.py:355
  59.5 13.8 %all-to-all-start.1 = ((bf16[4,128,256]{2,1,0:T(8,128)(2,1)}), bf16[4,128,256]{2,1,0:T(8,128)(2,1)S(1)}, u32[]{:S(2)}, u32[]{:S(2)}) async-start(bf16[4,128,256]{2,1,0:T(8,128)(2,1)} %shard_map.124), calls=%async_computation.1 | async-start | bytes 524288 | tf_op jit(solution)/shard_map/all_to_all | solution.py:477
  66.2 4.3 %collective-permute-start.6 = (bf16[256,1024]{1,0:T(8,128)(2,1)}, bf16[256,1024]{1,0:T(8,128)(2,1)S(1)}, u32[]{:S(2)}, u32[]{:S(2)}) collective-permute-start(bf16[256,1024]{1,0:T(8,128)(2,1)} %collective-permute-done.4.r3), channel_id=1, source_target_pairs={{0,32},{32,0},{1,33},{33,1},{2,34},{34,2},{3,35},{35,3},{4,36},{36... | collective-permute-start | bytes 1572872 | tf_op jit(solution)/shard_map/ppermute | solution.py:351
  68.2 4.1 %collective-permute-start.5 = (bf16[256,1024]{1,0:T(8,128)(2,1)}, bf16[256,1024]{1,0:T(8,128)(2,1)S(1)}, u32[]{:S(2)}, u32[]{:S(2)}) collective-permute-start(bf16[256,1024]{1,0:T(8,128)(2,1)} %collective-permute-done.1.r2), channel_id=1, source_target_pairs={{0,32},{32,0},{1,33},{33,1},{2,34},{34,2},{3,35},{35,3},{4,36},{36... | collective-permute-start | bytes 1572872 | tf_op jit(solution)/shard_map/ppermute | solution.py:351
  76.3 10.8 %collective-permute-start.7 = (bf16[64,2048]{1,0:T(8,128)(2,1)S(1)}, bf16[64,2048]{1,0:T(8,128)(2,1)S(1)}, u32[]{:S(2)}, u32[]{:S(2)}) collective-permute-start(bf16[64,2048]{1,0:T(8,128)(2,1)S(1)} %get-tuple-element.34), channel_id=1, source_target_pairs={{0,16},{16,0},{1,17},{17,1},{2,18},{18,2},{3,19},{19,3},{4,20},{20... | collective-permute-start | bytes 786440 | tf_op jit(solution)/shard_map/ppermute | solution.py:351

commit v5 on v4

--- a/solution.py
+++ b/solution.py
@@ -27,6 +27,7 @@
 PIPE = ("x", "yh", "c")
 TENSOR = ("yl", "za", "z1", "z0")
 CHIP = ("x", "yh")
+BLOCKS = ("yh", "x")
 NEAR = ("z1", "z0")
 OWNERS = ("za", "z1")
 
@@ -90,6 +91,10 @@
         out_ref[half, HD : HD + 8, :] = spread(jnp.broadcast_to(total, (8, 4)), half, 8)
 
 
+def block_of(chip):
+    return 4 * (chip % 2) + chip // 2
+
+
 def spread_copies(held, out_ref, begin, sems):
     rows = held.shape[0]
     copies = [pltpu.make_async_copy(held, out_ref.at[k, begin : begin + rows], sems.at[k]) for k in range(CHIPS)]
@@ -97,6 +102,10 @@
         copy.start()
     for copy in copies:
         copy.wait()
+
+
+def block_of(chip):
+    return 4 * (chip % 2) + chip // 2
 
 
 def spread_copies(held, out_ref, begin, sems):
@@ -153,13 +162,14 @@
         copy.wait()
 
 
-def scan_kernel(place_ref, all_ref, out_ref):
-    chip = place_ref[0]
+def scan_kernel(all_ref, out_ref):
+    chip = lax.axis_index(CHIP)
     state = jnp.zeros((HD, HD), f32)
     for k in range(CHIPS - 1):
-        tile = all_ref[k, 2 * HD : TILE, :].astype(f32)
+        block = block_of(k)
+        tile = all_ref[block, 2 * HD : TILE, :].astype(f32)
         decay = tile[0:1] + tile[1:2] + tile[2:3]
-        here = all_ref[k, 0:HD, :].astype(f32) + all_ref[k, HD : 2 * HD, :].astype(f32)
+        here = all_ref[block, 0:HD, :].astype(f32) + all_ref[block, HD : 2 * HD, :].astype(f32)
         state = jnp.where(k < chip, decay * state + here, state)
     out_ref[...] = state
 
@@ -181,11 +191,14 @@
         y_ref[half] = jnp.where(low, pieces[0], pieces[1]) + skip * inputs.astype(f32)
 
 
-def query_kernel(place_ref, y_ref, decay_ref, c_ref, carried_ref, both_ref, gain_ref, out_ref):
-    core = place_ref[1]
-    readout = c_ref[0]
+def query_kernel(y_ref, decay_ref, c_hbm, carried_ref, both_ref, gain_ref, out_ref, c_ref, sem):
+    core = lax.axis_index("c")
+    copy = pltpu.make_async_copy(c_hbm.at[own_group()], c_ref, sem)
+    copy.start()
     low = low_lanes(TOKENS)
     fade = jnp.exp(-cum_columns(decay_ref[...]))
+    copy.wait()
+    readout = c_ref[...]
     for half in range(2):
         carried = carried_ref[half]
         after = both_ref[0, half, HD : HD + 1] * carried + both_ref[0, half, 0:HD]
@@ -200,15 +213,15 @@
         out_ref[half * TOKENS : (half + 1) * TOKENS, :] = normed.astype(bf16)
 
 
-def attend_kernel(place_ref, q_ref, a_ref, b_ref, out_ref, scores_ref, top_ref, sum_ref, acc_ref):
-    chip, core = place_ref[0], place_ref[1]
+def attend_kernel(q_ref, a_ref, b_ref, out_ref, scores_ref, top_ref, sum_ref, acc_ref):
+    chip, core = lax.axis_index(CHIP), lax.axis_index("c")
     count = q_ref.shape[0]
     sides = (a_ref, b_ref)
     top_ref[...] = jnp.full((count, HD), -jnp.inf, f32)
 
     def score(k, side, extra, causal):
-        bias = sides[side][k, TILE:HEAD, :].astype(f32)[0:1]
-        raw = dot(q_ref[...], sides[side][k, HEAD : HEAD + SPAN, :], ((1,), (1,))) * SCALE
+        bias = sides[side][block_of(k), TILE:HEAD, :].astype(f32)[0:1]
+        raw = dot(q_ref[...], sides[side][block_of(k), HEAD : HEAD + SPAN, :], ((1,), (1,))) * SCALE
         top = top_ref[...]
         for tile in range(SPAN // HD):
             part = raw[:, tile * HD : (tile + 1) * HD]
@@ -249,7 +262,7 @@
                 expo = jnp.exp2(part - top)
                 total = total + expo
                 probs.append(expo.astype(bf16))
-            acc = acc + dot(jnp.concatenate(probs, axis=1), sides[side][k, HEAD + SPAN :, :])
+            acc = acc + dot(jnp.concatenate(probs, axis=1), sides[side][block_of(k), HEAD + SPAN :, :])
         sum_ref[...] = total
         acc_ref[...] = acc
         return carry
@@ -266,8 +279,8 @@
                 out_ref[2 * z1 + z0, :, half * HD : (half + 1) * HD] = piece
 
 
-def project_kernel(place_ref, att_ref, own_ref, r1, r2, r3, s1, s2, s3, keep_ref, send_ref):
-    near, core, side = place_ref[2], place_ref[1], place_ref[3] // 4
+def project_kernel(att_ref, own_ref, r1, r2, r3, s1, s2, s3, keep_ref, send_ref):
+    near, core, side = lax.axis_index(NEAR), lax.axis_index("c"), lax.axis_index("yl")
     rows, width = keep_ref.shape[0], r1.shape[1]
 
     def run(others, begin):
@@ -330,7 +343,7 @@
     )(scalars, *args)
 
 
-def plain(kernel, args, in_specs, out_shape, out_specs, scratch, aliases=None):
+def plain(kernel, args, in_specs, out_shape, out_specs, scratch=(), aliases=None, room=16):
     return pl.pallas_call(
         kernel,
         out_shape=out_shape,
@@ -338,7 +351,7 @@
         out_specs=out_specs,
         scratch_shapes=scratch,
         input_output_aliases=aliases or {},
-        compiler_params=pltpu.CompilerParams(vmem_limit_bytes=60 * 1024 * 1024),
+        compiler_params=pltpu.CompilerParams(vmem_limit_bytes=room * 1024 * 1024),
         cost_estimate=pl.CostEstimate(flops=0, bytes_accessed=1 << 12, transcendentals=0),
     )(*args)
 
@@ -391,18 +404,18 @@
             pltpu.SemaphoreType.DMA((2,)),
             pltpu.SemaphoreType.DMA((CHIPS,)),
         ],
+        room=60,
     )
     step_decay, filled = lax.optimization_barrier((step_decay, filled))
 
-    own = pl.pallas_call(
+    own = plain(
         state_kernel,
-        out_shape=shape(2, HD + 8, HD),
-        in_specs=[vmem, vmem, hbm],
-        out_specs=vmem,
-        scratch_shapes=[pltpu.VMEM((TOKENS, HD), bf16), pltpu.SemaphoreType.DMA],
-        compiler_params=pltpu.CompilerParams(vmem_limit_bytes=16 * 1024 * 1024),
-        cost_estimate=pl.CostEstimate(flops=0, bytes_accessed=1 << 12, transcendentals=0),
-    )(ssm_inputs, step_decay, state_inputs)
+        (ssm_inputs, step_decay, state_inputs),
+        [vmem, vmem, hbm],
+        shape(2, HD + 8, HD),
+        vmem,
+        [pltpu.VMEM((TOKENS, HD), bf16), pltpu.SemaphoreType.DMA],
+    )
     both = lax.all_gather(own, "c")
     packed = plain(
         pack_kernel,
@@ -412,11 +425,12 @@
         hbm,
         [pltpu.VMEM((TILE, HD), bf16), pltpu.SemaphoreType.DMA((CHIPS,))],
         {1: 0},
+        room=60,
     )
     place = jnp.stack([lax.axis_index(CHIP), core, near, group]).astype(jnp.int32)
     second = flip(second, 2)
     third = flip(second, 1)
-    same = lax.all_to_all(packed, CHIP, 0, 0, tiled=True)
+    same = lax.all_to_all(packed, BLOCKS, 0, 0, tiled=True)
     inside = call(
         inside_kernel,
         place,
@@ -431,44 +445,24 @@
     swapped = [swap(first, "c")]
     same, second, swapped, own_columns = lax.optimization_barrier((same, second, swapped, own_columns))
     other = swap(same, "c")
-    entering = call(
-        scan_kernel,
-        place,
-        (same,),
-        [pl.BlockSpec((CHIPS, TILE, HD), lambda i, s: (0, 0, 0))],
-        shape(HD, HD),
-        whole((HD, HD)),
-    )
+    entering = plain(scan_kernel, (same,), [vmem], shape(HD, HD), vmem)
     carried = lax.all_gather(entering, "c")
-    queries = call(
+    queries = plain(
         query_kernel,
-        place,
         (inside, step_decay, state_readout, carried, both, norm_gain.reshape(1, 2 * HD)),
-        [
-            whole((2, TOKENS, HD)),
-            whole((4, TOKENS)),
-            of_group(TOKENS),
-            whole((2, HD, HD)),
-            whole((2, 2, HD + 8, HD)),
-            whole((1, 2 * HD)),
-        ],
+        [vmem, vmem, hbm, vmem, vmem, vmem],
         shape(2 * TOKENS, HD, dtype=bf16),
-        whole((2 * TOKENS, HD)),
-    )
-
-    attended = call(
+        vmem,
+        [pltpu.VMEM((TOKENS, HD), bf16), pltpu.SemaphoreType.DMA],
+    )
+
+    attended = plain(
         attend_kernel,
-        place,
         (queries, same, other),
-        [pl.BlockSpec(memory_space=pltpu.VMEM)] * 3,
+        [vmem] * 3,
         shape(4, TOKENS // 2, 2 * HD, dtype=bf16),
-        whole((4, TOKENS // 2, 2 * HD)),
-        scratch=[
-            pltpu.VMEM((CHIPS, 2 * TOKENS, 2 * SPAN), f32),
-            pltpu.VMEM((2 * TOKENS, HD), f32),
-            pltpu.VMEM((2 * TOKENS, HD), f32),
-            pltpu.VMEM((2 * TOKENS, HD), f32),
-        ],
+        vmem,
+        [pltpu.VMEM((CHIPS, 2 * TOKENS, 2 * SPAN), f32)] + [pltpu.VMEM((2 * TOKENS, HD), f32)] * 3,
         room=24,
     )
     attended, second = lax.optimization_barrier((attended, second))
@@ -476,9 +470,8 @@
     swapped = swapped + [swap(part, "c") for part in (second, third)]
     attended = lax.all_to_all(attended, NEAR, 0, 0, tiled=True)
     vmem = pl.BlockSpec(memory_space=pltpu.VMEM)
-    keep, send = call(
+    keep, send = plain(
         project_kernel,
-        place,
         (attended, own_columns, *received, *swapped),
         [vmem] * 8,
         (shape(64, 2 * width, dtype=bf16),) * 2,

time: 123 us -> 124 us (level)
  waiting for transfers between devices: 28.9 us -> 34.7 us
  starting transfers between devices: 36.1 us -> 33.1 us
  Pallas kernels: 15.7 us -> 13.8 us
    pallas_call x5 -> x1, Pallas kernels: 9.65 us -> 1.76 us  [call(): pl.pallas_call(kernel, out_shape=out_shape, grid_spec=pltpu.PrefetchScala...]
    pallas_call x2 -> x7, Pallas kernels: 4.46 us -> 11.4 us  [plain(): pl.pallas_call(kernel, out_shape=out_shape, in_specs=in_specs, out_specs=...]
    ppermute x3, waiting for transfers between devices: 19.3 us -> 25.2 us  [flip(): return lax.ppermute(array, NEAR, [(j, j ^ i) for j in range(4)])]
    ppermute x5, starting transfers between devices: 12.3 us -> 10.9 us  [swap(): return lax.ppermute(array, axis, [(0, 1), (1, 0)])]
  transfers between devices with their start and end apart: 10 -> 10, of which waited for: 6 -> 5; matrix products, arithmetic and copies ran while one was open for 1% -> 1% of each run, Pallas kernels for 5% -> 4%
where the time goes in v5:
time: 124 us; the launch traced here: 123 us
  blocking collectives  38.1 us (31%)
  waiting for transfers between devices  34.7 us (28%)
  starting transfers between devices  33.1 us (27%)
  Pallas kernels  13.8 us (11%)
  local copies, waits for them, and re-layouts  2.1 us (2%)
    all_to_all x1, blocking collectives, per_device(): lax.all_to_all(partial.reshape(8, 8, 2 * width), OWNERS, 0, 0, tiled=True)  33.7 us
    ppermute x3, waiting for transfers between devices, flip(): return lax.ppermute(array, NEAR, [(j, j ^ i) for j in range(4)])  25.2 us
    pallas_call x7, Pallas kernels, plain(): pl.pallas_call(kernel, out_shape=out_shape, in_specs=in_specs, out_specs=...  11.4 us
    ppermute x5, starting transfers between devices, swap(): return lax.ppermute(array, axis, [(0, 1), (1, 0)])  10.9 us
    ppermute x3, starting transfers between devices, flip(): return lax.ppermute(array, NEAR, [(j, j ^ i) for j in range(4)])  10.9 us
    ppermute x5, waiting for transfers between devices, swap(): return lax.ppermute(array, axis, [(0, 1), (1, 0)])  9.53 us
    all_to_all x1, starting transfers between devices, per_device(): same = lax.all_to_all(packed, BLOCKS, 0, 0, tiled=True)  7.41 us
    all_to_all x1, starting transfers between devices, per_device(): attended = lax.all_to_all(attended, NEAR, 0, 0, tiled=True)  3.82 us
  transfers between devices with their start and end apart: 10, of which 5 were waited for; matrix products, arithmetic and copies ran while one was open for 1% of the time, Pallas kernels for 4%

profile of v5, /device:TPU:24, one launch (start us, length us, event | category | flops | bytes accessed | tf_op | source)
XLA Modules:
  0.0 122.9 jit_solution(15626829634938281703)
XLA Ops:
  0.0 0.0 copy-start.7
  0.0 0.0 copy-start.6
  0.0 0.0 copy-start.1
  0.7 2.6 %shard_map.118 = (bf16[8,1056,128]{2,1,0:T(8,128)(2,1)}, bf16[256,1024]{1,0:T(8,128)(2,1)}, bf16[256,1024]{1,0:T(8,128)(2,1)}) custom-call(bf16[8,128,128]{2,1,0:T(8,128)(2,1)} %ck_ref.1, bf16[8,256,128]{2,1,0:T(8,128)(2,1)} %nk_ref.1, bf16[8,128,128]{2,1,0:T(8,128)(2,1)} %cv_ref.1, bf16[8,256,128]{2,1,0:T(8,128)(2,1)} %nv_ref.1, bf16[256,4096]{1,0:T(8,128)(2,1)} %w_ref.1, ...), custom_call_target="tpu_custom_call" | custom-call | bytes 4096 | tf_op jit(solution)/shard_map/pallas_call | solution.py:347
  3.3 0.0 copy-done.7
  3.3 0.0 copy-done.6
  3.3 0.0 copy-done.1
  3.3 0.8 shard_map.120
  4.2 2.1 %all-gather = f32[4,136,128]{2,1,0:T(8,128)} all-gather(f32[2,136,128]{2,1,0:T(8,128)S(1)} %shard_map.120), channel_id=2, replica_groups=mesh['x'=4,'yh'=2,'c'=2,'yl'=2,'za'=4,'z1'=2,'z0'=2] {'c'}, dimensions={0}, use_global_device_ids=true | all-gather | bytes 417792 | tf_op jit(solution)/shard_map/all_gather | solution.py:419
  6.3 1.9 %shard_map.121 = bf16[8,1056,128]{2,1,0:T(8,128)(2,1)} custom-call(f32[2,2,136,128]{3,2,1,0:T(8,128)} %bitcast.8, bf16[8,1056,128]{2,1,0:T(8,128)(2,1)} %get-tuple-element.24.filled_ref), custom_call_target="tpu_custom_call", output_to_operand_aliasing={{}: (1, {})} | custom-call | bytes 4096 | tf_op jit(solution)/shard_map/pallas_call | solution.py:347
  8.2 0.0 copy-start.2
  8.2 0.0 copy-start.9
  8.2 7.4 %all-to-all-start = ((bf16[8,1056,128]{2,1,0:T(8,128)(2,1)}), bf16[8,1056,128]{2,1,0:T(8,128)(2,1)S(1)}, u32[]{:S(2)}, u32[]{:S(2)}) async-start(bf16[8,1056,128]{2,1,0:T(8,128)(2,1)} %shard_map.121), calls=%async_computation | async-start | bytes 4325376 | tf_op jit(solution)/shard_map/all_to_all | solution.py:433
  15.6 3.8 %collective-permute-start = (bf16[256,1024]{1,0:T(8,128)(2,1)}, bf16[256,1024]{1,0:T(8,128)(2,1)}, u32[]{:S(2)}, u32[]{:S(2)}) collective-permute-start(bf16[256,1024]{1,0:T(8,128)(2,1)} %get-tuple-element.20), channel_id=1, source_target_pairs={{0,1},{1,0},{2,3},{3,2},{4,5},{5,4},{6,7},{7,6},{8,9},{9,8},{10,11... | collective-permute-start | bytes 1572872 | tf_op jit(solution)/shard_map/ppermute | solution.py:368
  19.5 5.2 %collective-permute-start.1 = (bf16[256,1024]{1,0:T(8,128)(2,1)}, bf16[256,1024]{1,0:T(8,128)(2,1)}, u32[]{:S(2)}, u32[]{:S(2)}) collective-permute-start(bf16[256,1024]{1,0:T(8,128)(2,1)} %get-tuple-element.25), channel_id=1, source_target_pairs={{0,2},{1,3},{2,0},{3,1},{4,6},{5,7},{6,4},{7,5},{8,10},{9,11},{10,... | collective-permute-start | bytes 1572872 | tf_op jit(solution)/shard_map/ppermute | solution.py:368
  24.7 0.1 pad_add_fusion.group_ref
  24.7 0.0 copy-done.2
  24.7 0.0 copy-done.9
  24.7 1.8 %shard_map.119.y_ref = f32[2,256,128]{2,1,0:T(8,128)S(1)} custom-call(s32[4]{0:T(128)S(1)} %pad_add_fusion.group_ref, bf16[256,256]{1,0:T(8,128)(2,1)S(1)} %copy-done.6, f32[4,256]{1,0:T(4,128)S(1)} %copy-done.7, bf16[8,256,128]{2,1,0:T(8,128)(2,1)S(1)} %copy-done.1, bf16[8,256,128]{2,1,0:T(8,128)(2,1)S(1)} %copy-done.2, f32[4]{0:T(128)S(1)} %copy-done.9), custom_call_target="tpu_custom_call" | custom-call | bytes 4096 | tf_op jit(solution)/shard_map/pallas_call | solution.py:334
  26.5 0.0 copy-start.4
  26.5 0.7 copy-done.4
  27.2 13.3 %collective-permute-done.r1 = bf16[256,1024]{1,0:T(8,128)(2,1)} collective-permute-done((bf16[256,1024]{1,0:T(8,128)(2,1)}, bf16[256,1024]{1,0:T(8,128)(2,1)}, u32[]{:S(2)}, u32[]{:S(2)}) %collective-permute-start) | collective-permute-done | bytes 524320 | tf_op jit(solution)/shard_map/ppermute | solution.py:368
  40.5 1.9 %collective-permute-start.2 = (bf16[256,1024]{1,0:T(8,128)(2,1)}, bf16[256,1024]{1,0:T(8,128)(2,1)}, u32[]{:S(2)}, u32[]{:S(2)}) collective-permute-start(bf16[256,1024]{1,0:T(8,128)(2,1)} %collective-permute-done.r1), channel_id=1, source_target_pairs={{0,32},{32,0},{1,33},{33,1},{2,34},{34,2},{3,35},{35,3},{4,36},{36... | collective-permute-start | bytes 1572872 | tf_op jit(solution)/shard_map/ppermute | solution.py:364
  42.5 0.0 copy-start
  42.5 0.0 copy-start.8
  42.5 1.3 %constant_dynamic-slice_fusion.own_ref = bf16[256,2048]{1,0:T(8,128)(2,1)S(1)} fusion(bf16[256,4096]{1,0:T(8,128)(2,1)} %w_ref.1, s32[]{:T(128)S(6)} %select_n.9), kind=kLoop, calls=%fused_computation.1 | loop fusion | bytes 2097156 | tf_op jit(solution)/shard_map/dynamic_slice | solution.py:443
  43.8 3.8 %collective-permute-done.1.r2 = bf16[256,1024]{1,0:T(8,128)(2,1)} collective-permute-done((bf16[256,1024]{1,0:T(8,128)(2,1)}, bf16[256,1024]{1,0:T(8,128)(2,1)}, u32[]{:S(2)}, u32[]{:S(2)}) %collective-permute-start.1) | collective-permute-done | bytes 524320 | tf_op jit(solution)/shard_map/ppermute | solution.py:368
  47.6 0.0 collective-permute-done.2.s1
  47.6 0.0 all-to-all-done.all_ref.a_ref
  47.6 0.0 copy-start.3
  47.6 0.0 copy-start.5
  47.6 2.1 %collective-permute-start.3 = (bf16[8,1056,128]{2,1,0:T(8,128)(2,1)S(1)}, bf16[8,1056,128]{2,1,0:T(8,128)(2,1)S(1)}, u32[]{:S(2)}, u32[]{:S(2)}) collective-permute-start(bf16[8,1056,128]{2,1,0:T(8,128)(2,1)S(1)} %all-to-all-done.all_ref.a_ref), channel_id=1, source_target_pairs={{0,32},{32,0},{1,33},{33,1},{2,34},{34,2},{3,35},{35,3},{4,36},{36... | collective-permute-start | bytes 6488072 | tf_op jit(solution)/shard_map/ppermute | solution.py:364
  49.7 1.9 %collective-permute-start.4 = (bf16[256,1024]{1,0:T(8,128)(2,1)}, bf16[256,1024]{1,0:T(8,128)(2,1)}, u32[]{:S(2)}, u32[]{:S(2)}) collective-permute-start(bf16[256,1024]{1,0:T(8,128)(2,1)} %collective-permute-done.1.r2), channel_id=1, source_target_pairs={{0,1},{1,0},{2,3},{3,2},{4,5},{5,4},{6,7},{7,6},{8,9},{9,8},{10,11... | collective-permute-start | bytes 1572872 | tf_op jit(solution)/shard_map/ppermute | solution.py:368
  51.6 0.1 shard_map.122
  51.7 2.3 %all-gather.1 = f32[256,128]{1,0:T(8,128)S(1)} all-gather(f32[128,128]{1,0:T(8,128)S(1)} %shard_map.122), channel_id=3, replica_groups=mesh['x'=4,'yh'=2,'c'=2,'yl'=2,'za'=4,'z1'=2,'z0'=2] {'c'}, dimensions={0}, use_global_device_ids=true | all-gather | bytes 196608 | tf_op jit(solution)/shard_map/all_gather | solution.py:449
  54.0 0.0 copy-done
  54.0 0.0 copy-done.8
  54.0 0.0 copy-done.3
  54.0 0.0 copy-done.5
  54.0 0.9 shard_map.123.q_ref
  55.0 0.0 collective-permute-done.3.b_ref
  55.0 2.6 %shard_map.124 = bf16[4,128,256]{2,1,0:T(8,128)(2,1)} custom-call(bf16[512,128]{1,0:T(8,128)(2,1)S(1)} %shard_map.123.q_ref, bf16[8,1056,128]{2,1,0:T(8,128)(2,1)S(1)} %all-to-all-done.all_ref.a_ref, bf16[8,1056,128]{2,1,0:T(8,128)(2,1)S(1)} %collective-permute-done.3.b_ref), custom_call_target="tpu_custom_call" | custom-call | bytes 4096 | tf_op jit(solution)/shard_map/pallas_call | solution.py:347
  57.6 3.8 %all-to-all-start.1 = ((bf16[4,128,256]{2,1,0:T(8,128)(2,1)}), bf16[4,128,256]{2,1,0:T(8,128)(2,1)S(1)}, u32[]{:S(2)}, u32[]{:S(2)}) async-start(bf16[4,128,256]{2,1,0:T(8,128)(2,1)} %shard_map.124), calls=%async_computation.1 | async-start | bytes 524288 | tf_op jit(solution)/shard_map/all_to_all | solution.py:471
  61.4 8.1 %collective-permute-done.4.r3 = bf16[256,1024]{1,0:T(8,128)(2,1)} collective-permute-done((bf16[256,1024]{1,0:T(8,128)(2,1)}, bf16[256,1024]{1,0:T(8,128)(2,1)}, u32[]{:S(2)}, u32[]{:S(2)}) %collective-permute-start.4) | collective-permute-done | bytes 524320 | tf_op jit(solution)/shard_map/ppermute | solution.py:368
  69.4 1.9 %collective-permute-start.6 = (bf16[256,1024]{1,0:T(8,128)(2,1)}, bf16[256,1024]{1,0:T(8,128)(2,1)S(1)}, u32[]{:S(2)}, u32[]{:S(2)}) collective-permute-start(bf16[256,1024]{1,0:T(8,128)(2,1)} %collective-permute-done.4.r3), channel_id=1, source_target_pairs={{0,32},{32,0},{1,33},{33,1},{2,34},{34,2},{3,35},{35,3},{4,36},{36... | collective-permute-start | bytes 1572872 | tf_op jit(solution)/shard_map/ppermute | solution.py:364
  71.4 2.4 %collective-permute-start.5 = (bf16[256,1024]{1,0:T(8,128)(2,1)}, bf16[256,1024]{1,0:T(8,128)(2,1)S(1)}, u32[]{:S(2)}, u32[]{:S(2)}) collective-permute-start(bf16[256,1024]{1,0:T(8,128)(2,1)} %collective-permute-done.1.r2), channel_id=1, source_target_pairs={{0,32},{32,0},{1,33},{33,1},{2,34},{34,2},{3,35},{35,3},{4,36},{36... | collective-permute-start | bytes 1572872 | tf_op jit(solution)/shard_map/ppermute | solution.py:364
  73.8 0.0 collective-permute-done.6.s3
  73.8 1.7 %collective-permute-done.5.s2 = bf16[256,1024]{1,0:T(8,128)(2,1)S(1)} collective-permute-done((bf16[256,1024]{1,0:T(8,128)(2,1)}, bf16[256,1024]{1,0:T(8,128)(2,1)S(1)}, u32[]{:S(2)}, u32[]{:S(2)}) %collective-permute-start.5) | collective-permute-done | bytes 524320 | tf_op jit(solution)/shard_map/ppermute | solution.py:364
  75.5 0.0 all-to-all-done.1.att_ref
  75.5 2.5 %shard_map.125 = (bf16[64,2048]{1,0:T(8,128)(2,1)S(1)}, bf16[64,2048]{1,0:T(8,128)(2,1)S(1)}) custom-call(bf16[4,128,256]{2,1,0:T(8,128)(2,1)S(1)} %all-to-all-done.1.att_ref, bf16[256,2048]{1,0:T(8,128)(2,1)S(1)} %constant_dynamic-slice_fusion.own_ref, bf16[256,1024]{1,0:T(8,128)(2,1)} %collective-permute-done.r1, ...), custom_call_target="tpu_custom_call" | custom-call | bytes 4096 | tf_op jit(solution)/shard_map/pallas_call | solution.py:347
  78.0 2.7 %collective-permute-start.7 = (bf16[64,2048]{1,0:T(8,128)(2,1)S(1)}, bf16[64,2048]{1,0:T(8,128)(2,1)S(1)}, u32[]{:S(2)}, u32[]{:S(2)}) collective-permute-start(bf16[64,2048]{1,0:T(8,128)(2,1)S(1)} %get-tuple-element.34), channel_id=1, source_target_pairs={{0,16},{16,0},{1,17},{17,1},{2,18},{18,2},{3,19},{19,3},{4,20},{20... | collective-permute-start | bytes 786440 | tf_op jit(solution)/shard_map/ppermute | solution.py:364
  80.7 7.8 %collective-permute-done.7.second_ref = bf16[64,2048]{1,0:T(8,128)(2,1)S(1)} collective-permute-done((bf16[64,2048]{1,0:T(8,128)(2,1)S(1)}, bf16[64,2048]{1,0:T(8,128)(2,1)S(1)}, u32[]{:S(2)}, u32[]{:S(2)}) %collective-permute-start.7) | collective-permute-done | bytes 262176 | tf_op jit(solution)/shard_map/ppermute | solution.py:364
  88.5 0.1 shard_map.126
  88.5 33.7 %all_to_all.15.parts_ref = bf16[8,8,2048]{2,1,0:T(8,128)(2,1)S(1)} all-to-all(bf16[8,8,2048]{2,1,0:T(8,128)(2,1)S(1)} %bitcast.10), channel_id=1, replica_groups=mesh['x'=4,'yh'=2,'c'=2,'yl'=2,'za'=4,'z1'=2,'z0'=2] {'za','z1'}, dimensions={0} | all-to-all | bytes 524288 | tf_op jit(solution)/shard_map/all_to_all | solution.py:482
  122.2 0.7 shard_map.127
Async XLA Ops:
  0.0 3.3 %copy-start.7 = (f32[4,256]{1,0:T(4,128)S(1)}, f32[4,256]{1,0:T(4,128)}, u32[]{:S(2)}) copy-start(f32[4,256]{1,0:T(4,128)} %decay_ref.2) | copy-start | bytes 12292
  0.0 3.3 %copy-start.6 = (bf16[256,256]{1,0:T(8,128)(2,1)S(1)}, bf16[256,256]{1,0:T(8,128)(2,1)}, u32[]{:S(2)}) copy-start(bf16[256,256]{1,0:T(8,128)(2,1)} %x_ref.3) | copy-start | bytes 393220
  0.0 3.3 %copy-start.1 = (bf16[8,256,128]{2,1,0:T(8,128)(2,1)S(1)}, bf16[8,256,128]{2,1,0:T(8,128)(2,1)}, u32[]{:S(2)}) copy-start(bf16[8,256,128]{2,1,0:T(8,128)(2,1)} %b_hbm.1) | copy-start | bytes 1572868
  8.2 16.5 %copy-start.2 = (bf16[8,256,128]{2,1,0:T(8,128)(2,1)S(1)}, bf16[8,256,128]{2,1,0:T(8,128)(2,1)}, u32[]{:S(2)}) copy-start(bf16[8,256,128]{2,1,0:T(8,128)(2,1)} %c_hbm.1) | copy-start | bytes 1572868
  8.2 16.5 %copy-start.9 = (f32[4]{0:T(128)S(1)}, f32[4]{0:T(128)}, u32[]{:S(2)}) copy-start(f32[4]{0:T(128)} %gain_ref.1) | copy-start | bytes 52
  8.2 39.4 %all-to-all-start = ((bf16[8,1056,128]{2,1,0:T(8,128)(2,1)}), bf16[8,1056,128]{2,1,0:T(8,128)(2,1)S(1)}, u32[]{:S(2)}, u32[]{:S(2)}) async-start(bf16[8,1056,128]{2,1,0:T(8,128)(2,1)} %shard_map.121), calls=%async_computation | async-start | bytes 4325376 | tf_op jit(solution)/shard_map/all_to_all | solution.py:433
  15.6 24.9 %collective-permute-start = (bf16[256,1024]{1,0:T(8,128)(2,1)}, bf16[256,1024]{1,0:T(8,128)(2,1)}, u32[]{:S(2)}, u32[]{:S(2)}) collective-permute-start(bf16[256,1024]{1,0:T(8,128)(2,1)} %get-tuple-element.20), channel_id=1, source_target_pairs={{0,1},{1,0},{2,3},{3,2},{4,5},{5,4},{6,7},{7,6},{8,9},{9,8},{10,11... | collective-permute-start | bytes 1572872 | tf_op jit(solution)/shard_map/ppermute | solution.py:368
  19.5 28.2 %collective-permute-start.1 = (bf16[256,1024]{1,0:T(8,128)(2,1)}, bf16[256,1024]{1,0:T(8,128)(2,1)}, u32[]{:S(2)}, u32[]{:S(2)}) collective-permute-start(bf16[256,1024]{1,0:T(8,128)(2,1)} %get-tuple-element.25), channel_id=1, source_target_pairs={{0,2},{1,3},{2,0},{3,1},{4,6},{5,7},{6,4},{7,5},{8,10},{9,11},{10,... | collective-permute-start | bytes 1572872 | tf_op jit(solution)/shard_map/ppermute | solution.py:368
  26.5 0.7 copy-start.4
  40.5 7.1 %collective-permute-start.2 = (bf16[256,1024]{1,0:T(8,128)(2,1)}, bf16[256,1024]{1,0:T(8,128)(2,1)}, u32[]{:S(2)}, u32[]{:S(2)}) collective-permute-start(bf16[256,1024]{1,0:T(8,128)(2,1)} %collective-permute-done.r1), channel_id=1, source_target_pairs={{0,32},{32,0},{1,33},{33,1},{2,34},{34,2},{3,35},{35,3},{4,36},{36... | collective-permute-start | bytes 1572872 | tf_op jit(solution)/shard_map/ppermute | solution.py:364
  42.5 11.6 %copy-start = (f32[4,136,128]{2,1,0:T(8,128)S(1)}, f32[4,136,128]{2,1,0:T(8,128)}, u32[]{:S(2)}) copy-start(f32[4,136,128]{2,1,0:T(8,128)} %all-gather) | copy-start | bytes 835588
  42.5 11.6 %copy-start.8 = (f32[256]{0:T(256)S(1)}, f32[256]{0:T(256)}, u32[]{:S(2)}) copy-start(f32[256]{0:T(256)} %param.17) | copy-start | bytes 3076
  47.6 6.4 %copy-start.3 = (bf16[8,256,128]{2,1,0:T(8,128)(2,1)S(1)}, bf16[8,256,128]{2,1,0:T(8,128)(2,1)}, u32[]{:S(2)}) copy-start(bf16[8,256,128]{2,1,0:T(8,128)(2,1)} %c_hbm.1) | copy-start | bytes 1572868
  47.6 6.4 %copy-start.5 = (f32[2,256,128]{2,1,0:T(8,128)S(1)}, f32[2,256,128]{2,1,0:T(8,128)}, u32[]{:S(2)}) copy-start(f32[2,256,128]{2,1,0:T(8,128)} %copy-done.4) | copy-start | bytes 786436
  47.6 7.3 %collective-permute-start.3 = (bf16[8,1056,128]{2,1,0:T(8,128)(2,1)S(1)}, bf16[8,1056,128]{2,1,0:T(8,128)(2,1)S(1)}, u32[]{:S(2)}, u32[]{:S(2)}) collective-permute-start(bf16[8,1056,128]{2,1,0:T(8,128)(2,1)S(1)} %all-to-all-done.all_ref.a_ref), channel_id=1, source_target_pairs={{0,32},{32,0},{1,33},{33,1},{2,34},{34,2},{3,35},{35,3},{4,36},{36... | collective-permute-start | bytes 6488072 | tf_op jit(solution)/shard_map/ppermute | solution.py:364
  49.7 19.7 %collective-permute-start.4 = (bf16[256,1024]{1,0:T(8,128)(2,1)}, bf16[256,1024]{1,0:T(8,128)(2,1)}, u32[]{:S(2)}, u32[]{:S(2)}) collective-permute-start(bf16[256,1024]{1,0:T(8,128)(2,1)} %collective-permute-done.1.r2), channel_id=1, source_target_pairs={{0,1},{1,0},{2,3},{3,2},{4,5},{5,4},{6,7},{7,6},{8,9},{9,8},{10,11... | collective-permute-start | bytes 1572872 | tf_op jit(solution)/shard_map/ppermute | solution.py:368
  57.6 18.0 %all-to-all-start.1 = ((bf16[4,128,256]{2,1,0:T(8,128)(2,1)}), bf16[4,128,256]{2,1,0:T(8,128)(2,1)S(1)}, u32[]{:S(2)}, u32[]{:S(2)}) async-start(bf16[4,128,256]{2,1,0:T(8,128)(2,1)} %shard_map.124), calls=%async_computation.1 | async-start | bytes 524288 | tf_op jit(solution)/shard_map/all_to_all | solution.py:471
  69.4 4.3 %collective-permute-start.6 = (bf16[256,1024]{1,0:T(8,128)(2,1)}, bf16[256,1024]{1,0:T(8,128)(2,1)S(1)}, u32[]{:S(2)}, u32[]{:S(2)}) collective-permute-start(bf16[256,1024]{1,0:T(8,128)(2,1)} %collective-permute-done.4.r3), channel_id=1, source_target_pairs={{0,32},{32,0},{1,33},{33,1},{2,34},{34,2},{3,35},{35,3},{4,36},{36... | collective-permute-start | bytes 1572872 | tf_op jit(solution)/shard_map/ppermute | solution.py:364
  71.4 4.1 %collective-permute-start.5 = (bf16[256,1024]{1,0:T(8,128)(2,1)}, bf16[256,1024]{1,0:T(8,128)(2,1)S(1)}, u32[]{:S(2)}, u32[]{:S(2)}) collective-permute-start(bf16[256,1024]{1,0:T(8,128)(2,1)} %collective-permute-done.1.r2), channel_id=1, source_target_pairs={{0,32},{32,0},{1,33},{33,1},{2,34},{34,2},{3,35},{35,3},{4,36},{36... | collective-permute-start | bytes 1572872 | tf_op jit(solution)/shard_map/ppermute | solution.py:364
  78.0 10.5 %collective-permute-start.7 = (bf16[64,2048]{1,0:T(8,128)(2,1)S(1)}, bf16[64,2048]{1,0:T(8,128)(2,1)S(1)}, u32[]{:S(2)}, u32[]{:S(2)}) collective-permute-start(bf16[64,2048]{1,0:T(8,128)(2,1)S(1)} %get-tuple-element.34), channel_id=1, source_target_pairs={{0,16},{16,0},{1,17},{17,1},{2,18},{18,2},{3,19},{19,3},{4,20},{20... | collective-permute-start | bytes 786440 | tf_op jit(solution)/shard_map/ppermute | solution.py:364

commit v6 on v5

--- a/solution.py
+++ b/solution.py
@@ -29,7 +29,7 @@
 CHIP = ("x", "yh")
 BLOCKS = ("yh", "x")
 NEAR = ("z1", "z0")
-OWNERS = ("za", "z1")
+OWNERS = ("z1", "za")
 
 bf16 = jnp.bfloat16
 f32 = jnp.float32
@@ -272,7 +272,7 @@
     result = acc_ref[...] / total
     for z0 in range(2):
         for half in range(2):
-            blocks = [16 * yl + 4 * za + 2 * z1 + z0 for yl in range(2) for za in range(4) for z1 in range(2)]
+            blocks = [16 * yl + 4 * za + 2 * z1 + z0 for yl in range(2) for z1 in range(2) for za in range(4)]
             rows = [half * TOKENS + 8 * block for block in blocks]
             piece = jnp.concatenate([result[row : row + 8] for row in rows], axis=0).astype(bf16)
             for z1 in range(2):
@@ -316,9 +316,9 @@
 
 def finish_kernel(parts_ref, out_ref):
     for half in range(2):
-        total = parts_ref[half].astype(f32)
+        total = parts_ref[4 * half].astype(f32)
         for i in range(1, 4):
-            total = total + parts_ref[2 * i + half].astype(f32)
+            total = total + parts_ref[4 * half + i].astype(f32)
         width = parts_ref.shape[2]
         out_ref[:, half * width : (half + 1) * width] = total.astype(bf16)
 

time: 124 us -> 121 us (0.976)
  blocking collectives: 38.1 us -> 35.9 us
    all_to_all x1, blocking collectives: 33.7 us -> 31.5 us  [per_device(): lax.all_to_all(partial.reshape(8, 8, 2 * width), OWNERS, 0, 0, tiled=True)]
where the time goes in v6:
time: 121 us
  blocking collectives  35.9 us (30%)
  waiting for transfers between devices  34.7 us (29%)
  starting transfers between devices  33.1 us (27%)
  Pallas kernels  13.8 us (11%)
  local copies, waits for them, and re-layouts  2.1 us (2%)
    all_to_all x1, blocking collectives, per_device(): lax.all_to_all(partial.reshape(8, 8, 2 * width), OWNERS, 0, 0, tiled=True)  31.5 us
    ppermute x3, waiting for transfers between devices, flip(): return lax.ppermute(array, NEAR, [(j, j ^ i) for j in range(4)])  25.2 us
    pallas_call x7, Pallas kernels, plain(): pl.pallas_call(kernel, out_shape=out_shape, in_specs=in_specs, out_specs=...  11.4 us
    ppermute x5, starting transfers between devices, swap(): return lax.ppermute(array, axis, [(0, 1), (1, 0)])  10.9 us
    ppermute x3, starting transfers between devices, flip(): return lax.ppermute(array, NEAR, [(j, j ^ i) for j in range(4)])  10.9 us
    ppermute x5, waiting for transfers between devices, swap(): return lax.ppermute(array, axis, [(0, 1), (1, 0)])  9.53 us
    all_to_all x1, starting transfers between devices, per_device(): same = lax.all_to_all(packed, BLOCKS, 0, 0, tiled=True)  7.41 us
    all_to_all x1, starting transfers between devices, per_device(): attended = lax.all_to_all(attended, NEAR, 0, 0, tiled=True)  3.82 us
  transfers between devices with their start and end apart: 10, of which 5 were waited for; matrix products, arithmetic and copies ran while one was open for 1% of the time, Pallas kernels for 4%

profile of v6, /device:TPU:24, one launch (start us, length us, event | category | flops | bytes accessed | tf_op | source)
XLA Modules:
  0.0 120.7 jit_solution(11056931287924421625)
XLA Ops:
  0.0 0.0 copy-start.7
  0.0 0.0 copy-start.6
  0.0 0.0 copy-start.1
  0.7 2.6 %shard_map.118 = (bf16[8,1056,128]{2,1,0:T(8,128)(2,1)}, bf16[256,1024]{1,0:T(8,128)(2,1)}, bf16[256,1024]{1,0:T(8,128)(2,1)}) custom-call(bf16[8,128,128]{2,1,0:T(8,128)(2,1)} %ck_ref.1, bf16[8,256,128]{2,1,0:T(8,128)(2,1)} %nk_ref.1, bf16[8,128,128]{2,1,0:T(8,128)(2,1)} %cv_ref.1, bf16[8,256,128]{2,1,0:T(8,128)(2,1)} %nv_ref.1, bf16[256,4096]{1,0:T(8,128)(2,1)} %w_ref.1, ...), custom_call_target="tpu_custom_call" | custom-call | bytes 4096 | tf_op jit(solution)/shard_map/pallas_call | solution.py:347
  3.3 0.0 copy-done.7
  3.3 0.0 copy-done.6
  3.3 0.0 copy-done.1
  3.3 0.8 shard_map.120
  4.2 2.1 %all-gather = f32[4,136,128]{2,1,0:T(8,128)} all-gather(f32[2,136,128]{2,1,0:T(8,128)S(1)} %shard_map.120), channel_id=2, replica_groups=mesh['x'=4,'yh'=2,'c'=2,'yl'=2,'za'=4,'z1'=2,'z0'=2] {'c'}, dimensions={0}, use_global_device_ids=true | all-gather | bytes 417792 | tf_op jit(solution)/shard_map/all_gather | solution.py:419
  6.3 1.9 %shard_map.121 = bf16[8,1056,128]{2,1,0:T(8,128)(2,1)} custom-call(f32[2,2,136,128]{3,2,1,0:T(8,128)} %bitcast.8, bf16[8,1056,128]{2,1,0:T(8,128)(2,1)} %get-tuple-element.24.filled_ref), custom_call_target="tpu_custom_call", output_to_operand_aliasing={{}: (1, {})} | custom-call | bytes 4096 | tf_op jit(solution)/shard_map/pallas_call | solution.py:347
  8.2 0.0 copy-start.2
  8.2 0.0 copy-start.9
  8.2 7.4 %all-to-all-start = ((bf16[8,1056,128]{2,1,0:T(8,128)(2,1)}), bf16[8,1056,128]{2,1,0:T(8,128)(2,1)S(1)}, u32[]{:S(2)}, u32[]{:S(2)}) async-start(bf16[8,1056,128]{2,1,0:T(8,128)(2,1)} %shard_map.121), calls=%async_computation | async-start | bytes 4325376 | tf_op jit(solution)/shard_map/all_to_all | solution.py:433
  15.6 3.8 %collective-permute-start = (bf16[256,1024]{1,0:T(8,128)(2,1)}, bf16[256,1024]{1,0:T(8,128)(2,1)}, u32[]{:S(2)}, u32[]{:S(2)}) collective-permute-start(bf16[256,1024]{1,0:T(8,128)(2,1)} %get-tuple-element.20), channel_id=1, source_target_pairs={{0,1},{1,0},{2,3},{3,2},{4,5},{5,4},{6,7},{7,6},{8,9},{9,8},{10,11... | collective-permute-start | bytes 1572872 | tf_op jit(solution)/shard_map/ppermute | solution.py:368
  19.5 5.2 %collective-permute-start.1 = (bf16[256,1024]{1,0:T(8,128)(2,1)}, bf16[256,1024]{1,0:T(8,128)(2,1)}, u32[]{:S(2)}, u32[]{:S(2)}) collective-permute-start(bf16[256,1024]{1,0:T(8,128)(2,1)} %get-tuple-element.25), channel_id=1, source_target_pairs={{0,2},{1,3},{2,0},{3,1},{4,6},{5,7},{6,4},{7,5},{8,10},{9,11},{10,... | collective-permute-start | bytes 1572872 | tf_op jit(solution)/shard_map/ppermute | solution.py:368
  24.7 0.1 pad_add_fusion.group_ref
  24.7 0.0 copy-done.2
  24.7 0.0 copy-done.9
  24.7 1.8 %shard_map.119.y_ref = f32[2,256,128]{2,1,0:T(8,128)S(1)} custom-call(s32[4]{0:T(128)S(1)} %pad_add_fusion.group_ref, bf16[256,256]{1,0:T(8,128)(2,1)S(1)} %copy-done.6, f32[4,256]{1,0:T(4,128)S(1)} %copy-done.7, bf16[8,256,128]{2,1,0:T(8,128)(2,1)S(1)} %copy-done.1, bf16[8,256,128]{2,1,0:T(8,128)(2,1)S(1)} %copy-done.2, f32[4]{0:T(128)S(1)} %copy-done.9), custom_call_target="tpu_custom_call" | custom-call | bytes 4096 | tf_op jit(solution)/shard_map/pallas_call | solution.py:334
  26.5 0.0 copy-start.4
  26.5 0.7 copy-done.4
  27.2 13.3 %collective-permute-done.r1 = bf16[256,1024]{1,0:T(8,128)(2,1)} collective-permute-done((bf16[256,1024]{1,0:T(8,128)(2,1)}, bf16[256,1024]{1,0:T(8,128)(2,1)}, u32[]{:S(2)}, u32[]{:S(2)}) %collective-permute-start) | collective-permute-done | bytes 524320 | tf_op jit(solution)/shard_map/ppermute | solution.py:368
  40.5 1.9 %collective-permute-start.2 = (bf16[256,1024]{1,0:T(8,128)(2,1)}, bf16[256,1024]{1,0:T(8,128)(2,1)}, u32[]{:S(2)}, u32[]{:S(2)}) collective-permute-start(bf16[256,1024]{1,0:T(8,128)(2,1)} %collective-permute-done.r1), channel_id=1, source_target_pairs={{0,32},{32,0},{1,33},{33,1},{2,34},{34,2},{3,35},{35,3},{4,36},{36... | collective-permute-start | bytes 1572872 | tf_op jit(solution)/shard_map/ppermute | solution.py:364
  42.5 0.0 copy-start
  42.5 0.0 copy-start.8
  42.5 1.3 %constant_dynamic-slice_fusion.own_ref = bf16[256,2048]{1,0:T(8,128)(2,1)S(1)} fusion(bf16[256,4096]{1,0:T(8,128)(2,1)} %w_ref.1, s32[]{:T(128)S(6)} %select_n.9), kind=kLoop, calls=%fused_computation.1 | loop fusion | bytes 2097156 | tf_op jit(solution)/shard_map/dynamic_slice | solution.py:443
  43.8 3.8 %collective-permute-done.1.r2 = bf16[256,1024]{1,0:T(8,128)(2,1)} collective-permute-done((bf16[256,1024]{1,0:T(8,128)(2,1)}, bf16[256,1024]{1,0:T(8,128)(2,1)}, u32[]{:S(2)}, u32[]{:S(2)}) %collective-permute-start.1) | collective-permute-done | bytes 524320 | tf_op jit(solution)/shard_map/ppermute | solution.py:368
  47.6 0.0 collective-permute-done.2.s1
  47.6 0.0 all-to-all-done.all_ref.a_ref
  47.6 0.0 copy-start.3
  47.6 0.0 copy-start.5
  47.6 2.1 %collective-permute-start.3 = (bf16[8,1056,128]{2,1,0:T(8,128)(2,1)S(1)}, bf16[8,1056,128]{2,1,0:T(8,128)(2,1)S(1)}, u32[]{:S(2)}, u32[]{:S(2)}) collective-permute-start(bf16[8,1056,128]{2,1,0:T(8,128)(2,1)S(1)} %all-to-all-done.all_ref.a_ref), channel_id=1, source_target_pairs={{0,32},{32,0},{1,33},{33,1},{2,34},{34,2},{3,35},{35,3},{4,36},{36... | collective-permute-start | bytes 6488072 | tf_op jit(solution)/shard_map/ppermute | solution.py:364
  49.7 1.9 %collective-permute-start.4 = (bf16[256,1024]{1,0:T(8,128)(2,1)}, bf16[256,1024]{1,0:T(8,128)(2,1)}, u32[]{:S(2)}, u32[]{:S(2)}) collective-permute-start(bf16[256,1024]{1,0:T(8,128)(2,1)} %collective-permute-done.1.r2), channel_id=1, source_target_pairs={{0,1},{1,0},{2,3},{3,2},{4,5},{5,4},{6,7},{7,6},{8,9},{9,8},{10,11... | collective-permute-start | bytes 1572872 | tf_op jit(solution)/shard_map/ppermute | solution.py:368
  51.6 0.1 shard_map.122
  51.7 2.3 %all-gather.1 = f32[256,128]{1,0:T(8,128)S(1)} all-gather(f32[128,128]{1,0:T(8,128)S(1)} %shard_map.122), channel_id=3, replica_groups=mesh['x'=4,'yh'=2,'c'=2,'yl'=2,'za'=4,'z1'=2,'z0'=2] {'c'}, dimensions={0}, use_global_device_ids=true | all-gather | bytes 196608 | tf_op jit(solution)/shard_map/all_gather | solution.py:449
  54.0 0.0 copy-done
  54.0 0.0 copy-done.8
  54.0 0.0 copy-done.3
  54.0 0.0 copy-done.5
  54.0 0.9 shard_map.123.q_ref
  55.0 0.0 collective-permute-done.3.b_ref
  55.0 2.6 %shard_map.124 = bf16[4,128,256]{2,1,0:T(8,128)(2,1)} custom-call(bf16[512,128]{1,0:T(8,128)(2,1)S(1)} %shard_map.123.q_ref, bf16[8,1056,128]{2,1,0:T(8,128)(2,1)S(1)} %all-to-all-done.all_ref.a_ref, bf16[8,1056,128]{2,1,0:T(8,128)(2,1)S(1)} %collective-permute-done.3.b_ref), custom_call_target="tpu_custom_call" | custom-call | bytes 4096 | tf_op jit(solution)/shard_map/pallas_call | solution.py:347
  57.6 3.8 %all-to-all-start.1 = ((bf16[4,128,256]{2,1,0:T(8,128)(2,1)}), bf16[4,128,256]{2,1,0:T(8,128)(2,1)S(1)}, u32[]{:S(2)}, u32[]{:S(2)}) async-start(bf16[4,128,256]{2,1,0:T(8,128)(2,1)} %shard_map.124), calls=%async_computation.1 | async-start | bytes 524288 | tf_op jit(solution)/shard_map/all_to_all | solution.py:471
  61.4 8.1 %collective-permute-done.4.r3 = bf16[256,1024]{1,0:T(8,128)(2,1)} collective-permute-done((bf16[256,1024]{1,0:T(8,128)(2,1)}, bf16[256,1024]{1,0:T(8,128)(2,1)}, u32[]{:S(2)}, u32[]{:S(2)}) %collective-permute-start.4) | collective-permute-done | bytes 524320 | tf_op jit(solution)/shard_map/ppermute | solution.py:368
  69.4 1.9 %collective-permute-start.6 = (bf16[256,1024]{1,0:T(8,128)(2,1)}, bf16[256,1024]{1,0:T(8,128)(2,1)S(1)}, u32[]{:S(2)}, u32[]{:S(2)}) collective-permute-start(bf16[256,1024]{1,0:T(8,128)(2,1)} %collective-permute-done.4.r3), channel_id=1, source_target_pairs={{0,32},{32,0},{1,33},{33,1},{2,34},{34,2},{3,35},{35,3},{4,36},{36... | collective-permute-start | bytes 1572872 | tf_op jit(solution)/shard_map/ppermute | solution.py:364
  71.4 2.4 %collective-permute-start.5 = (bf16[256,1024]{1,0:T(8,128)(2,1)}, bf16[256,1024]{1,0:T(8,128)(2,1)S(1)}, u32[]{:S(2)}, u32[]{:S(2)}) collective-permute-start(bf16[256,1024]{1,0:T(8,128)(2,1)} %collective-permute-done.1.r2), channel_id=1, source_target_pairs={{0,32},{32,0},{1,33},{33,1},{2,34},{34,2},{3,35},{35,3},{4,36},{36... | collective-permute-start | bytes 1572872 | tf_op jit(solution)/shard_map/ppermute | solution.py:364
  73.8 0.0 collective-permute-done.6.s3
  73.8 1.7 %collective-permute-done.5.s2 = bf16[256,1024]{1,0:T(8,128)(2,1)S(1)} collective-permute-done((bf16[256,1024]{1,0:T(8,128)(2,1)}, bf16[256,1024]{1,0:T(8,128)(2,1)S(1)}, u32[]{:S(2)}, u32[]{:S(2)}) %collective-permute-start.5) | collective-permute-done | bytes 524320 | tf_op jit(solution)/shard_map/ppermute | solution.py:364
  75.5 0.0 all-to-all-done.1.att_ref
  75.5 2.5 %shard_map.125 = (bf16[64,2048]{1,0:T(8,128)(2,1)S(1)}, bf16[64,2048]{1,0:T(8,128)(2,1)S(1)}) custom-call(bf16[4,128,256]{2,1,0:T(8,128)(2,1)S(1)} %all-to-all-done.1.att_ref, bf16[256,2048]{1,0:T(8,128)(2,1)S(1)} %constant_dynamic-slice_fusion.own_ref, bf16[256,1024]{1,0:T(8,128)(2,1)} %collective-permute-done.r1, ...), custom_call_target="tpu_custom_call" | custom-call | bytes 4096 | tf_op jit(solution)/shard_map/pallas_call | solution.py:347
  78.0 2.7 %collective-permute-start.7 = (bf16[64,2048]{1,0:T(8,128)(2,1)S(1)}, bf16[64,2048]{1,0:T(8,128)(2,1)S(1)}, u32[]{:S(2)}, u32[]{:S(2)}) collective-permute-start(bf16[64,2048]{1,0:T(8,128)(2,1)S(1)} %get-tuple-element.34), channel_id=1, source_target_pairs={{0,16},{16,0},{1,17},{17,1},{2,18},{18,2},{3,19},{19,3},{4,20},{20... | collective-permute-start | bytes 786440 | tf_op jit(solution)/shard_map/ppermute | solution.py:364
  80.7 7.8 %collective-permute-done.7.second_ref = bf16[64,2048]{1,0:T(8,128)(2,1)S(1)} collective-permute-done((bf16[64,2048]{1,0:T(8,128)(2,1)S(1)}, bf16[64,2048]{1,0:T(8,128)(2,1)S(1)}, u32[]{:S(2)}, u32[]{:S(2)}) %collective-permute-start.7) | collective-permute-done | bytes 262176 | tf_op jit(solution)/shard_map/ppermute | solution.py:364
  88.5 0.1 shard_map.126
  88.5 31.5 %all_to_all.15.parts_ref = bf16[8,8,2048]{2,1,0:T(8,128)(2,1)S(1)} all-to-all(bf16[8,8,2048]{2,1,0:T(8,128)(2,1)S(1)} %bitcast.10), channel_id=1, replica_groups=mesh['x'=4,'yh'=2,'c'=2,'yl'=2,'za'=4,'z1'=2,'z0'=2] {'z1','za'}, dimensions={0} | all-to-all | bytes 524288 | tf_op jit(solution)/shard_map/all_to_all | solution.py:482
  120.1 0.7 shard_map.127
Async XLA Ops:
  0.0 3.3 %copy-start.7 = (f32[4,256]{1,0:T(4,128)S(1)}, f32[4,256]{1,0:T(4,128)}, u32[]{:S(2)}) copy-start(f32[4,256]{1,0:T(4,128)} %decay_ref.2) | copy-start | bytes 12292
  0.0 3.3 %copy-start.6 = (bf16[256,256]{1,0:T(8,128)(2,1)S(1)}, bf16[256,256]{1,0:T(8,128)(2,1)}, u32[]{:S(2)}) copy-start(bf16[256,256]{1,0:T(8,128)(2,1)} %x_ref.3) | copy-start | bytes 393220
  0.0 3.3 %copy-start.1 = (bf16[8,256,128]{2,1,0:T(8,128)(2,1)S(1)}, bf16[8,256,128]{2,1,0:T(8,128)(2,1)}, u32[]{:S(2)}) copy-start(bf16[8,256,128]{2,1,0:T(8,128)(2,1)} %b_hbm.1) | copy-start | bytes 1572868
  8.2 16.5 %copy-start.2 = (bf16[8,256,128]{2,1,0:T(8,128)(2,1)S(1)}, bf16[8,256,128]{2,1,0:T(8,128)(2,1)}, u32[]{:S(2)}) copy-start(bf16[8,256,128]{2,1,0:T(8,128)(2,1)} %c_hbm.1) | copy-start | bytes 1572868
  8.2 16.5 %copy-start.9 = (f32[4]{0:T(128)S(1)}, f32[4]{0:T(128)}, u32[]{:S(2)}) copy-start(f32[4]{0:T(128)} %gain_ref.1) | copy-start | bytes 52
  8.2 39.4 %all-to-all-start = ((bf16[8,1056,128]{2,1,0:T(8,128)(2,1)}), bf16[8,1056,128]{2,1,0:T(8,128)(2,1)S(1)}, u32[]{:S(2)}, u32[]{:S(2)}) async-start(bf16[8,1056,128]{2,1,0:T(8,128)(2,1)} %shard_map.121), calls=%async_computation | async-start | bytes 4325376 | tf_op jit(solution)/shard_map/all_to_all | solution.py:433
  15.6 24.9 %collective-permute-start = (bf16[256,1024]{1,0:T(8,128)(2,1)}, bf16[256,1024]{1,0:T(8,128)(2,1)}, u32[]{:S(2)}, u32[]{:S(2)}) collective-permute-start(bf16[256,1024]{1,0:T(8,128)(2,1)} %get-tuple-element.20), channel_id=1, source_target_pairs={{0,1},{1,0},{2,3},{3,2},{4,5},{5,4},{6,7},{7,6},{8,9},{9,8},{10,11... | collective-permute-start | bytes 1572872 | tf_op jit(solution)/shard_map/ppermute | solution.py:368
  19.5 28.2 %collective-permute-start.1 = (bf16[256,1024]{1,0:T(8,128)(2,1)}, bf16[256,1024]{1,0:T(8,128)(2,1)}, u32[]{:S(2)}, u32[]{:S(2)}) collective-permute-start(bf16[256,1024]{1,0:T(8,128)(2,1)} %get-tuple-element.25), channel_id=1, source_target_pairs={{0,2},{1,3},{2,0},{3,1},{4,6},{5,7},{6,4},{7,5},{8,10},{9,11},{10,... | collective-permute-start | bytes 1572872 | tf_op jit(solution)/shard_map/ppermute | solution.py:368
  26.5 0.7 copy-start.4
  40.5 7.1 %collective-permute-start.2 = (bf16[256,1024]{1,0:T(8,128)(2,1)}, bf16[256,1024]{1,0:T(8,128)(2,1)}, u32[]{:S(2)}, u32[]{:S(2)}) collective-permute-start(bf16[256,1024]{1,0:T(8,128)(2,1)} %collective-permute-done.r1), channel_id=1, source_target_pairs={{0,32},{32,0},{1,33},{33,1},{2,34},{34,2},{3,35},{35,3},{4,36},{36... | collective-permute-start | bytes 1572872 | tf_op jit(solution)/shard_map/ppermute | solution.py:364
  42.5 11.6 %copy-start = (f32[4,136,128]{2,1,0:T(8,128)S(1)}, f32[4,136,128]{2,1,0:T(8,128)}, u32[]{:S(2)}) copy-start(f32[4,136,128]{2,1,0:T(8,128)} %all-gather) | copy-start | bytes 835588
  42.5 11.6 %copy-start.8 = (f32[256]{0:T(256)S(1)}, f32[256]{0:T(256)}, u32[]{:S(2)}) copy-start(f32[256]{0:T(256)} %param.17) | copy-start | bytes 3076
  47.6 6.4 %copy-start.3 = (bf16[8,256,128]{2,1,0:T(8,128)(2,1)S(1)}, bf16[8,256,128]{2,1,0:T(8,128)(2,1)}, u32[]{:S(2)}) copy-start(bf16[8,256,128]{2,1,0:T(8,128)(2,1)} %c_hbm.1) | copy-start | bytes 1572868
  47.6 6.4 %copy-start.5 = (f32[2,256,128]{2,1,0:T(8,128)S(1)}, f32[2,256,128]{2,1,0:T(8,128)}, u32[]{:S(2)}) copy-start(f32[2,256,128]{2,1,0:T(8,128)} %copy-done.4) | copy-start | bytes 786436
  47.6 7.3 %collective-permute-start.3 = (bf16[8,1056,128]{2,1,0:T(8,128)(2,1)S(1)}, bf16[8,1056,128]{2,1,0:T(8,128)(2,1)S(1)}, u32[]{:S(2)}, u32[]{:S(2)}) collective-permute-start(bf16[8,1056,128]{2,1,0:T(8,128)(2,1)S(1)} %all-to-all-done.all_ref.a_ref), channel_id=1, source_target_pairs={{0,32},{32,0},{1,33},{33,1},{2,34},{34,2},{3,35},{35,3},{4,36},{36... | collective-permute-start | bytes 6488072 | tf_op jit(solution)/shard_map/ppermute | solution.py:364
  49.7 19.7 %collective-permute-start.4 = (bf16[256,1024]{1,0:T(8,128)(2,1)}, bf16[256,1024]{1,0:T(8,128)(2,1)}, u32[]{:S(2)}, u32[]{:S(2)}) collective-permute-start(bf16[256,1024]{1,0:T(8,128)(2,1)} %collective-permute-done.1.r2), channel_id=1, source_target_pairs={{0,1},{1,0},{2,3},{3,2},{4,5},{5,4},{6,7},{7,6},{8,9},{9,8},{10,11... | collective-permute-start | bytes 1572872 | tf_op jit(solution)/shard_map/ppermute | solution.py:368
  57.6 18.0 %all-to-all-start.1 = ((bf16[4,128,256]{2,1,0:T(8,128)(2,1)}), bf16[4,128,256]{2,1,0:T(8,128)(2,1)S(1)}, u32[]{:S(2)}, u32[]{:S(2)}) async-start(bf16[4,128,256]{2,1,0:T(8,128)(2,1)} %shard_map.124), calls=%async_computation.1 | async-start | bytes 524288 | tf_op jit(solution)/shard_map/all_to_all | solution.py:471
  69.4 4.3 %collective-permute-start.6 = (bf16[256,1024]{1,0:T(8,128)(2,1)}, bf16[256,1024]{1,0:T(8,128)(2,1)S(1)}, u32[]{:S(2)}, u32[]{:S(2)}) collective-permute-start(bf16[256,1024]{1,0:T(8,128)(2,1)} %collective-permute-done.4.r3), channel_id=1, source_target_pairs={{0,32},{32,0},{1,33},{33,1},{2,34},{34,2},{3,35},{35,3},{4,36},{36... | collective-permute-start | bytes 1572872 | tf_op jit(solution)/shard_map/ppermute | solution.py:364
  71.4 4.1 %collective-permute-start.5 = (bf16[256,1024]{1,0:T(8,128)(2,1)}, bf16[256,1024]{1,0:T(8,128)(2,1)S(1)}, u32[]{:S(2)}, u32[]{:S(2)}) collective-permute-start(bf16[256,1024]{1,0:T(8,128)(2,1)} %collective-permute-done.1.r2), channel_id=1, source_target_pairs={{0,32},{32,0},{1,33},{33,1},{2,34},{34,2},{3,35},{35,3},{4,36},{36... | collective-permute-start | bytes 1572872 | tf_op jit(solution)/shard_map/ppermute | solution.py:364
  78.0 10.5 %collective-permute-start.7 = (bf16[64,2048]{1,0:T(8,128)(2,1)S(1)}, bf16[64,2048]{1,0:T(8,128)(2,1)S(1)}, u32[]{:S(2)}, u32[]{:S(2)}) collective-permute-start(bf16[64,2048]{1,0:T(8,128)(2,1)S(1)} %get-tuple-element.34), channel_id=1, source_target_pairs={{0,16},{16,0},{1,17},{17,1},{2,18},{18,2},{3,19},{19,3},{4,20},{20... | collective-permute-start | bytes 786440 | tf_op jit(solution)/shard_map/ppermute | solution.py:364
